TPU v7x, 32 devices: a whole 2x2x4 slice. The times are simulated.
32 devices in a mesh: dp: 4 (over z), seq: 8 (over y, x, core).
Axes of the slice: x: 2, y: 2, z: 4, core: 2. Of those that a mesh axis runs over, the one named last changes fastest.
Arguments:
- inputs: bfloat16 [12, 1024, 512], P('dp', 'seq'), may hold values from -6 to 6
- random_blocks: int32 [12, 8, 16, 3], P('dp', None, 'seq'), may hold values from 1 to 14, as said below
- entry_weight: bfloat16 [512, 1536], replicated, may hold values from -0.375 to 0.375
- query_bias: bfloat16 [512], replicated, may hold values from -1.5 to 1.5
- value_bias: bfloat16 [512], replicated, may hold values from -1.5 to 1.5
- out_weight: bfloat16 [512, 512], replicated, may hold values from -1 to 1
- out_bias: bfloat16 [512], replicated, may hold values from -1.5 to 1.5
- norm_gain: bfloat16 [512], replicated, may hold values from 0.5 to 1.5
- norm_shift: bfloat16 [512], replicated, may hold values from -1.5 to 1.5
- inner_weight: bfloat16 [512, 2048], replicated, may hold values from -0.25 to 0.25
- inner_bias: bfloat16 [2048], replicated, may hold values from -2.5 to 2.5
- outer_weight: bfloat16 [2048, 512], replicated, may hold values from -0.25 to 0.25
- outer_bias: bfloat16 [512], replicated, may hold values from -1.5 to 1.5
- final_gain: bfloat16 [512], replicated, may hold values from 0.5 to 1.5
- final_shift: bfloat16 [512], replicated, may hold values from -1.5 to 1.5
- cotangent: bfloat16 [12, 1024, 512], P('dp', 'seq'), may hold values from -6 to 6
Outputs:
- layer_out: bfloat16 [12, 1024, 512], P('dp', 'seq')
- input_grad: bfloat16 [12, 1024, 512], P('dp', 'seq')
- entry_weight_grad: float32 [512, 1536], replicated
- query_bias_grad: float32 [512], replicated
- value_bias_grad: float32 [512], replicated
- out_weight_grad: float32 [512, 512], replicated
- out_bias_grad: float32 [512], replicated
- norm_gain_grad: float32 [512], replicated
- norm_shift_grad: float32 [512], replicated
- inner_weight_grad: float32 [512, 2048], replicated
- inner_bias_grad: float32 [2048], replicated
- outer_weight_grad: float32 [2048, 512], replicated
- outer_bias_grad: float32 [512], replicated
- final_gain_grad: float32 [512], replicated
- final_shift_grad: float32 [512], replicated
Inputs may be any that keep to these rules, and one draw needn't show every extreme that they name: `random_blocks`: every entry names an interior block (neither 0 nor 16 - 1) of the same sequence that does not lie on the index of seq holding the query block; the three entries of one query block lie on three different indices of seq. Over all entries held by one index of seq (its sequences, heads and query blocks), at most 21 lie on any one index of seq, and every index of seq reaches 21 for some index.
All inputs are finite; a program needn't handle non-finite values.
Results may differ from a plain program's by a relative error of at most 0.015.
The roundings to bfloat16 on the way count: a program that leaves them out, or rounds other values in their place, can miss the bound.
Values may be sent and summed in bfloat16 or wider, within the bound.
A program may use at most 192 MiB of HBM per device.

v0:
```python
from functools import partial

import jax
import jax.numpy as jnp
from jax import lax
from jax.sharding import PartitionSpec as P

HEADS = 8
HEAD = 64
BLOCK = 64


HIGHEST = lax.Precision.HIGHEST
EPSILON = 1e-05
NEGATIVE = -1e30


def spread_2(value, axis, root):
    mine = lax.axis_index(axis) == root
    return lax.psum(jnp.where(mine, value, jnp.zeros_like(value)), axis)


def for_sending(value):

    def short(part):
        return part.astype(jnp.bfloat16) if part.dtype == jnp.float32 else part

    return jax.tree.map(short, value)


def extended(block, sides, width):
    for axis, dim in sides:
        count = lax.axis_size(axis)
        forward = [(i, i + 1) for i in range(count - 1)]
        backward = [(target, source) for source, target in forward]
        low = lax.ppermute(
            lax.slice_in_dim(block, block.shape[dim] - width, None, axis=dim), axis, forward
        )
        high = lax.ppermute(lax.slice_in_dim(block, 0, width, axis=dim), axis, backward)
        block = jnp.concatenate([low, block, high], axis=dim)
    return block


def combined_all(part, axis, combine):
    gathered = jax.tree.map(lambda a: lax.all_gather(a, axis), part)

    def take(source):
        return jax.tree.map(lambda a: lax.dynamic_index_in_dim(a, source, 0, False), gathered)

    return lax.fori_loop(
        1, lax.axis_size(axis), lambda source, state: combine(state, take(source)), take(0)
    )


def norm_apply(values, gain_vec, shift_vec):
    center = values - jnp.mean(values, axis=-1, keepdims=True)
    spread = jnp.mean(center * center, axis=-1, keepdims=True)
    return center * lax.rsqrt(spread + EPSILON) * gain_vec + shift_vec


def pair_blocks(row_data, head_count, block_rows):
    seq_count, length_here, full_width = row_data.shape
    head_width = full_width // (2 * head_count)
    shaped = row_data.reshape(
        seq_count, length_here // block_rows, block_rows, 2, head_count, head_width
    )
    return shaped.transpose(0, 4, 1, 2, 3, 5).reshape(
        seq_count, head_count, length_here // block_rows, block_rows, 2 * head_width
    )


def pair_tokens(blocked):
    seq_count, head_count, block_count, block_rows, double_width = blocked.shape
    head_width = double_width // 2
    shaped = blocked.reshape(seq_count, head_count, block_count, block_rows, 2, head_width)
    return shaped.transpose(0, 2, 3, 4, 1, 5).reshape(
        seq_count, block_count * block_rows, 2 * head_count * head_width
    )


def head_rows(row_data, head_count):
    seq_count, length_here, full_width = row_data.shape
    return row_data.reshape(seq_count, length_here, head_count, full_width // head_count).transpose(
        0, 2, 1, 3
    )


def row_heads(split_rows):
    seq_count, head_count, length_here, head_width = split_rows.shape
    return split_rows.transpose(0, 2, 1, 3).reshape(seq_count, length_here, head_count * head_width)


def merge_parts(earlier, later):
    peak_one, total_one, out_one = earlier
    peak_two, total_two, out_two = later
    row_peak = jnp.maximum(peak_one, peak_two)
    factor_one = jnp.exp(peak_one - row_peak)
    factor_two = jnp.exp(peak_two - row_peak)
    return (
        row_peak,
        total_one * factor_one + total_two * factor_two,
        out_one * factor_one[..., None] + out_two * factor_two[..., None],
    )


def share_rows(row_data, root_device):
    return spread_2(row_data, "seq", root_device)


def share_grads(grad_rows, grad_delta, root_device):
    return (
        spread_2(grad_rows.astype(jnp.bfloat16), "seq", root_device).astype(grad_rows.dtype),
        spread_2(for_sending(grad_delta), "seq", root_device).astype(grad_delta.dtype),
    )


def on_device(
    inputs,
    random_blocks,
    entry_weight,
    query_bias,
    value_bias,
    out_weight,
    out_bias,
    norm_gain,
    norm_shift,
    inner_weight,
    inner_bias,
    outer_weight,
    outer_bias,
    final_gain,
    final_shift,
    cotangent,
):
    seq_count, token_count, model_width = inputs.shape
    head_count = HEADS
    head_width = HEAD
    block_rows = BLOCK
    per_dev = token_count // block_rows
    devices = lax.axis_size("seq")
    device = lax.axis_index("seq")
    block_total = devices * per_dev
    request_total = seq_count * head_count * per_dev * 3
    capacity = (request_total + devices - 2) // (devices - 1)
    table_rows = seq_count * head_count * per_dev
    query_scale = head_width ** (-0.5)
    is_first = device == 0
    is_last = device == devices - 1
    bfloat = jnp.bfloat16
    single = jnp.float32
    flat_in = inputs.reshape(-1, model_width)
    entry_out = jnp.dot(flat_in, entry_weight, preferred_element_type=single)
    packed = jnp.concatenate(
        [
            (entry_out[:, :model_width] + query_bias) * query_scale,
            entry_out[:, model_width : 2 * model_width],
            entry_out[:, 2 * model_width :] + value_bias,
        ],
        axis=1,
    )
    packed = packed.astype(bfloat).reshape(seq_count, token_count, 3 * model_width)
    key_value = packed[:, :, model_width:]
    padded = extended(key_value, (("seq", 1),), block_rows)
    global_rows = jnp.concatenate(
        [
            share_rows(packed[:, :block_rows], 0),
            share_rows(packed[:, token_count - block_rows :], devices - 1),
        ],
        axis=1,
    )
    owners = (random_blocks // per_dev).reshape(-1)
    within = random_blocks % per_dev
    seq_index = lax.broadcasted_iota(jnp.int32, random_blocks.shape, 0)
    head_index = lax.broadcasted_iota(jnp.int32, random_blocks.shape, 1)
    request_codes = ((seq_index * head_count + head_index) * per_dev + within).reshape(-1)
    onehot = (owners[:, None] == jnp.arange(devices, dtype=jnp.int32)[None, :]).astype(jnp.int32)
    slot_index = jnp.sum((jnp.cumsum(onehot, axis=0) - onehot) * onehot, axis=1)
    slot_place = owners * capacity + slot_index
    requests = (
        jnp.full((devices * capacity,), -1, jnp.int32)
        .at[slot_place]
        .set(request_codes)
        .reshape(devices, capacity)
    )
    incoming = lax.all_to_all(requests, "seq", split_axis=0, concat_axis=0, tiled=True)
    head_table = pair_blocks(key_value, head_count, block_rows).reshape(
        table_rows, block_rows, 2 * head_width
    )
    served = head_table[jnp.maximum(incoming, 0)]
    served = jnp.where((incoming >= 0)[:, :, None, None], served, jnp.zeros((), bfloat))
    fetched = lax.all_to_all(served, "seq", split_axis=0, concat_axis=0, tiled=True)
    random_kv = fetched.reshape(devices * capacity, block_rows, 2 * head_width)[slot_place]
    random_kv = random_kv.reshape(seq_count, head_count, per_dev, 3, block_rows, 2 * head_width)
    window_view = pair_blocks(padded, head_count, block_rows)
    window_kv = jnp.stack(
        [window_view[:, :, :per_dev], window_view[:, :, 1 : per_dev + 1], window_view[:, :, 2:]],
        axis=3,
    )
    global_kv = pair_blocks(global_rows[:, :, model_width:], head_count, block_rows)
    global_kv = jnp.broadcast_to(
        global_kv[:, :, None], (seq_count, head_count, per_dev, 2, block_rows, 2 * head_width)
    )
    all_kv = jnp.concatenate([window_kv, global_kv, random_kv], axis=3).reshape(
        seq_count, head_count, per_dev, 8 * block_rows, 2 * head_width
    )
    key_part = all_kv[..., :head_width]
    value_part = all_kv[..., head_width:]
    query_view = head_rows(packed[:, :, :model_width], head_count).reshape(
        seq_count, head_count, per_dev, block_rows, head_width
    )
    block_ids = device * per_dev + jnp.arange(per_dev)[:, None]
    column = jnp.arange(8 * block_rows)[None, :]
    neighbor = block_ids + column // block_rows - 1
    key_keep = (column >= 3 * block_rows) | (neighbor >= 1) & (neighbor <= block_total - 2)
    key_keep = key_keep[None, None, :, None, :]

    def block_scores():
        raw_scores = jnp.einsum(
            "shiqd,shikd->shiqk", query_view, key_part, preferred_element_type=single
        )
        return jnp.where(key_keep, raw_scores, NEGATIVE)

    scores = block_scores()
    row_peak = jnp.max(scores, axis=-1, keepdims=True)
    exponent = jnp.exp(scores - row_peak)
    row_total = jnp.sum(exponent, axis=-1, keepdims=True)
    probability = exponent / row_total
    log_total = row_peak + jnp.log(row_total)
    prob_low = probability.astype(bfloat)
    window_out = jnp.einsum(
        "shiqk,shikd->shiqd", prob_low, value_part, preferred_element_type=single
    )
    global_query = head_rows(global_rows[:, :, :model_width], head_count)
    local_keys = head_rows(packed[:, :, model_width : 2 * model_width], head_count)
    local_values = head_rows(packed[:, :, 2 * model_width :], head_count)
    global_scores = jnp.einsum(
        "shqd,shkd->shqk", global_query, local_keys, preferred_element_type=single
    )
    global_peak = jnp.max(global_scores, axis=-1)
    global_exp = jnp.exp(global_scores - global_peak[..., None])
    global_total = jnp.sum(global_exp, axis=-1)
    global_sum = jnp.einsum(
        "shqk,shkd->shqd", global_exp, local_values.astype(single), precision=HIGHEST
    )
    global_peak, global_total, global_sum = combined_all(
        (global_peak, global_total, global_sum), "seq", merge_parts
    )
    global_out = global_sum / global_total[..., None]
    global_log = global_peak + jnp.log(global_total)
    block_pos = jnp.arange(per_dev)
    take_first = ((block_pos == 0) & is_first)[None, None, :, None, None]
    take_last = ((block_pos == per_dev - 1) & is_last)[None, None, :, None, None]
    combined = jnp.where(take_first, global_out[:, :, None, :block_rows], window_out)
    combined = jnp.where(take_last, global_out[:, :, None, block_rows:], combined)
    attended = (
        row_heads(combined.reshape(seq_count, head_count, token_count, head_width))
        .reshape(-1, model_width)
        .astype(bfloat)
    )
    branch = jnp.dot(attended, out_weight, preferred_element_type=single) + out_bias
    residual_in = flat_in.astype(single) + branch
    first_norm, first_pull = jax.vjp(
        norm_apply, residual_in, norm_gain.astype(single), norm_shift.astype(single)
    )
    first_low = first_norm.astype(bfloat)
    inner_pre = jnp.dot(first_low, inner_weight, preferred_element_type=single) + inner_bias
    activated, gelu_pull = jax.vjp(partial(jax.nn.gelu, approximate=False), inner_pre)
    hidden = activated.astype(bfloat)
    second = first_norm + (
        jnp.dot(hidden, outer_weight, preferred_element_type=single) + outer_bias
    )
    final_norm, final_pull = jax.vjp(
        norm_apply, second, final_gain.astype(single), final_shift.astype(single)
    )
    layer_out = final_norm.astype(bfloat).reshape(inputs.shape)
    grad_second, final_gain_grad, final_shift_grad = final_pull(
        cotangent.reshape(-1, model_width).astype(single)
    )
    grad_outer = grad_second.astype(bfloat)
    outer_weight_grad = jnp.dot(hidden.T, grad_outer, preferred_element_type=single)
    outer_bias_grad = jnp.sum(grad_outer.astype(single), axis=0)
    (grad_active,) = gelu_pull(jnp.dot(grad_outer, outer_weight.T, preferred_element_type=single))
    grad_inner = grad_active.astype(bfloat)
    inner_weight_grad = jnp.dot(first_low.T, grad_inner, preferred_element_type=single)
    inner_bias_grad = jnp.sum(grad_inner.astype(single), axis=0)
    grad_first = grad_second + jnp.dot(grad_inner, inner_weight.T, preferred_element_type=single)
    grad_resid, norm_gain_grad, norm_shift_grad = first_pull(grad_first)
    grad_branch = grad_resid.astype(bfloat)
    out_weight_grad = jnp.dot(attended.T, grad_branch, preferred_element_type=single)
    out_bias_grad = jnp.sum(grad_branch.astype(single), axis=0)
    grad_attended = jnp.dot(grad_branch, out_weight.T, preferred_element_type=single).astype(bfloat)
    grad_heads = head_rows(
        grad_attended.reshape(seq_count, token_count, model_width), head_count
    ).reshape(seq_count, head_count, per_dev, block_rows, head_width)
    grad_window = jnp.where(take_first | take_last, jnp.zeros((), bfloat), grad_heads)
    probability = jnp.exp(block_scores() - log_total)
    prob_low = probability.astype(bfloat)
    grad_prob = jnp.einsum(
        "shiqd,shikd->shiqk", grad_window, value_part, preferred_element_type=single
    )
    row_delta = jnp.sum(probability * grad_prob, axis=-1, keepdims=True)
    grad_scores = (probability * (grad_prob - row_delta)).astype(bfloat)
    grad_query_block = jnp.einsum(
        "shiqk,shikd->shiqd", grad_scores, key_part, preferred_element_type=single
    )
    grad_key_block = jnp.einsum(
        "shiqk,shiqd->shikd", grad_scores, query_view, preferred_element_type=single
    )
    grad_value_block = jnp.einsum(
        "shiqk,shiqd->shikd", prob_low, grad_window, preferred_element_type=single
    )
    grad_kv = jnp.concatenate([grad_key_block, grad_value_block], axis=-1).reshape(
        seq_count, head_count, per_dev, 8, block_rows, 2 * head_width
    )
    pad_none = ((0, 0), (0, 0))
    grad_pad = (
        jnp.pad(grad_kv[:, :, :, 0], pad_none + ((0, 2), (0, 0), (0, 0)))
        + jnp.pad(grad_kv[:, :, :, 1], pad_none + ((1, 1), (0, 0), (0, 0)))
        + jnp.pad(grad_kv[:, :, :, 2], pad_none + ((2, 0), (0, 0), (0, 0)))
    )
    grad_tokens = pair_tokens(grad_pad)
    edge_grads = jnp.concatenate(
        [grad_tokens[:, :block_rows], grad_tokens[:, token_count + block_rows :]], axis=1
    )
    returned = extended(edge_grads.astype(jnp.bfloat16), (("seq", 1),), block_rows).astype(
        edge_grads.dtype
    )
    gap = token_count - block_rows
    grad_kv_local = (
        grad_tokens[:, block_rows : block_rows + token_count]
        + jnp.pad(returned[:, :block_rows], ((0, 0), (0, gap), (0, 0)))
        + jnp.pad(returned[:, 3 * block_rows :], ((0, 0), (gap, 0), (0, 0)))
    )
    grad_global_kv = pair_tokens(jnp.sum(grad_kv[:, :, :, 3:5], axis=2))
    grad_random = grad_kv[:, :, :, 5:8].reshape(request_total, block_rows, 2 * head_width)
    outgoing = (
        jnp.zeros((devices * capacity, block_rows, 2 * head_width), single)
        .at[slot_place]
        .set(grad_random)
    )
    outgoing = outgoing.reshape(devices, capacity, block_rows, 2 * head_width)
    returned_random = lax.all_to_all(
        outgoing.astype(jnp.bfloat16), "seq", split_axis=0, concat_axis=0, tiled=True
    ).astype(outgoing.dtype)
    segment_ids = jnp.where(incoming >= 0, incoming, table_rows).reshape(-1)
    grad_table = jax.ops.segment_sum(
        returned_random.reshape(devices * capacity, block_rows, 2 * head_width),
        segment_ids,
        num_segments=table_rows + 1,
    )[:table_rows]
    grad_owned = pair_tokens(
        grad_table.reshape(seq_count, head_count, per_dev, block_rows, 2 * head_width)
    )
    first_cot = grad_heads[:, :, 0].astype(single)
    last_cot = grad_heads[:, :, per_dev - 1].astype(single)
    first_cot, first_delta = share_grads(
        first_cot, jnp.sum(first_cot * global_out[:, :, :block_rows], axis=-1), 0
    )
    last_cot, last_delta = share_grads(
        last_cot, jnp.sum(last_cot * global_out[:, :, block_rows:], axis=-1), devices - 1
    )
    global_cot = jnp.concatenate([first_cot, last_cot], axis=2)
    global_delta = jnp.concatenate([first_delta, last_delta], axis=2)
    global_prob = jnp.exp(
        jnp.einsum("shqd,shkd->shqk", global_query, local_keys, preferred_element_type=single)
        - global_log[..., None]
    )
    global_dprob = jnp.einsum(
        "shqd,shkd->shqk", global_cot.astype(bfloat), local_values, preferred_element_type=single
    )
    global_grads = (global_prob * (global_dprob - global_delta[..., None])).astype(bfloat)
    grad_global_query = jnp.einsum(
        "shqk,shkd->shqd", global_grads, local_keys, preferred_element_type=single
    )
    grad_local_key = jnp.einsum(
        "shqk,shqd->shkd", global_grads, global_query, preferred_element_type=single
    )
    grad_local_value = jnp.einsum("shqk,shqd->shkd", global_prob, global_cot, precision=HIGHEST)
    partials = jnp.concatenate([row_heads(grad_global_query), grad_global_kv], axis=-1)
    partials = lax.psum(partials.astype(jnp.bfloat16), "seq").astype(jnp.float32)
    owner_part = jnp.where(
        is_first, jnp.pad(partials[:, :block_rows], ((0, 0), (0, gap), (0, 0))), 0.0
    ) + jnp.where(is_last, jnp.pad(partials[:, block_rows:], ((0, 0), (gap, 0), (0, 0))), 0.0)
    grad_query_tokens = row_heads(
        grad_query_block.reshape(seq_count, head_count, token_count, head_width)
    )
    grad_kv_tokens = (
        grad_kv_local
        + grad_owned
        + jnp.concatenate([row_heads(grad_local_key), row_heads(grad_local_value)], axis=-1)
    )
    grad_packed = (
        jnp.concatenate([grad_query_tokens, grad_kv_tokens], axis=-1) + owner_part
    ).astype(bfloat)
    column_scale = jnp.concatenate(
        [jnp.full((model_width,), query_scale, single), jnp.ones((2 * model_width,), single)]
    )
    grad_entry = (
        (grad_packed.astype(single) * column_scale).astype(bfloat).reshape(-1, 3 * model_width)
    )
    entry_weight_grad = jnp.dot(flat_in.T, grad_entry, preferred_element_type=single)
    query_bias_grad = jnp.sum(grad_entry[:, :model_width].astype(single), axis=0)
    value_bias_grad = jnp.sum(grad_entry[:, 2 * model_width :].astype(single), axis=0)
    input_grad = (
        (grad_resid + jnp.dot(grad_entry, entry_weight.T, preferred_element_type=single))
        .astype(bfloat)
        .reshape(inputs.shape)
    )
    (
        total_entry,
        total_query,
        total_value,
        total_out,
        total_out_bias,
        total_norm_gain,
        total_norm_shift,
        total_inner,
        total_inner_bias,
        total_outer,
        total_outer_bias,
        total_final_gain,
        total_final_shift,
    ) = lax.psum(
        (
            entry_weight_grad,
            query_bias_grad,
            value_bias_grad,
            out_weight_grad,
            out_bias_grad,
            norm_gain_grad,
            norm_shift_grad,
            inner_weight_grad,
            inner_bias_grad,
            outer_weight_grad,
            outer_bias_grad,
            final_gain_grad,
            final_shift_grad,
        ),
        ("dp", "seq"),
    )
    return (
        layer_out,
        input_grad,
        total_entry,
        total_query,
        total_value,
        total_out,
        total_out_bias,
        total_norm_gain,
        total_norm_shift,
        total_inner,
        total_inner_bias,
        total_outer,
        total_outer_bias,
        total_final_gain,
        total_final_shift,
    )


def solution(mesh):
    in_specs = (
        P("dp", "seq", None),
        P("dp", None, "seq", None),
        P(),
        P(),
        P(),
        P(),
        P(),
        P(),
        P(),
        P(),
        P(),
        P(),
        P(),
        P(),
        P(),
        P("dp", "seq", None),
    )
    out_specs = (
        P("dp", "seq", None),
        P("dp", "seq", None),
        P(),
        P(),
        P(),
        P(),
        P(),
        P(),
        P(),
        P(),
        P(),
        P(),
        P(),
        P(),
        P(),
    )
    return jax.shard_map(
        on_device, mesh=mesh, in_specs=in_specs, out_specs=out_specs, check_vma=False
    )
```

profile of v0, /device:TPU:0, one launch (start us, length us, event | category | flops | bytes accessed | tf_op | source)
XLA Modules:
  0.0 860.7 jit_solution(11020319071241141336)
XLA Ops:
  19.2 53.5 %all-reduce.22.cloned.1.call-done = (bf16[3,64,1536]{2,1,0:T(8,128)(2,1)}, bf16[3,64,1536]{2,1,0:T(8,128)(2,1)}) async-done(((bf16[3,64,1536]{2,1,0:T(8,128)(2,1)}, bf16[3,64,1536]{2,1,0:T(8,128)(2,1)}), (bf16[3,64,1536]{2,1,0:T(8,128)(2,1)}, bf16[3,64,1536]{2,1,0:T(8,128)(2,1)})) %all-reduce.22.cloned.1.call-update) | async-done | bytes 1179664 | tf_op jit(solution)/shard_map/psum | solution.py:20
  88.0 3.3 all-to-all-start
  92.3 3.1 collective-permute-start
  101.5 3.2 reshape.448
  104.7 4.2 copy.171
  108.9 3.2 reshape_reshape.10
  114.8 3.6 broadcast_select_fusion
  118.4 6.2 all-to-all-start.1
  129.1 5.2 reshape.442
  134.3 7.1 copy.254
  141.4 6.3 reshape.443
  155.5 4.2 copy.166
  159.7 3.1 broadcast_in_dim.143
  164.5 10.7 %all-gather.1 = f32[24,8,128]{2,1,0:T(8,128)S(1)} all-gather(f32[3,8,128]{2,1,0:T(8,128)S(1)} %fusion.34), channel_id=3, replica_groups=mesh['dp'=4,'seq'=8] {'seq'}, dimensions={0}, use_global_device_ids=true | all-gather | bytes 110592 | tf_op jit(solution)/shard_map/all_gather | solution.py:45
  175.2 8.6 all-gather
  185.4 4.2 gather_fusion.1
  189.6 4.0 constant_dynamic-update-slice_fusion.2
  193.6 5.2 select_reduce_fusion
  204.3 42.5 %while.19 = (s32[]{:T(128)}, f32[3,8,128]{2,1,0:T(8,128)S(1)}, f32[3,8,128]{2,1,0:T(8,128)S(1)}, f32[3,8,128,64]{3,2,1,0:T(8,128)}, f32[8,3,8,128]{3,2,1,0:T(8,1...) while((s32[]{:T(128)}, f32[3,8,128]{2,1,0:T(8,128)S(1)}, ...), condition=%wide.region_5.6_spmd, body=%wide.region_4.5_spmd.sunk | while | flops 608261 | bytes 5628047 | solution.py:50
  207.1 3.2 fusion.133
  213.2 3.2 fusion.133
  219.3 3.2 fusion.133
  225.3 3.2 fusion.133
  231.4 3.2 fusion.133
  237.5 3.2 fusion.133
  243.6 3.2 fusion.133
  254.6 9.4 %select_convert_fusion = bf16[3,8,2,64,64]{4,3,2,1,0:T(8,128)(2,1)} fusion(bf16[3,8,2,512,128]{4,3,2,1,0:T(8,128)(2,1)} %bitcast.35, f32[3,8,2,64,512]{4,3,2,1,0:T(8,128)} %copy-done.2, f32[3,8,2,64]{3,2,1,0:T(2,128)S(1)} %fusion.3, f32[3,8,2,64]{3,2,1,0:T(2,128)S(1)} %get-tuple-element.361, pred[2,512]{1,0:T(4,128)(4,1)S(1)} %and_or_fusion, ...), kind=kOutput, calls=%fused_computation.79 | convolution fusion | flops 208011264 | bytes 13394948 | tf_op jit(solution)/shard_map/shiqk,shikd->shiqd/dot_general | solution.py:230
  268.3 7.4 multiply_convert_fusion.1
  289.3 4.9 fusion.103
  294.9 6.8 fusion.13
  301.7 6.3 multiply_reduce_fusion
  309.8 5.3 fusion.10
  315.1 3.6 fusion.56
  318.7 11.7 %pad_maximum_fusion = f32[3,8,2,512,128]{3,4,2,1,0:T(8,128)} fusion(f32[3,8,2,512,64]{3,4,2,1,0:T(8,128)} %fusion.13, f32[3,8,2,512,64]{3,4,2,1,0:T(8,128)} %fusion.56), kind=kLoop, calls=%fused_computation.14 | loop fusion | flops 3145728 | bytes 25165824 | tf_op jit(solution)/shard_map/concatenate | solution.py:312
  330.5 12.6 %copy.186 = f32[3,8,2,512,128]{4,3,2,1,0:T(8,128)} copy(f32[3,8,2,512,128]{3,4,2,1,0:T(8,128)} %pad_maximum_fusion) | data formatting | bytes 25165824 | tf_op jit(solution)/shard_map/concatenate | solution.py:312
  343.1 3.3 slice_reduce_fusion
  346.4 5.2 slice.199
  351.6 4.9 slice_bitcast_fusion.2
  358.1 3.2 reshape.466
  364.3 3.4 reshape.467
  367.7 3.1 broadcast_in_dim.156
  370.8 21.7 %scatter_fusion = f32[168,64,128]{2,1,0:T(8,128)} fusion(f32[168,64,128]{2,1,0:T(8,128)} %broadcast_in_dim.156, s32[144]{0:T(256)S(1)} %bitcast.265, f32[144,64,128]{2,1,0:T(8,128)} %bitcast.216), kind=kCustom, calls=%fused_computation.3 | custom fusion | bytes 14156352 | tf_op jit(solution)/shard_map/scatter | solution.py:339
  392.5 4.8 convert_element_type.200
  397.3 4.6 all-to-all-start.2
  401.9 4.2 pad_add_fusion
  406.1 7.3 reshape.457
  413.4 9.8 %copy.189 = f32[3,4,64,2,8,64]{5,4,3,2,1,0:T(8,128)} copy(f32[3,4,64,2,8,64]{5,3,2,1,4,0:T(2,128)} %bitcast.215) | data formatting | bytes 6291456 | tf_op jit(solution)/shard_map/transpose | solution.py:76
  423.2 6.3 reshape.458
  431.8 3.0 collective-permute-start.2
  436.2 27.8 %all-reduce.8 = (bf16[3,8,64]{2,1,0:T(8,128)(2,1)S(1)}, bf16[3,8,64]{2,1,0:T(8,128)(2,1)S(1)}) all-reduce(bf16[3,8,64]{2,1,0:T(8,128)(2,1)S(1)} %convert_select_fusion, bf16[3,8,64]{2,1,0:T(8,128)(2,1)S(1)} %convert_select_fusion.1), channel_id=1, replica_groups=mesh['dp'=4,'seq'=8] {'seq'}, use_global_device_ids=true, to_apply=%region_28.29 | all-reduce | flops 3072 | bytes 12288 | tf_op jit(solution)/shard_map/psum | solution.py:20
  464.0 4.9 fusion.88
  469.0 25.4 %all-reduce.20.cloned.1.call-done = (bf16[3,8,64,64]{2,3,1,0:T(8,128)(2,1)}, bf16[3,8,64,64]{2,3,1,0:T(8,128)(2,1)}) async-done(((bf16[3,8,64,64]{2,3,1,0:T(8,128)(2,1)}, bf16[3,8,64,64]{2,3,1,0:T(8,128)(2,1)}), (bf16[3,8,64,64]{2,3,1,0:T(8,128)(2,1)}, bf16[3,8,64,64]{2,3,1,0:T(8,128)(2,1)})) %all-reduce.20.cloned.1.call-update) | async-done | bytes 393232 | tf_op jit(solution)/shard_map/psum | solution.py:20
  500.3 3.9 fusion.35
  511.7 3.2 maximum_convert_fusion
  514.9 49.2 %all-reduce.16.cloned.1.call-done = bf16[3,128,1536]{2,1,0:T(8,128)(2,1)} async-done(((bf16[3,128,1536]{2,1,0:T(8,128)(2,1)}), bf16[3,128,1536]{2,1,0:T(8,128)(2,1)}) %all-reduce.16.cloned.1.call-update) | async-done | bytes 1179664 | tf_op jit(solution)/shard_map/psum | solution.py:380
  565.3 4.9 bitcast_convert_fusion
  570.4 18.2 %scatter_fusion.1 = f32[49,64,128]{2,1,0:T(8,128)S(1)} fusion(f32[49,64,128]{2,1,0:T(8,128)S(1)} %broadcast_in_dim.155, s32[168]{0:T(256)S(1)} %bitcast.266, f32[168,64,128]{2,1,0:T(8,128)} %bitcast_convert_fusion), kind=kCustom, calls=%fused_computation.4 | custom fusion | flops 1376256 | bytes 16515744 | tf_op jit(solution)/shard_map/scatter-add | solution.py:346
  590.0 4.1 reshape_reshape.12
  594.1 5.3 copy.190
  602.4 3.6 fusion.32
  610.9 41.4 %all-reduce.6 = (f32[512]{0:T(512)}, f32[512]{0:T(512)}, f32[512]{0:T(512)}, f32[512]{0:T(512)}, f32[512]{0:T(512)}, /*index=5*/f32[2048]{0:T(1024)}, f32[512]{0:T(512)}, f32[512]{0:T(512)}, f32[512]{0:T(512)}) all-reduce(f32[512]{0:T(512)S(1)} %get-tuple-element.289, ...), channel_id=1, replica_groups=mesh['dp'=4,'seq'=8] {'dp','seq'}, use_global_device_ids=true, to_apply=%region_33.34 | all-reduce | flops 6144 | bytes 49152 | tf_op jit(solution)/shard_map/psum | solution.py:423
  655.2 187.0 %all-reduce.18.cloned.1.call-done = (f32[512,1536]{0,1:T(8,128)}, f32[512,512]{1,0:T(8,128)}, f32[512,2048]{1,0:T(8,128)}, f32[2048,512]{1,0:T(8,128)}) async-done(((f32[512,1536]{0,1:T(8,128)}, f32[512,512]{1,0:T(8,128)}, f32[512,2048]{1,0:T(8,128)}, f32[2048,512]{1,0:T(8,128)}), (f32[512,1536]{0,1:T(8,128)}, f32[512,512]{1,0:T(8,128)}, f32[512,2048]{1,0:T(8,128)}, ...) | async-done | bytes 12582928 | tf_op jit(solution)/shard_map/psum | solution.py:423
  842.3 3.6 copy.204
  846.9 4.8 copy.286
  (279 shorter events, 143.8 us)
Async XLA Ops:
  7.2 261.1 %copy-start = (bf16[512,2048]{1,0:T(8,128)(2,1)S(1)}, bf16[512,2048]{1,0:T(8,128)(2,1)}, u32[]{:S(2)}) copy-start(bf16[512,2048]{1,0:T(8,128)(2,1)} %param.27) | copy-start | bytes 6291460
  7.2 65.5 %all-reduce.22.cloned.1.call-start = ((), (), s32[]{:S(2)}) async-start(), calls=%async_computation.7 | async-start | bytes 2359296 | tf_op jit(solution)/shard_map/psum | solution.py:20
  11.3 86.3 %copy-start.5 = (bf16[384,512]{1,0:T(8,128)(2,1)}, bf16[384,512]{1,0:T(8,128)(2,1)S(1)}, u32[]{:S(2)}) copy-start(bf16[384,512]{1,0:T(8,128)(2,1)S(1)} %get-tuple-element.348) | copy-start | bytes 1179652
  12.6 188.9 %all-gather.5.cloned.1.call-start = ((), (), s32[]{:S(2)}) async-start(), calls=%async_computation.4 | async-start | bytes 7077888 | tf_op jit(solution)/shard_map/all_gather | solution.py:45
  74.9 1.0 copy-start.24
  78.6 5.8 copy-start.33
  80.2 1.2 copy-start.3
  80.2 17.3 %copy-start.38 = (bf16[512]{0:T(512)(128)(2,1)S(1)}, bf16[512]{0:T(512)(128)(2,1)}, u32[]{:S(2)}) copy-start(bf16[512]{0:T(512)(128)(2,1)} %param.25) | copy-start | bytes 3076
  80.2 17.3 %copy-start.39 = (bf16[512]{0:T(512)(128)(2,1)S(1)}, bf16[512]{0:T(512)(128)(2,1)}, u32[]{:S(2)}) copy-start(bf16[512]{0:T(512)(128)(2,1)} %param.26) | copy-start | bytes 3076
  80.2 17.3 %copy-start.40 = (bf16[512]{0:T(512)(128)(2,1)S(1)}, bf16[512]{0:T(512)(128)(2,1)}, u32[]{:S(2)}) copy-start(bf16[512]{0:T(512)(128)(2,1)} %param.31) | copy-start | bytes 3076
  80.3 17.3 %copy-start.41 = (bf16[512]{0:T(512)(128)(2,1)S(1)}, bf16[512]{0:T(512)(128)(2,1)}, u32[]{:S(2)}) copy-start(bf16[512]{0:T(512)(128)(2,1)} %param.24) | copy-start | bytes 3076
  80.3 17.3 %copy-start.42 = (bf16[512]{0:T(512)(128)(2,1)S(1)}, bf16[512]{0:T(512)(128)(2,1)}, u32[]{:S(2)}) copy-start(bf16[512]{0:T(512)(128)(2,1)} %param.30) | copy-start | bytes 3076
  84.4 14.3 %copy-start.43 = (bf16[512]{0:T(512)(128)(2,1)S(1)}, bf16[512]{0:T(512)(128)(2,1)}, u32[]{:S(2)}) copy-start(bf16[512]{0:T(512)(128)(2,1)} %param.32) | copy-start | bytes 3076
  84.4 14.3 %copy-start.36 = (bf16[2048]{0:T(1024)(128)(2,1)S(1)}, bf16[2048]{0:T(1024)(128)(2,1)}, u32[]{:S(2)}) copy-start(bf16[2048]{0:T(1024)(128)(2,1)} %param.28) | copy-start | bytes 12292
  88.0 24.2 %all-to-all-start = ((s32[8,1,21]{2,1,0:T(1,128)}), s32[8,1,21]{2,1,0:T(1,128)S(1)}, u32[]{:S(2)}, u32[]{:S(2)}) async-start(s32[8,1,21]{2,1,0:T(1,128)} %all_to_all.14), calls=%async_computation | async-start | bytes 8192 | tf_op jit(solution)/shard_map/all_to_all | solution.py:185
  92.3 34.3 %collective-permute-start = (bf16[3,64,1024]{2,1,0:T(8,128)(2,1)}, bf16[3,64,1024]{2,1,0:T(8,128)(2,1)}, u32[]{:S(2)}, u32[]{:S(2)}) collective-permute-start(bf16[3,64,1024]{2,1,0:T(8,128)(2,1)} %get-tuple-element.358), channel_id=1, source_target_pairs={{0,1},{1,2},{2,3},{3,4},{4,5},{5,6},{6,7},{8,9},{9,10},{10,11},{11... | collective-permute-start | bytes 1179656 | tf_op jit(solution)/shard_map/ppermute | solution.py:36
  95.4 31.3 %collective-permute-start.1 = (bf16[3,64,1024]{2,1,0:T(8,128)(2,1)}, bf16[3,64,1024]{2,1,0:T(8,128)(2,1)}, u32[]{:S(2)}, u32[]{:S(2)}) collective-permute-start(bf16[3,64,1024]{2,1,0:T(8,128)(2,1)} %get-tuple-element.359), channel_id=1, source_target_pairs={{1,0},{2,1},{3,2},{4,3},{5,4},{6,5},{7,6},{9,8},{10,9},{11,10},{12... | collective-permute-start | bytes 1179656 | tf_op jit(solution)/shard_map/ppermute | solution.py:39
  118.4 8.2 copy-start.6
  118.4 67.0 %all-to-all-start.1 = ((bf16[8,21,64,128]{3,2,1,0:T(8,128)(2,1)}), bf16[8,21,64,128]{3,2,1,0:T(8,128)(2,1)}, u32[]{:S(2)}, u32[]{:S(2)}) async-start(bf16[8,21,64,128]{3,2,1,0:T(8,128)(2,1)} %broadcast_select_fusion), calls=%async_computation.1 | async-start | bytes 5505024 | tf_op jit(solution)/shard_map/all_to_all | solution.py:191
  147.7 4.7 copy-start.7
  147.7 5.8 copy-start.25
  189.6 4.0 copy-start.8
  198.8 2.7 copy-start.2
  254.6 11.7 %copy-start.26 = (bf16[3,128,512]{2,1,0:T(8,128)(2,1)S(1)}, bf16[3,128,512]{2,1,0:T(8,128)(2,1)}, u32[]{:S(2)}) copy-start(bf16[3,128,512]{2,1,0:T(8,128)(2,1)} %param.18) | copy-start | bytes 1179652
  268.0 14.4 %copy-start.10 = (f32[384,512]{1,0:T(8,128)}, f32[384,512]{1,0:T(8,128)S(1)}, u32[]{:S(2)}) copy-start(f32[384,512]{1,0:T(8,128)S(1)} %get-tuple-element.366) | copy-start | bytes 2359300
  268.3 7.4 copy-start.44
  275.7 1.1 copy-start.19
  275.7 1.4 copy-start.16
  280.7 1.7 copy-start.30
  282.4 1.0 copy-start.32
  282.4 1.4 copy-start.28
  282.8 2.8 copy-start.21
  289.3 12.4 %slice-start = ((s8[6291456]{0:T(1024)(128)(4,1)}), s8[4194304]{0:T(1024)(128)(4,1)S(1)}, s32[]{:S(2)}) async-start(s8[6291456]{0:T(1024)(128)(4,1)} %bitcast.210), calls=%async_computation.8 | async-start | bytes 8388608
  294.9 6.8 slice-start.1
  309.8 5.3 copy-start.9
  351.6 4.9 copy-start.13
  397.3 4.6 copy-start.12
  397.3 168.0 %all-to-all-start.2 = ((bf16[8,21,64,128]{3,2,1,0:T(8,128)(2,1)}), bf16[8,21,64,128]{3,2,1,0:T(8,128)(2,1)}, u32[]{:S(2)}, u32[]{:S(2)}) async-start(bf16[8,21,64,128]{3,2,1,0:T(8,128)(2,1)} %bitcast.229), calls=%async_computation.2 | async-start | bytes 5505024 | tf_op jit(solution)/shard_map/all_to_all | solution.py:342
  401.9 92.5 %all-reduce.20.cloned.1.call-start = ((), (), s32[]{:S(2)}) async-start(), calls=%async_computation.6 | async-start | bytes 1572864 | tf_op jit(solution)/shard_map/psum | solution.py:20
  429.6 34.5 %copy-start.11 = (f32[384,512]{1,0:T(8,128)S(1)}, f32[384,512]{1,0:T(8,128)}, u32[]{:S(2)}) copy-start(f32[384,512]{1,0:T(8,128)} %copy-done.10) | copy-start | bytes 2359300
  431.8 77.9 %collective-permute-start.2 = (bf16[3,64,1024]{2,1,0:T(8,128)(2,1)S(1)}, bf16[3,64,1024]{2,1,0:T(8,128)(2,1)}, u32[]{:S(2)}, u32[]{:S(2)}) collective-permute-start(bf16[3,64,1024]{2,1,0:T(8,128)(2,1)S(1)} %get-tuple-element.349), channel_id=1, source_target_pairs={{0,1},{1,2},{2,3},{3,4},{4,5},{5,6},{6,7},{8,9},{9,10},{10,11},{11... | collective-permute-start | bytes 1179656 | tf_op jit(solution)/shard_map/ppermute | solution.py:36
  434.8 74.9 %collective-permute-start.3 = (bf16[3,64,1024]{2,1,0:T(8,128)(2,1)S(1)}, bf16[3,64,1024]{2,1,0:T(8,128)(2,1)}, u32[]{:S(2)}, u32[]{:S(2)}) collective-permute-start(bf16[3,64,1024]{2,1,0:T(8,128)(2,1)S(1)} %get-tuple-element.350), channel_id=1, source_target_pairs={{1,0},{2,1},{3,2},{4,3},{5,4},{6,5},{7,6},{9,8},{10,9},{11,10},{12... | collective-permute-start | bytes 1179656 | tf_op jit(solution)/shard_map/ppermute | solution.py:39
  436.1 128.0 %all-reduce.16.cloned.1.call-start = ((), (), s32[]{:S(2)}) async-start(), calls=%async_computation.3 | async-start | bytes 2359296 | tf_op jit(solution)/shard_map/psum | solution.py:380
  464.0 30.3 %copy-start.4 = (f32[3,8,128,128]{2,3,1,0:T(8,128)S(1)}, f32[3,8,128,128]{2,3,1,0:T(8,128)}, u32[]{:S(2)}) copy-start(f32[3,8,128,128]{2,3,1,0:T(8,128)} %copy-done.3) | copy-start | bytes 4718596
  500.3 3.9 copy-start.23
  500.3 3.9 copy-start.29
  504.2 3.8 copy-start.18
  507.6 334.6 %all-reduce.18.cloned.1.call-start = ((), (), s32[]{:S(2)}) async-start(), calls=%async_computation.5 | async-start | bytes 25165824 | tf_op jit(solution)/shard_map/psum | solution.py:423
  565.3 5.1 copy-start.35
  599.5 2.9 copy-start.37
  602.4 3.6 copy-start.14
  602.4 3.6 copy-start.20
  602.4 3.6 copy-start.34
  606.0 1.0 copy-start.27
  609.7 1.0 copy-start.17
  609.7 42.6 %copy-start.22 = (f32[384,512]{1,0:T(8,128)S(1)}, f32[384,512]{1,0:T(8,128)}, u32[]{:S(2)}) copy-start(f32[384,512]{1,0:T(8,128)} %copy-done.21) | copy-start | bytes 2359300
  842.3 3.6 copy-start.31
  846.9 4.9 copy-start.15
  846.9 6.9 copy-start.1
Sparse Core Ops, SparseCore 0:
  12.7 59.9 all-reduce.21
  84.5 48.6 all-gather.4
  436.2 58.0 all-reduce.19
  507.8 56.3 all-reduce.15
  609.8 232.4 all-reduce.17
where the time goes:
time: 873 us; the launch traced here: 861 us
  waiting for transfers between devices  315 us (36%)
  local copies, waits for them, and re-layouts  228 us (26%)
  other arithmetic  108 us (12%)
  blocking collectives  88.4 us (10%)
  matrix products  82.8 us (9%)
  starting transfers between devices  23.1 us (3%)
  between operations  15.2 us (2%)
    psum x1, waiting for transfers between devices, on_device(): lax.psum((entry_weight_grad, query_bias_grad, value_bias_grad, out_weight...  187 us
    psum x2, waiting for transfers between devices, spread_2(): return lax.psum(jnp.where(mine, value, jnp.zeros_like(value)), axis)  78.9 us
    psum x1, waiting for transfers between devices, on_device(): lax.psum(partials.astype(jnp.bfloat16), 'seq').astype(jnp.float32)  49.2 us
    psum x1, blocking collectives, on_device(): lax.psum((entry_weight_grad, query_bias_grad, value_bias_grad, out_weight...  41.4 us
    psum x1, blocking collectives, spread_2(): return lax.psum(jnp.where(mine, value, jnp.zeros_like(value)), axis)  27.8 us
    unnamed x103, local copies, waits for them, and re-layouts  25.3 us
    add x7, other arithmetic, merge_parts(): out_one * factor_one[..., None] + out_two * factor_two[..., None]  22.7 us
    scatter x1, local copies, waits for them, and re-layouts, on_device(): outgoing = jnp.zeros((devices * capacity, block_rows, 2 * head_width), si...  21.7 us
  transfers between devices with their start and end apart: 12, of which 4 were waited for; matrix products, arithmetic and copies ran while one was open for 17% of the time, Pallas kernels for 0%

commit v1 on v0

--- a/solution.py
+++ b/solution.py
@@ -3,6 +3,8 @@
 import jax
 import jax.numpy as jnp
 from jax import lax
+from jax.experimental import pallas as pl
+from jax.experimental.pallas import tpu as pltpu
 from jax.sharding import PartitionSpec as P
 
 HEADS = 8
@@ -457,6 +459,887 @@
     )
 
 
+MESH = pl.DeviceIdType.MESH
+bfloat = jnp.bfloat16
+single = jnp.float32
+WIDE = 512
+PIECE = 256
+QUERIES = 256
+INV_SQRT2 = 0.7071067811865476
+INV_SQRT_2PI = 0.3989422804014327
+
+
+def dot(a, b, a_dim, b_dim):
+    return lax.dot_general(
+        a, b, (((a_dim,), (b_dim,)), ((), ())), preferred_element_type=single
+    )
+
+
+def aligned(index, step):
+    return pl.multiple_of(index, step)
+
+
+class Place:
+    def __init__(self, groups):
+        self.groups = groups
+        self.z = lax.axis_index("dp")
+        self.me = lax.axis_index("seq")
+        self.y = self.me // 4
+        self.x = (self.me // 2) % 2
+        self.core = self.me % 2
+
+    def peer(self, offset):
+        off_y, off_x, off_core = offset // 4, (offset // 2) % 2, offset % 2
+        return (
+            ((self.y + off_y) % 2) * 4
+            + ((self.x + off_x) % 2) * 2
+            + (self.core + off_core) % 2
+        )
+
+    def in_plane(self, offset):
+        return (self.z, self.peer(offset))
+
+    def in_column(self, offset):
+        return ((self.z + offset) % self.groups, self.me)
+
+
+def remote(src, dst, send, recv, device):
+    return pltpu.make_async_remote_copy(
+        src_ref=src,
+        dst_ref=dst,
+        send_sem=send,
+        recv_sem=recv,
+        device_id=device,
+        device_id_type=MESH,
+    )
+
+
+def layer_kernel(
+    groups,
+    cut,
+    x_ref,
+    blocks_ref,
+    we_hbm,
+    qb_ref,
+    vb_ref,
+    wo_hbm,
+    bo_ref,
+    g1_ref,
+    s1_ref,
+    w1_hbm,
+    b1_ref,
+    w2_hbm,
+    b2_ref,
+    g2_ref,
+    s2_ref,
+    cot_hbm,
+    out_ref,
+    dx_ref,
+    sums_hbm,
+    small_ref,
+    we,
+    wo,
+    w1,
+    w2,
+    cot,
+    load_sem,
+    send_qkv,
+    qkv,
+    krow,
+    vrow,
+    probs,
+    inv_total,
+    out_wide,
+    out_low,
+    att_t,
+    hat1,
+    rstd1,
+    low1,
+    hidden,
+    slope,
+    grad_inner,
+    grad_outer,
+    grad_resid,
+    grad_branch,
+    gatt_t,
+    dout_t,
+    dqkv,
+    dk_acc,
+    dv_acc,
+    gpacked_t,
+    x_t,
+    part,
+    r0,
+    r1,
+    r2,
+    r3,
+    total,
+    small_in,
+    a_send,
+    a_recv,
+    o_send,
+    o_recv,
+    d_send,
+    d_recv,
+    p_send,
+    p_recv,
+    rs_send,
+    rs_recv,
+    z_send,
+    z_recv,
+    v_send,
+    v_recv,
+    done_sem,
+):
+    seqs, tokens, width = x_ref.shape
+    rows = seqs * tokens
+    place = Place(groups)
+    me = place.me
+    barrier = pltpu.get_barrier_semaphore()
+    for k in range(1, 8):
+        pl.semaphore_signal(
+            barrier, inc=1, device_id=place.in_plane(k), device_id_type=MESH
+        )
+    for k in range(1, groups):
+        pl.semaphore_signal(
+            barrier, inc=1, device_id=place.in_column(k), device_id_type=MESH
+        )
+    loads = [
+        pltpu.make_async_copy(src, dst, load_sem.at[i])
+        for i, (src, dst) in enumerate(
+            ((we_hbm, we), (wo_hbm, wo), (w1_hbm, w1), (w2_hbm, w2), (cot_hbm, cot))
+        )
+    ]
+    for load in loads:
+        load.start()
+
+    lane = lax.broadcasted_iota(jnp.int32, (16, tokens), 1)
+    key_block = lax.broadcasted_iota(jnp.int32, (16, tokens), 0)
+    query_block = me * 2 + lane // BLOCK
+    inside = (key_block >= 1) & (key_block <= 14)
+    near = (key_block >= query_block - 1) & (key_block <= query_block + 1) & inside
+    fixed = jnp.where(near, 1.0, 0.0) + jnp.where(inside, 0.0, 1.0)
+    outer_query = (query_block == 0) | (query_block == 15)
+    for s in range(seqs):
+        for h in range(HEADS):
+            times = fixed
+            for j in range(3):
+                picked = jnp.where(
+                    lane < BLOCK, blocks_ref[s, h, 0, j], blocks_ref[s, h, 1, j]
+                )
+                times = times + jnp.where(picked == key_block, 1.0, 0.0)
+            send_qkv[s, h, 3 * HEAD :, :] = jnp.where(outer_query, 1.0, times).astype(bfloat)
+    for s in range(seqs):
+        x_t[:, s * tokens : (s + 1) * tokens] = x_ref[s].T
+    small_ref[...] = jnp.zeros(small_ref.shape, single)
+
+    def vec(ref):
+        return ref[...].astype(single).reshape(1, ref.shape[0])
+
+    pl.semaphore_wait(barrier, 7 + groups - 1)
+    loads[0].wait()
+
+    def qkv_copy(s, k):
+        other = place.peer(k)
+        return other, remote(
+            send_qkv.at[s, other],
+            qkv.at[s, :, pl.ds(aligned(me * tokens, 128), tokens)],
+            a_send.at[s, k],
+            a_recv.at[s, k],
+            place.in_plane(k),
+        )
+
+    def pack(s, _):
+        packed = jnp.dot(x_ref[s], we[...], preferred_element_type=single)
+        for j, bias in enumerate((qb_ref, None, vb_ref)):
+            piece = packed[:, j * width : (j + 1) * width]
+            if bias is not None:
+                piece = piece + vec(bias)
+            if j == 0:
+                piece = piece * HEAD**-0.5
+            piece = piece.astype(bfloat).T
+            for h in range(HEADS):
+                send_qkv[s, h, j * HEAD : (j + 1) * HEAD, :] = piece[
+                    h * HEAD : (h + 1) * HEAD
+                ]
+        for k in (6, 7, 2, 3, 4, 5, 1):
+            qkv_copy(s, k)[1].start()
+        own = pl.ds(aligned(me * tokens, 128), tokens)
+        qkv[s, :, own] = send_qkv[s, me]
+        return 0
+
+    lax.fori_loop(0, seqs, pack, 0)
+
+    def arrived_at(ref_of, send, recv, s):
+        for k in range(1, 8):
+            other = place.peer(k)
+            slot = ref_of(other)
+            remote(slot, slot, send.at[s, k], recv.at[s, k], place.in_plane(k)).wait_recv()
+
+    def sent(ref_of, send, recv, s):
+        for k in range(1, 8):
+            slot = ref_of(place.peer(k))
+            remote(slot, slot, send.at[s, k], recv.at[s, k], place.in_plane(k)).wait_send()
+
+    def lanes_of(device):
+        return pl.ds(aligned(device * tokens, 128), tokens)
+
+    length = qkv.shape[2]
+    chunks = length // QUERIES
+
+    def attend(s, _):
+        arrived_at(lambda other: qkv.at[s, :, lanes_of(other)], a_send, a_recv, s)
+        krow[s] = qkv[s, HEAD : 2 * HEAD, :].T
+        vrow[s] = qkv[s, 2 * HEAD : 3 * HEAD, :].T
+
+        def chunk(i, _):
+            at = pl.ds(aligned(i * QUERIES, QUERIES), QUERIES)
+            score = jnp.dot(krow[s], qkv[s, 0:HEAD, at], preferred_element_type=single)
+            times = qkv[s, 3 * HEAD :, at].astype(single)
+            bias = jnp.where(times > 1.5, 0.6931471805599453, 0.0)
+            bias = jnp.where(times > 0.5, bias, NEGATIVE)
+            score = score.reshape(16, BLOCK, QUERIES) + bias[:, None, :]
+            score = score.reshape(length, QUERIES)
+            peak = jnp.max(score, axis=0, keepdims=True)
+            grown = jnp.exp(score - peak)
+            inverse = 1.0 / jnp.sum(grown, axis=0, keepdims=True)
+            grown = grown.astype(bfloat)
+            probs[s, :, at] = grown
+            inv_total[s, :, at] = inverse
+            result = inverse * jnp.dot(
+                qkv[s, 2 * HEAD : 3 * HEAD, :], grown, preferred_element_type=single
+            )
+            out_wide[s, :, at] = result
+            out_low[s, :, at] = result.astype(bfloat)
+            return 0
+
+        lax.fori_loop(0, chunks, chunk, 0)
+        for k in (6, 7, 2, 3, 4, 5, 1):
+            out_copy(s, k).start()
+        att_t[head_rows_of(me), seq_lanes(s)] = out_low[s, :, lanes_of(me)]
+        return 0
+
+    def head_rows_of(device):
+        return pl.ds(aligned(device * HEAD, HEAD), HEAD)
+
+    def seq_lanes(s):
+        return pl.ds(aligned(s * tokens, 128), tokens)
+
+    def out_copy(s, k):
+        return remote(
+            out_low.at[s, :, lanes_of(place.peer(k))],
+            att_t.at[head_rows_of(me), seq_lanes(s)],
+            o_send.at[s, k],
+            o_recv.at[s, k],
+            place.in_plane(k),
+        )
+
+    lax.fori_loop(0, seqs, attend, 0)
+    for load in loads[1:]:
+        load.wait()
+
+    def dout_copy(s, k):
+        return remote(
+            gatt_t.at[head_rows_of(place.peer(k)), seq_lanes(s)],
+            dout_t.at[s, :, lanes_of(me)],
+            d_send.at[s, k],
+            d_recv.at[s, k],
+            place.in_plane(k),
+        )
+
+    def mean_of(value):
+        return jnp.mean(value, axis=-1, keepdims=True)
+
+    def add_small(row, value):
+        small_ref[row : row + 1, :] += jnp.sum(value, axis=0, keepdims=True)
+
+    def tokens_part(s, _):
+        arrived_at(lambda other: att_t.at[head_rows_of(other), seq_lanes(s)], o_send, o_recv, s)
+        here = pl.ds(aligned(s * tokens, 128), tokens)
+        branch = dot(att_t[:, here], wo[...], 0, 0) + vec(bo_ref)
+        resid = x_ref[s].astype(single) + branch
+        center = resid - mean_of(resid)
+        scale1 = lax.rsqrt(mean_of(center * center) + EPSILON)
+        normed1 = center * scale1
+        hat1[here, :] = normed1
+        rstd1[here, :] = scale1
+        first = normed1 * vec(g1_ref) + vec(s1_ref)
+        first_low = first.astype(bfloat)
+        low1[here, :] = first_low
+        second = first + vec(b2_ref)
+        bias1 = vec(b1_ref)
+        for j in range(w1.shape[1] // WIDE):
+            span = slice(j * WIDE, (j + 1) * WIDE)
+            pre = jnp.dot(first_low, w1[:, span], preferred_element_type=single) + bias1[:, span]
+            share = 0.5 * (1.0 + lax.erf(pre * INV_SQRT2))
+            active = (pre * share).astype(bfloat)
+            hidden[here, span] = active
+            slope[:, span] = share + pre * jnp.exp(-0.5 * pre * pre) * INV_SQRT_2PI
+            second = second + jnp.dot(active, w2[span, :], preferred_element_type=single)
+        center = second - mean_of(second)
+        scale2 = lax.rsqrt(mean_of(center * center) + EPSILON)
+        normed2 = center * scale2
+        out_ref[s] = (normed2 * vec(g2_ref) + vec(s2_ref)).astype(bfloat)
+        incoming = cot[s].astype(single)
+        add_small(10, incoming * normed2)
+        add_small(11, incoming)
+        scaled = incoming * vec(g2_ref)
+        grad_second = scale2 * (
+            scaled - mean_of(scaled) - normed2 * mean_of(scaled * normed2)
+        )
+        grad_low = grad_second.astype(bfloat)
+        grad_outer[here, :] = grad_low
+        add_small(9, grad_low.astype(single))
+        back = grad_second
+        for j in range(w1.shape[1] // WIDE):
+            span = slice(j * WIDE, (j + 1) * WIDE)
+            grad_hidden = dot(grad_low, w2[span, :], 1, 1)
+            inner = (grad_hidden * slope[:, span]).astype(bfloat)
+            grad_inner[here, span] = inner
+            add_small(5 + j, inner.astype(single))
+            back = back + dot(inner, w1[:, span], 1, 1)
+        normed1 = hat1[here, :]
+        add_small(3, back * normed1)
+        add_small(4, back)
+        scaled = back * vec(g1_ref)
+        grad = rstd1[here, :] * (scaled - mean_of(scaled) - normed1 * mean_of(scaled * normed1))
+        grad_resid[here, :] = grad
+        grad = grad.astype(bfloat)
+        grad_branch[here, :] = grad
+        add_small(2, grad.astype(single))
+        gatt_t[:, here] = dot(wo[...], grad, 1, 1).astype(bfloat)
+        for k in (6, 7, 2, 3, 4, 5, 1):
+            dout_copy(s, k).start()
+        dout_t[s, :, lanes_of(me)] = gatt_t[head_rows_of(me), seq_lanes(s)]
+        return 0
+
+    lax.fori_loop(0, seqs, tokens_part, 0)
+
+    def steps_of(half):
+        along_x, along_y = (place.x, 2), (place.y, 4)
+        return (along_x, along_y) if half == 0 else (along_y, along_x)
+
+    def spans_of(base, count, half):
+        (first, first_off), (last, last_off) = steps_of(half)
+        core_at = base + place.core * (count // 2)
+        core_not = base + (1 - place.core) * (count // 2)
+        first_at = core_at + first * (count // 4)
+        first_not = core_at + (1 - first) * (count // 4)
+        last_at = first_at + last * (count // 8)
+        last_not = first_at + (1 - last) * (count // 8)
+        return (
+            (core_at, core_not, count // 2, 1),
+            (first_at, first_not, count // 4, first_off),
+            (last_at, last_not, count // 8, last_off),
+        )
+
+    def rows_at(start, count):
+        return pl.ds(aligned(start, 16), count)
+
+    def landing(stage, base, count, half):
+        buffer = (r0, r1, r2)[stage]
+        return buffer.at[half, pl.ds(base >> (stage + 1), count), :]
+
+    def reduce_copy(unit, stage, half):
+        index, base, count = unit
+        _, away, size, offset = spans_of(base, count, half)[stage]
+        return remote(
+            part.at[half, rows_at(away, size), :],
+            landing(stage, base, size, half),
+            rs_send.at[index, stage, half],
+            rs_recv.at[index, stage, half],
+            place.in_plane(offset),
+        )
+
+    def add_rows(half, start, buffer, at, size):
+        step = 128 if size % 128 == 0 else 64
+
+        def add(i, _):
+            mine = rows_at(start + i * step, step)
+            other = buffer[half, pl.ds(aligned(at + i * step, 16), step), :]
+            value = part[half, mine, :].astype(single) + other.astype(single)
+            part[half, mine, :] = value.astype(bfloat)
+            return 0
+
+        lax.fori_loop(0, size // step, add, 0)
+
+    def reduce_start(unit, stage):
+        for half in range(2):
+            reduce_copy(unit, stage, half).start()
+
+    def reduce_finish(unit, stage):
+        _, base, count = unit
+        for half in range(2):
+            reduce_copy(unit, stage, half).wait()
+            keep, _, size, _ = spans_of(base, count, half)[stage]
+            add_rows(half, keep, (r0, r1, r2)[stage], base >> (stage + 1), size)
+
+    def column_copy(unit, half, offset):
+        index, base, count = unit
+        keep, _, size, _ = spans_of(base, count, half)[2]
+        size = size // groups
+        target = (place.z + offset) % groups
+        return remote(
+            part.at[half, rows_at(keep + target * size, size), :],
+            r3.at[offset - 1, half, pl.ds(base // (8 * groups), size), :],
+            z_send.at[index, 0, offset - 1, half],
+            z_recv.at[index, 0, offset - 1, half],
+            place.in_column(offset),
+        )
+
+    def column_start(unit):
+        for half in range(2):
+            for offset in range(1, groups):
+                column_copy(unit, half, offset).start()
+
+    def column_back(unit, half, offset):
+        index, base, count = unit
+        keep, _, size, _ = spans_of(base, count, half)[2]
+        size = size // groups
+        at = rows_at(keep + place.z * size, size)
+        return remote(
+            total.at[half, at, :],
+            total.at[half, at, :],
+            z_send.at[index, 1, offset - 1, half],
+            z_recv.at[index, 1, offset - 1, half],
+            place.in_column(offset),
+        )
+
+    def column_back_from(unit, half, offset):
+        index, base, count = unit
+        keep, _, size, _ = spans_of(base, count, half)[2]
+        size = size // groups
+        source = (place.z + groups - offset) % groups
+        at = rows_at(keep + source * size, size)
+        return remote(
+            total.at[half, at, :],
+            total.at[half, at, :],
+            z_send.at[index, 1, offset - 1, half],
+            z_recv.at[index, 1, offset - 1, half],
+            place.in_column(offset),
+        )
+
+    def column_finish(unit):
+        _, base, count = unit
+        for half in range(2):
+            keep, _, size, _ = spans_of(base, count, half)[2]
+            size = size // groups
+            for offset in range(1, groups):
+                column_copy(unit, half, offset).wait()
+            mine = rows_at(keep + place.z * size, size)
+            value = part[half, mine, :].astype(single)
+            for offset in range(1, groups):
+                value = value + r3[
+                    offset - 1, half, pl.ds(base // (8 * groups), size), :
+                ].astype(single)
+            total[half, mine, :] = value.astype(bfloat)
+            for offset in range(1, groups):
+                column_back(unit, half, offset).start()
+
+    def column_end(unit):
+        for half in range(2):
+            for offset in range(1, groups):
+                column_back(unit, half, offset).wait_send()
+                column_back_from(unit, half, offset).wait_recv()
+
+    def gather_copy(unit, stage, half, arriving):
+        index, base, count = unit
+        keep, away, size, offset = spans_of(base, count, half)[stage]
+        at = rows_at(away if arriving else keep, size)
+        return remote(
+            total.at[half, at, :],
+            total.at[half, at, :],
+            rs_send.at[index, 3 + stage, half],
+            rs_recv.at[index, 3 + stage, half],
+            place.in_plane(offset),
+        )
+
+    def gather_start(unit, stage):
+        for half in range(2):
+            gather_copy(unit, stage, half, False).start()
+
+    def gather_finish(unit, stage):
+        for half in range(2):
+            gather_copy(unit, stage, half, False).wait_send()
+            gather_copy(unit, stage, half, True).wait_recv()
+
+    def result_copy(unit):
+        index, base, count = unit
+        return pltpu.make_async_copy(
+            total.at[:, pl.ds(base, count), :],
+            sums_hbm.at[:, pl.ds(base, count), :],
+            done_sem.at[index],
+        )
+
+    ff = hidden.shape[1]
+    outer_unit = (0, 0, ff)
+    inner_unit = (1, ff, ff)
+    out_unit = (2, 2 * ff, width)
+    entry_unit = (3, 2 * ff + width, 3 * width)
+
+    def keep_part(base, value):
+        low = value.astype(bfloat)
+        for half in range(2):
+            part[half, pl.ds(aligned(base, 128), value.shape[0]), :] = low[
+                :, half * PIECE : (half + 1) * PIECE
+            ]
+
+    def outer_tile(j, _):
+        at = pl.ds(aligned(j * WIDE, WIDE), WIDE)
+        keep_part(j * WIDE, dot(hidden[:, at], grad_outer[...], 0, 0))
+        return 0
+
+    def inner_tile(j, _):
+        at = pl.ds(aligned(j * WIDE, WIDE), WIDE)
+        keep_part(ff + j * WIDE, dot(low1[...], grad_inner[:, at], 0, 0))
+        return 0
+
+    lax.fori_loop(0, ff // WIDE, outer_tile, 0)
+    reduce_start(outer_unit, 0)
+    lax.fori_loop(0, ff // WIDE, inner_tile, 0)
+    reduce_start(inner_unit, 0)
+    keep_part(2 * ff, jnp.dot(att_t[...], grad_branch[...], preferred_element_type=single))
+    reduce_start(out_unit, 0)
+
+    def pack_copies(s, k):
+        other = place.peer(k)
+        return [
+            remote(
+                dqkv.at[s, j * HEAD : (j + 1) * HEAD, lanes_of(other)],
+                gpacked_t.at[j, head_rows_of(me), seq_lanes(s)],
+                p_send.at[s, k, j],
+                p_recv.at[s, k, j],
+                place.in_plane(k),
+            )
+            for j in range(3)
+        ]
+
+    def back_chunk(s):
+        def chunk(i, _):
+            at = pl.ds(aligned(i * QUERIES, QUERIES), QUERIES)
+            cot_t = dout_t[s, :, at].astype(single)
+            inverse = inv_total[s, :, at]
+            delta = inverse * jnp.sum(cot_t * out_wide[s, :, at], axis=0, keepdims=True)
+            cot_low = (cot_t * inverse).astype(bfloat)
+            grown = probs[s, :, at]
+            grad = jnp.dot(vrow[s], cot_low, preferred_element_type=single) - delta
+            grad = (grown.astype(single) * grad).astype(bfloat)
+            query_grad = jnp.dot(
+                qkv[s, HEAD : 2 * HEAD, :], grad, preferred_element_type=single
+            )
+            dqkv[s, 0:HEAD, at] = (query_grad.astype(bfloat) * HEAD**-0.5).astype(bfloat)
+            dv_acc[...] += dot(cot_low, grown, 1, 1)
+            dk_acc[...] += dot(qkv[s, 0:HEAD, at], grad, 1, 1)
+            return 0
+
+        return chunk
+
+    def back_begin(s):
+        arrived_at(lambda other: dout_t.at[s, :, lanes_of(other)], d_send, d_recv, s)
+        dk_acc[...] = jnp.zeros(dk_acc.shape, single)
+        dv_acc[...] = jnp.zeros(dv_acc.shape, single)
+
+    def back_end(s):
+        dqkv[s, HEAD : 2 * HEAD, :] = dk_acc[...].astype(bfloat)
+        dqkv[s, 2 * HEAD :, :] = dv_acc[...].astype(bfloat)
+        for k in (6, 7, 2, 3, 4, 5, 1):
+            for copy in pack_copies(s, k):
+                copy.start()
+        for j in range(3):
+            gpacked_t[j, head_rows_of(me), seq_lanes(s)] = dqkv[
+                s, j * HEAD : (j + 1) * HEAD, lanes_of(me)
+            ]
+
+    def ahead(*units_and_stages):
+        for unit, stage in units_and_stages:
+            if stage < 2:
+                reduce_finish(unit, stage)
+                reduce_start(unit, stage + 1)
+            elif stage == 2:
+                reduce_finish(unit, stage)
+                column_start(unit)
+            elif stage == 3:
+                column_finish(unit)
+            elif stage == 4:
+                column_end(unit)
+                gather_start(unit, 2)
+            elif stage == 5:
+                gather_finish(unit, 2)
+                gather_start(unit, 1)
+            elif stage == 6:
+                gather_finish(unit, 1)
+                gather_start(unit, 0)
+            else:
+                gather_finish(unit, 0)
+                result_copy(unit).start()
+
+    ahead((outer_unit, 0), (inner_unit, 0), (out_unit, 0))
+    plan = (
+        ((outer_unit, 1),),
+        ((inner_unit, 1), (out_unit, 1), (outer_unit, 2)),
+        ((inner_unit, 2), (out_unit, 2), (outer_unit, 3)),
+        ((inner_unit, 3), (out_unit, 3), (outer_unit, 4)),
+        ((inner_unit, 4), (out_unit, 4), (outer_unit, 5)),
+        ((inner_unit, 5), (out_unit, 5), (outer_unit, 6)),
+    )
+    for s in range(seqs):
+        back_begin(s)
+        for turn in range(2):
+            half_chunks = chunks // 2
+            lax.fori_loop(turn * half_chunks, (turn + 1) * half_chunks, back_chunk(s), 0)
+            if turn == 1:
+                back_end(s)
+            ahead(*plan[2 * s + turn])
+
+    for s in range(seqs):
+        for k in range(1, 8):
+            other = place.peer(k)
+            for j in range(3):
+                slot = gpacked_t.at[j, head_rows_of(other), seq_lanes(s)]
+                remote(
+                    slot, slot, p_send.at[s, k, j], p_recv.at[s, k, j], place.in_plane(k)
+                ).wait_recv()
+    entry_base = entry_unit[1]
+    for j in range(3):
+        keep_part(entry_base + j * width, dot(x_t[...], gpacked_t[j], 1, 1))
+    reduce_start(entry_unit, 0)
+    ones = jnp.ones((8, rows), bfloat)
+    small_ref[0:1, :] = dot(ones, gpacked_t[0], 1, 1)[0:1]
+    small_ref[1:2, :] = dot(ones, gpacked_t[2], 1, 1)[0:1]
+
+    def small_copy(turn, device):
+        return remote(
+            small_ref, small_in.at[turn], v_send.at[turn], v_recv.at[turn], device
+        )
+
+    def small_add(turn):
+        small_ref[...] += small_in[turn]
+
+    small_copy(0, place.in_plane(1)).start()
+    grad_in = grad_resid[...]
+    for j in range(3):
+        grad_in = grad_in + dot(gpacked_t[j], we[:, j * width : (j + 1) * width], 0, 1)
+    for s in range(seqs):
+        dx_ref[s] = grad_in[s * tokens : (s + 1) * tokens].astype(bfloat)
+    small_copy(0, place.in_plane(1)).wait()
+    small_add(0)
+    small_copy(1, place.in_plane(2)).start()
+    ahead((entry_unit, 0), (inner_unit, 6), (out_unit, 6), (outer_unit, 7))
+    small_copy(1, place.in_plane(2)).wait()
+    small_add(1)
+    small_copy(2, place.in_plane(4)).start()
+    ahead((entry_unit, 1), (inner_unit, 7), (out_unit, 7))
+    small_copy(2, place.in_plane(4)).wait()
+    small_add(2)
+
+    def small_column(offset):
+        return small_copy(2 + offset, place.in_column(offset))
+
+    for offset in range(1, groups):
+        small_column(offset).start()
+    ahead((entry_unit, 2), (entry_unit, 3))
+    for offset in range(1, groups):
+        small_column(offset).wait()
+    sum_small = jnp.zeros(small_ref.shape, single)
+    mine = small_ref[...]
+    for source in range(groups):
+        value = jnp.zeros(small_ref.shape, single)
+        for offset in range(groups):
+            term = mine if offset == 0 else small_in[2 + offset]
+            value = value + jnp.where((place.z + groups - offset) % groups == source, term, 0.0)
+        sum_small = sum_small + value
+    small_ref[...] = sum_small
+    ahead((entry_unit, 4), (entry_unit, 5), (entry_unit, 6), (entry_unit, 7))
+    for unit in (outer_unit, inner_unit, out_unit, entry_unit):
+        result_copy(unit).wait()
+    for s in range(seqs):
+        sent(lambda other: send_qkv.at[s, other], a_send, a_recv, s)
+        sent(lambda other: out_low.at[s, :, lanes_of(other)], o_send, o_recv, s)
+        sent(lambda other: gatt_t.at[head_rows_of(other), seq_lanes(s)], d_send, d_recv, s)
+        for k in range(1, 8):
+            for copy in pack_copies(s, k):
+                copy.wait_send()
+
+
+def widen_kernel(sums_ref, small_ref, *outs):
+    entry, query_b, value_b, out_w, out_b, gain1, shift1, inner_w, inner_b, outer_w, outer_b, gain2, shift2 = outs
+    step = pl.program_id(0)
+    tiles = outer_w.shape[0], inner_w.shape[1]
+    del tiles
+    value = jnp.concatenate([sums_ref[0], sums_ref[1]], axis=1).astype(single)
+
+    @pl.when(step < 4)
+    def _():
+        outer_w[...] = value
+
+    @pl.when((step >= 4) & (step < 8))
+    def _():
+        inner_w[...] = value
+
+    @pl.when(step == 8)
+    def _():
+        out_w[...] = value
+
+    @pl.when(step > 8)
+    def _():
+        entry[...] = value
+
+    @pl.when(step == 0)
+    def _():
+        def row(at):
+            return small_ref[at : at + 1, :].reshape(WIDE)
+
+        for ref, at in (
+            (query_b, 0),
+            (value_b, 1),
+            (out_b, 2),
+            (gain1, 3),
+            (shift1, 4),
+            (outer_b, 9),
+            (gain2, 10),
+            (shift2, 11),
+        ):
+            ref[...] = row(at)
+        for j in range(inner_b.shape[0] // WIDE):
+            inner_b[j * WIDE : (j + 1) * WIDE] = row(5 + j)
+
+
+def by_heads(groups, cut=None):
+    def run(inputs, blocks, we, qb, vb, wo, bo, g1, s1, w1, b1, w2, b2, g2, s2, cot):
+        seqs, tokens, width = inputs.shape
+        ff = w1.shape[1]
+        rows = seqs * tokens
+        length = tokens * HEADS
+        grad_rows = 2 * ff + 4 * width
+        vmem = pl.BlockSpec(memory_space=pltpu.VMEM)
+        smem = pl.BlockSpec(memory_space=pltpu.SMEM)
+        hbm = pl.BlockSpec(memory_space=pl.ANY)
+        dma = pltpu.SemaphoreType.DMA
+        out, dx, sums, small = pl.pallas_call(
+            partial(layer_kernel, groups, cut),
+            out_shape=[
+                jax.ShapeDtypeStruct(inputs.shape, bfloat),
+                jax.ShapeDtypeStruct(inputs.shape, bfloat),
+                jax.ShapeDtypeStruct((2, grad_rows, PIECE), bfloat),
+                jax.ShapeDtypeStruct((16, width), single),
+            ],
+            in_specs=[
+                vmem, smem, hbm, vmem, vmem, hbm, vmem, vmem, vmem, hbm, vmem, hbm, vmem, vmem,
+                vmem, hbm,
+            ],
+            out_specs=[vmem, vmem, hbm, vmem],
+            scratch_shapes=[
+                pltpu.VMEM(we.shape, bfloat),
+                pltpu.VMEM(wo.shape, bfloat),
+                pltpu.VMEM(w1.shape, bfloat),
+                pltpu.VMEM(w2.shape, bfloat),
+                pltpu.VMEM(cot.shape, bfloat),
+                dma((5,)),
+                pltpu.VMEM((seqs, HEADS, 3 * HEAD + 16, tokens), bfloat),
+                pltpu.VMEM((seqs, 3 * HEAD + 16, length), bfloat),
+                pltpu.VMEM((seqs, length, HEAD), bfloat),
+                pltpu.VMEM((seqs, length, HEAD), bfloat),
+                pltpu.VMEM((seqs, length, length), bfloat),
+                pltpu.VMEM((seqs, 1, length), single),
+                pltpu.VMEM((seqs, HEAD, length), single),
+                pltpu.VMEM((seqs, HEAD, length), bfloat),
+                pltpu.VMEM((width, rows), bfloat),
+                pltpu.VMEM((rows, width), single),
+                pltpu.VMEM((rows, 1), single),
+                pltpu.VMEM((rows, width), bfloat),
+                pltpu.VMEM((rows, ff), bfloat),
+                pltpu.VMEM((tokens, ff), single),
+                pltpu.VMEM((rows, ff), bfloat),
+                pltpu.VMEM((rows, width), bfloat),
+                pltpu.VMEM((rows, width), single),
+                pltpu.VMEM((rows, width), bfloat),
+                pltpu.VMEM((width, rows), bfloat),
+                pltpu.VMEM((seqs, HEAD, length), bfloat),
+                pltpu.VMEM((seqs, 3 * HEAD, length), bfloat),
+                pltpu.VMEM((HEAD, length), single),
+                pltpu.VMEM((HEAD, length), single),
+                pltpu.VMEM((3, width, rows), bfloat),
+                pltpu.VMEM((width, rows), bfloat),
+                pltpu.VMEM((2, grad_rows, PIECE), bfloat),
+                pltpu.VMEM((2, grad_rows // 2, PIECE), bfloat),
+                pltpu.VMEM((2, grad_rows // 4, PIECE), bfloat),
+                pltpu.VMEM((2, grad_rows // 8, PIECE), bfloat),
+                pltpu.VMEM((max(groups - 1, 1), 2, grad_rows // (8 * groups), PIECE), bfloat),
+                pltpu.VMEM((2, grad_rows, PIECE), bfloat),
+                pltpu.VMEM((3 + groups, 16, width), single),
+                dma((seqs, 8)),
+                dma((seqs, 8)),
+                dma((seqs, 8)),
+                dma((seqs, 8)),
+                dma((seqs, 8)),
+                dma((seqs, 8)),
+                dma((seqs, 8, 3)),
+                dma((seqs, 8, 3)),
+                dma((4, 6, 2)),
+                dma((4, 6, 2)),
+                dma((4, 2, max(groups - 1, 1), 2)),
+                dma((4, 2, max(groups - 1, 1), 2)),
+                dma((3 + groups,)),
+                dma((3 + groups,)),
+                dma((4,)),
+            ],
+            compiler_params=pltpu.CompilerParams(
+                collective_id=0, has_side_effects=True, vmem_limit_bytes=60 * 2**20
+            ),
+            name="layer",
+        )(inputs, blocks, we, qb, vb, wo, bo, g1, s1, w1, b1, w2, b2, g2, s2, cot)
+
+        def flat(size):
+            return pl.BlockSpec((size,), lambda i: (0,))
+
+        def shape(*dims):
+            return jax.ShapeDtypeStruct(dims, single)
+
+        tile = (WIDE, WIDE)
+        grads = pl.pallas_call(
+            widen_kernel,
+            grid=(grad_rows // WIDE,),
+            in_specs=[
+                pl.BlockSpec((2, WIDE, PIECE), lambda i: (0, i, 0)),
+                pl.BlockSpec((16, width), lambda i: (0, 0)),
+            ],
+            out_specs=[
+                pl.BlockSpec(tile, lambda i: (0, jnp.clip(i - 9, 0, 2))),
+                flat(width),
+                flat(width),
+                pl.BlockSpec(tile, lambda i: (0, 0)),
+                flat(width),
+                flat(width),
+                flat(width),
+                pl.BlockSpec(tile, lambda i: (0, jnp.clip(i - 4, 0, 3))),
+                flat(ff),
+                pl.BlockSpec(tile, lambda i: (jnp.clip(i, 0, 3), 0)),
+                flat(width),
+                flat(width),
+                flat(width),
+            ],
+            out_shape=[
+                shape(width, 3 * width),
+                shape(width),
+                shape(width),
+                shape(width, width),
+                shape(width),
+                shape(width),
+                shape(width),
+                shape(width, ff),
+                shape(ff),
+                shape(ff, width),
+                shape(width),
+                shape(width),
+                shape(width),
+            ],
+            name="widen",
+        )(sums, small)
+        return (out, dx, *grads)
+
+    return run
+
+
 def solution(mesh):
     in_specs = (
         P("dp", "seq", None),
@@ -493,6 +1376,8 @@
         P(),
         P(),
     )
+    heads_fit = mesh.shape["seq"] == HEADS
+    plan = by_heads(mesh.shape["dp"]) if heads_fit else on_device
     return jax.shard_map(
-        on_device, mesh=mesh, in_specs=in_specs, out_specs=out_specs, check_vma=False
-    )
+        plan, mesh=mesh, in_specs=in_specs, out_specs=out_specs, check_vma=False
+    )

time: 873 us -> 163 us (0.19); the launches traced: 861 us -> 163 us
  waiting for transfers between devices: 315 us -> 0 us
  local copies, waits for them, and re-layouts: 228 us -> 2.91 us
  Pallas kernels: 0 us -> 159 us
  other arithmetic: 108 us -> 0 us
  blocking collectives: 88.4 us -> 0 us
  matrix products: 82.8 us -> 0 us
  starting transfers between devices: 23.1 us -> 0 us
  between operations: 15.2 us -> 0.67 us
    psum x4 -> x0, waiting for transfers between devices: 315 us -> none  [the longest x1 187 us: on_device(): lax.psum((entry_weight_grad, query_bias_grad, value_bias_grad, out_weight...]
    pallas_call x0 -> x2, Pallas kernels: none -> 159 us  [the longest x1 147 us: run(): pl.pallas_call(partial(layer_kernel, groups, cut), out_shape=[jax.ShapeDt...]
    dot_general x24 -> x0, matrix products: 82.8 us -> none  [the longest x1 9.39 us: on_device(): jnp.einsum('shiqk,shikd->shiqd', prob_low, value_part, preferred_element_...]
    psum x2 -> x0, blocking collectives: 69.2 us -> none  [the longest x1 41.4 us: on_device(): lax.psum((entry_weight_grad, query_bias_grad, value_bias_grad, out_weight...]
    reshape x22 -> x0, local copies, waits for them, and re-layouts: 62.8 us -> none  [the longest x4 17.4 us: pair_blocks(): row_data.reshape(seq_count, length_here // block_rows, block_rows, 2, hea...]
    add x19 -> x0, other arithmetic: 30.6 us -> none  [the longest x7 22.7 us: merge_parts(): out_one * factor_one[..., None] + out_two * factor_two[..., None]]
    transpose x6 -> x0, local copies, waits for them, and re-layouts: 26.7 us -> none  [the longest x3 18.1 us: pair_tokens(): shaped.transpose(0, 2, 3, 4, 1, 5)]
    scatter x2 -> x0, local copies, waits for them, and re-layouts: 22.8 us -> none  [the longest x1 21.7 us: on_device(): outgoing = jnp.zeros((devices * capacity, block_rows, 2 * head_width), si...]
  transfers between devices with their start and end apart: 12 -> 0, of which waited for: 4 -> 0; matrix products, arithmetic and copies ran while one was open for 17% -> 0% of each run, Pallas kernels for 0% -> 0%
where the time goes in v1:
time: 163 us
  Pallas kernels  159 us (98%)
  local copies, waits for them, and re-layouts  2.91 us (2%)
    pallas_call x1, Pallas kernels, run(): pl.pallas_call(partial(layer_kernel, groups, cut), out_shape=[jax.ShapeDt...  147 us
    pallas_call x1, Pallas kernels, run(): pl.pallas_call(widen_kernel, grid=(grad_rows // WIDE,), in_specs=[pl.Bloc...  12.1 us

profile of v1, /device:TPU:0, one launch (start us, length us, event | category | flops | bytes accessed | tf_op | source)
XLA Modules:
  0.0 162.9 jit_solution(17286453740602237975)
XLA Ops:
  0.6 1.4 copy.31.blocks_ref
  2.1 147.2 %layer.1 = (bf16[3,128,512]{2,1,0:T(8,128)(2,1)}, bf16[3,128,512]{2,1,0:T(8,128)(2,1)}, bf16[2,6144,256]{2,1,0:T(8,128)(2,1)}, f32[16,512]{1,0:T(8,128)}) custom-call(bf16[3,128,512]{2,1,0:T(8,128)(2,1)} %x_ref.1, s32[3,8,2,3]{3,2,1,0:T(2,128)} %copy.31.blocks_ref, bf16[512,1536]{1,0:T(8,128)(2,1)} %we_hbm.1, bf16[512]{0:T(512)(128)(2,1)} %qb_ref.1, ...), custom_call_target="tpu_custom_call" | custom-call | tf_op jit(solution)/shard_map/layer/pallas_call | solution.py:1218
  149.3 0.0 copy-start.1
  149.3 0.0 copy-start
  149.3 12.1 %widen.1 = (f32[512,1536]{1,0:T(8,128)}, f32[512]{0:T(512)}, f32[512]{0:T(512)}, f32[512,512]{1,0:T(8,128)}, f32[512]{0:T(512)}, /*index=5*/f32[512]{0:T(512)}, ...) custom-call(bf16[2,6144,256]{2,1,0:T(8,128)(2,1)} %get-tuple-element, ...), custom_call_target="tpu_custom_call" | custom-call | tf_op jit(solution)/shard_map/widen/pallas_call | solution.py:1299
  161.4 0.0 copy-done.1
  161.4 0.7 copy.34
  162.2 0.0 copy-done
  162.2 0.7 copy.35
Async XLA Ops:
  149.3 12.1 %copy-start.1 = (bf16[3,128,512]{2,1,0:T(8,128)(2,1)S(1)}, bf16[3,128,512]{2,1,0:T(8,128)(2,1)}, u32[]{:S(2)}) copy-start(bf16[3,128,512]{2,1,0:T(8,128)(2,1)} %get-tuple-element.64) | copy-start | bytes 1179652
  149.3 12.9 %copy-start = (bf16[3,128,512]{2,1,0:T(8,128)(2,1)S(1)}, bf16[3,128,512]{2,1,0:T(8,128)(2,1)}, u32[]{:S(2)}) copy-start(bf16[3,128,512]{2,1,0:T(8,128)(2,1)} %get-tuple-element.65) | copy-start | bytes 1179652

commit v2 on v0

--- a/solution.py
+++ b/solution.py
@@ -3,6 +3,8 @@
 import jax
 import jax.numpy as jnp
 from jax import lax
+from jax.experimental import pallas as pl
+from jax.experimental.pallas import tpu as pltpu
 from jax.sharding import PartitionSpec as P
 
 HEADS = 8
@@ -457,6 +459,1151 @@
     )
 
 
+MESH = pl.DeviceIdType.MESH
+bfloat = jnp.bfloat16
+single = jnp.float32
+WIDE = 512
+QUERIES = 256
+INV_SQRT2 = 0.7071067811865476
+INV_SQRT_2PI = 0.3989422804014327
+
+
+def dot(a, b, a_dim, b_dim):
+    return lax.dot_general(
+        a, b, (((a_dim,), (b_dim,)), ((), ())), preferred_element_type=single
+    )
+
+
+def aligned(index, step):
+    return pl.multiple_of(index, step)
+
+
+class Place:
+    def __init__(self, groups):
+        self.groups = groups
+        self.z = lax.axis_index("dp")
+        self.me = lax.axis_index("seq")
+        self.y = self.me // 4
+        self.x = (self.me // 2) % 2
+        self.core = self.me % 2
+
+    def peer(self, offset):
+        off_y, off_x, off_core = offset // 4, (offset // 2) % 2, offset % 2
+        return (
+            ((self.y + off_y) % 2) * 4
+            + ((self.x + off_x) % 2) * 2
+            + (self.core + off_core) % 2
+        )
+
+    def in_plane(self, offset):
+        return (self.z, self.peer(offset))
+
+    def in_column(self, offset):
+        return ((self.z + offset) % self.groups, self.me)
+
+
+def remote(src, dst, send, recv, device):
+    return pltpu.make_async_remote_copy(
+        src_ref=src,
+        dst_ref=dst,
+        send_sem=send,
+        recv_sem=recv,
+        device_id=device,
+        device_id_type=MESH,
+    )
+
+
+def layer_kernel(
+    groups,
+    units,
+    plan,
+    x_hbm,
+    blocks_ref,
+    we_hbm,
+    qb_hbm,
+    vb_hbm,
+    wo_hbm,
+    bo_hbm,
+    g1_hbm,
+    s1_hbm,
+    w1_hbm,
+    b1_hbm,
+    w2_hbm,
+    b2_hbm,
+    g2_hbm,
+    s2_hbm,
+    cot_hbm,
+    out_hbm,
+    dx_hbm,
+    sums_hbm,
+    entry_hbm,
+    small_hbm,
+    x_ref,
+    qb_ref,
+    vb_ref,
+    bo_ref,
+    g1_ref,
+    s1_ref,
+    b1_ref,
+    b2_ref,
+    g2_ref,
+    s2_ref,
+    out_ref,
+    dx_ref,
+    small_ref,
+    we,
+    wo,
+    w1,
+    w2,
+    cot,
+    load_sem,
+    wh_t,
+    xall,
+    ids_send,
+    ids_all,
+    ids,
+    qkv,
+    krow,
+    vrow,
+    probs,
+    inv_total,
+    out_wide,
+    out_low,
+    att_t,
+    hat1,
+    rstd1,
+    low1,
+    hidden,
+    slope,
+    grad_inner,
+    grad_outer,
+    grad_resid,
+    grad_branch,
+    gatt_t,
+    dout_t,
+    dqkv,
+    dk_acc,
+    dv_acc,
+    gpacked_t,
+    entry_acc,
+    entry_part,
+    entry_in,
+    part,
+    landed,
+    total,
+    small_in,
+    x_send,
+    x_recv,
+    i_send,
+    i_recv,
+    o_send,
+    o_recv,
+    d_send,
+    d_recv,
+    p_send,
+    p_recv,
+    rs_send,
+    rs_recv,
+    e_send,
+    e_recv,
+    v_send,
+    v_recv,
+    done_sem,
+    store_sem,
+):
+    seqs, tokens, width = x_ref.shape
+    place = Place(groups)
+    me = place.me
+    barrier = pltpu.get_barrier_semaphore()
+    for k in range(1, 8):
+        pl.semaphore_signal(
+            barrier, inc=1, device_id=place.in_plane(k), device_id_type=MESH
+        )
+    for k in range(1, groups):
+        pl.semaphore_signal(
+            barrier, inc=1, device_id=place.in_column(k), device_id_type=MESH
+        )
+    def load(*pairs):
+        copies = []
+        for src, dst in pairs:
+            copies.append(pltpu.make_async_copy(src, dst, load_sem.at[len(loads)]))
+            copies[-1].start()
+            loads.append(copies[-1])
+        return copies
+
+    loads = []
+    load_x = load((x_hbm, x_ref))
+    load_entry = load((we_hbm, we), (qb_hbm, qb_ref), (vb_hbm, vb_ref))
+    load_rest = load(
+        (wo_hbm, wo),
+        (bo_hbm, bo_ref),
+        (g1_hbm, g1_ref),
+        (s1_hbm, s1_ref),
+        (w1_hbm, w1),
+        (b1_hbm, b1_ref),
+        (w2_hbm, w2),
+        (b2_hbm, b2_ref),
+        (g2_hbm, g2_ref),
+        (s2_hbm, s2_ref),
+        (cot_hbm, cot),
+    )
+
+    def lanes_of(device):
+        return pl.ds(aligned(device * tokens, 128), tokens)
+
+    def head_rows_of(device):
+        return pl.ds(aligned(device * HEAD, HEAD), HEAD)
+
+    def seq_lanes(s):
+        return pl.ds(aligned(s * tokens, 128), tokens)
+
+    def vec(ref):
+        return ref[...].astype(single).reshape(1, ref.shape[0])
+
+    lane = lax.broadcasted_iota(jnp.int32, (16, tokens), 1)
+    row = lax.broadcasted_iota(jnp.int32, (16, tokens), 0)
+    for h in range(HEADS):
+        numbers = jnp.zeros((16, tokens), jnp.int32)
+        for s in range(seqs):
+            for j in range(3):
+                picked = jnp.where(
+                    lane < BLOCK, blocks_ref[s, j, 0, h], blocks_ref[s, j, 1, h]
+                )
+                numbers = jnp.where(row == s * 3 + j, picked, numbers)
+        ids_send[h] = numbers.astype(single).astype(bfloat)
+    small_ref[...] = jnp.zeros(small_ref.shape, single)
+    entry_acc[...] = jnp.zeros(entry_acc.shape, single)
+
+    load_x[0].wait()
+    pl.semaphore_wait(barrier, 7 + groups - 1)
+
+    def x_copy(s, k):
+        return remote(
+            x_ref.at[s],
+            xall.at[s, lanes_of(me), :],
+            x_send.at[s, k],
+            x_recv.at[s, k],
+            place.in_plane(k),
+        )
+
+    def x_forward(s, k):
+        slab = xall.at[s, lanes_of(place.peer(k)), :]
+        return remote(
+            slab, slab, x_send.at[s, k + 1], x_recv.at[s, k + 1], place.in_plane(1)
+        )
+
+    def x_arrived(s, k):
+        slab = xall.at[s, lanes_of(place.peer(k)), :]
+        remote(slab, slab, x_send.at[s, k], x_recv.at[s, k], place.in_plane(k)).wait_recv()
+
+    def ids_copy(k):
+        other = place.peer(k)
+        return remote(
+            ids_send.at[other],
+            ids_all.at[:, lanes_of(me)],
+            i_send.at[k],
+            i_recv.at[k],
+            place.in_plane(k),
+        )
+
+    for s in range(seqs):
+        for k in (6, 2, 4, 1):
+            x_copy(s, k).start()
+        if s == 0:
+            for k in range(1, 8):
+                ids_copy(k).start()
+    ids_all[:, lanes_of(me)] = ids_send[me]
+    for s in range(seqs):
+        xall[s, lanes_of(me), :] = x_ref[s]
+
+    for copy in load_entry:
+        copy.wait()
+    pair = me // 2
+    odd = me % 2
+    for j in range(3):
+        columns = we[:, pl.ds(aligned(j * width + pair * 2 * HEAD, 128), 2 * HEAD)].T
+        wh_t[j * HEAD : (j + 1) * HEAD, :] = jnp.where(
+            odd == 1, columns[HEAD:], columns[:HEAD]
+        )
+    spread = lax.broadcasted_iota(jnp.int32, (HEAD, width), 1) == me * HEAD + (
+        lax.broadcasted_iota(jnp.int32, (HEAD, width), 0)
+    )
+
+    def column(ref):
+        return jnp.sum(jnp.where(spread, vec(ref), 0.0), axis=1, keepdims=True)
+
+    query_column = column(qb_ref)
+    value_column = column(vb_ref)
+
+    def arrived_at(ref_of, send, recv, s):
+        for k in range(1, 8):
+            slot = ref_of(place.peer(k))
+            remote(slot, slot, send.at[s, k], recv.at[s, k], place.in_plane(k)).wait_recv()
+
+    def sent(ref_of, send, recv, s):
+        for k in range(1, 8):
+            slot = ref_of(place.peer(k))
+            remote(slot, slot, send.at[s, k], recv.at[s, k], place.in_plane(k)).wait_send()
+
+    for k in range(1, 8):
+        slot = ids_all.at[:, lanes_of(place.peer(k))]
+        remote(slot, slot, i_send.at[k], i_recv.at[k], place.in_plane(k)).wait_recv()
+    for s in range(seqs):
+        ids[s, 0:3, :] = ids_all[...].astype(single)[3 * s : 3 * s + 3]
+
+    length = qkv.shape[2]
+    chunks = length // QUERIES
+    blocks = length // BLOCK
+    key_block = lax.broadcasted_iota(jnp.int32, (blocks, QUERIES), 0)
+    query_lane = lax.broadcasted_iota(jnp.int32, (blocks, QUERIES), 1)
+
+    def out_copy(s, k):
+        return remote(
+            out_low.at[s, :, lanes_of(place.peer(k))],
+            att_t.at[head_rows_of(me), seq_lanes(s)],
+            o_send.at[s, k],
+            o_recv.at[s, k],
+            place.in_plane(k),
+        )
+
+    def project(s, k):
+        owner = place.peer(k)
+        packed = dot(wh_t[...], xall[s, lanes_of(owner), :], 1, 1)
+        qkv[s, 0:HEAD, lanes_of(owner)] = (
+            (packed[0:HEAD] + query_column) * HEAD**-0.5
+        ).astype(bfloat)
+        qkv[s, HEAD : 2 * HEAD, lanes_of(owner)] = packed[HEAD : 2 * HEAD].astype(bfloat)
+        qkv[s, 2 * HEAD :, lanes_of(owner)] = (packed[2 * HEAD :] + value_column).astype(bfloat)
+
+    def attend(s, _):
+        for k in (2, 4, 6):
+            x_arrived(s, k)
+            x_forward(s, k).start()
+        for k in (0, 2, 4, 6):
+            project(s, k)
+        for k in (1, 3, 5, 7):
+            x_arrived(s, k)
+            project(s, k)
+        krow[s] = qkv[s, HEAD : 2 * HEAD, :].T
+        vrow[s] = qkv[s, 2 * HEAD : 3 * HEAD, :].T
+
+        def chunk(i, _):
+            at = pl.ds(aligned(i * QUERIES, QUERIES), QUERIES)
+            query_block = (i * QUERIES + query_lane) // BLOCK
+            inside = (key_block >= 1) & (key_block <= blocks - 2)
+            near = (key_block >= query_block - 1) & (key_block <= query_block + 1) & inside
+            times = jnp.where(near, 1.0, 0.0) + jnp.where(inside, 0.0, 1.0)
+            for j in range(3):
+                times = times + jnp.where(
+                    ids[s, j : j + 1, at] == key_block.astype(single), 1.0, 0.0
+                )
+            bias = jnp.where(times > 1.5, 0.6931471805599453, 0.0)
+            bias = jnp.where(times > 0.5, bias, NEGATIVE)
+            bias = jnp.where((query_block == 0) | (query_block == blocks - 1), 0.0, bias)
+            score = jnp.dot(krow[s], qkv[s, 0:HEAD, at], preferred_element_type=single)
+            score = score.reshape(blocks, BLOCK, QUERIES) + bias[:, None, :]
+            score = score.reshape(length, QUERIES)
+            peak = jnp.max(score, axis=0, keepdims=True)
+            grown = jnp.exp(score - peak)
+            inverse = 1.0 / jnp.sum(grown, axis=0, keepdims=True)
+            grown = grown.astype(bfloat)
+            probs[s, :, at] = grown
+            inv_total[s, :, at] = inverse
+            result = inverse * jnp.dot(
+                qkv[s, 2 * HEAD :, :], grown, preferred_element_type=single
+            )
+            out_wide[s, :, at] = result
+            out_low[s, :, at] = result.astype(bfloat)
+            return 0
+
+        lax.fori_loop(0, chunks, chunk, 0)
+        for k in (6, 7, 2, 3, 4, 5, 1):
+            out_copy(s, k).start()
+        att_t[head_rows_of(me), seq_lanes(s)] = out_low[s, :, lanes_of(me)]
+        return 0
+
+    lax.fori_loop(0, seqs, attend, 0)
+    for copy in load_rest:
+        copy.wait()
+
+    def dout_copy(s, k):
+        return remote(
+            gatt_t.at[head_rows_of(place.peer(k)), seq_lanes(s)],
+            dout_t.at[s, :, lanes_of(me)],
+            d_send.at[s, k],
+            d_recv.at[s, k],
+            place.in_plane(k),
+        )
+
+    def mean_of(value):
+        return jnp.mean(value, axis=-1, keepdims=True)
+
+    def add_small(row, value):
+        small_ref[row : row + 1, :] += jnp.sum(value, axis=0, keepdims=True)
+
+    ff = hidden.shape[1]
+
+    def store(which, s):
+        src, dst = ((out_ref, out_hbm), (dx_ref, dx_hbm))[which]
+        return pltpu.make_async_copy(src.at[s], dst.at[s], store_sem.at[which, s])
+
+    def forward(s, _):
+        arrived_at(lambda other: att_t.at[head_rows_of(other), seq_lanes(s)], o_send, o_recv, s)
+        here = seq_lanes(s)
+        branch = dot(att_t[:, here], wo[...], 0, 0) + vec(bo_ref)
+        resid = x_ref[s].astype(single) + branch
+        center = resid - mean_of(resid)
+        scale1 = lax.rsqrt(mean_of(center * center) + EPSILON)
+        normed1 = center * scale1
+        hat1[here, :] = normed1
+        rstd1[here, :] = scale1
+        first = normed1 * vec(g1_ref) + vec(s1_ref)
+        first_low = first.astype(bfloat)
+        low1[here, :] = first_low
+        second = first + vec(b2_ref)
+        bias1 = vec(b1_ref)
+        for j in range(ff // WIDE):
+            span = slice(j * WIDE, (j + 1) * WIDE)
+            pre = jnp.dot(first_low, w1[:, span], preferred_element_type=single) + bias1[:, span]
+            share = 0.5 * (1.0 + lax.erf(pre * INV_SQRT2))
+            active = (pre * share).astype(bfloat)
+            hidden[here, span] = active
+            slope[here, span] = share + pre * jnp.exp(-0.5 * pre * pre) * INV_SQRT_2PI
+            second = second + jnp.dot(active, w2[span, :], preferred_element_type=single)
+        center = second - mean_of(second)
+        scale2 = lax.rsqrt(mean_of(center * center) + EPSILON)
+        normed2 = center * scale2
+        out_ref[s] = (normed2 * vec(g2_ref) + vec(s2_ref)).astype(bfloat)
+        store(0, s).start()
+        incoming = cot[s].astype(single)
+        add_small(10, incoming * normed2)
+        add_small(11, incoming)
+        scaled = incoming * vec(g2_ref)
+        grad_second = scale2 * (
+            scaled - mean_of(scaled) - normed2 * mean_of(scaled * normed2)
+        )
+        grad_resid[here, :] = grad_second
+        grad_low = grad_second.astype(bfloat)
+        grad_outer[here, :] = grad_low
+        add_small(9, grad_low.astype(single))
+        return 0
+
+    lax.fori_loop(0, seqs, forward, 0)
+
+    def stages_of(unit):
+        base, count, order = units[unit]
+        size = count // 2
+        start = base + place.core * size
+        stages = [("c", start, base + (1 - place.core) * size, size)]
+        for axis in order:
+            if axis == "z":
+                size = size // groups
+                stages.append((axis, start + place.z * size, start, size))
+                start = start + place.z * size
+            else:
+                size = size // 2
+                index = place.x if axis == "x" else place.y
+                stages.append((axis, start + index * size, start + (1 - index) * size, size))
+                start = start + index * size
+        return stages
+
+    hops = {"c": 1, "x": 2, "y": 4}
+
+    def rows_at(start, count):
+        return pl.ds(aligned(start, 16), count)
+
+    def landing(unit, stage):
+        before = 0
+        for other in range(unit):
+            before += units[other][1]
+        for earlier in range(stage):
+            axis, _, _, size = stages_of(unit)[earlier]
+            before += size * (groups - 1 if axis == "z" else 1)
+        return before
+
+    def reduce_copies(unit, stage):
+        axis, _, away, size = stages_of(unit)[stage]
+        at = landing(unit, stage)
+        if axis != "z":
+            return [
+                remote(
+                    part.at[rows_at(away, size), :],
+                    landed.at[at : at + size, :],
+                    rs_send.at[unit, stage, 0],
+                    rs_recv.at[unit, stage, 0],
+                    place.in_plane(hops[axis]),
+                )
+            ]
+        return [
+            remote(
+                part.at[rows_at(away + ((place.z + offset) % groups) * size, size), :],
+                landed.at[at + (offset - 1) * size : at + offset * size, :],
+                rs_send.at[unit, stage, offset - 1],
+                rs_recv.at[unit, stage, offset - 1],
+                place.in_column(offset),
+            )
+            for offset in range(1, groups)
+        ]
+
+    def reduce_start(unit, stage):
+        for copy in reduce_copies(unit, stage):
+            copy.start()
+
+    def reduce_finish(unit, stage):
+        copies = reduce_copies(unit, stage)
+        for copy in copies:
+            copy.wait()
+        _, keep, _, size = stages_of(unit)[stage]
+        at = landing(unit, stage)
+        result = total if stage == 3 else part
+        tile = next(rows for rows in (64, 32, 16) if size % rows == 0)
+
+        def add(i, _):
+            mine = rows_at(keep + i * tile, tile)
+            value = part[mine, :].astype(single)
+            for j in range(len(copies)):
+                value = value + landed[rows_at(at + j * size + i * tile, tile), :].astype(single)
+            result[mine, :] = value.astype(bfloat)
+            return 0
+
+        lax.fori_loop(0, size // tile, add, 0)
+
+    def gather_copies(unit, stage, arriving):
+        axis, keep, away, size = stages_of(unit)[stage]
+        if axis != "z":
+            slot = total.at[rows_at(away if arriving else keep, size), :]
+            return [
+                remote(
+                    slot,
+                    slot,
+                    rs_send.at[unit, 4 + stage, 0],
+                    rs_recv.at[unit, 4 + stage, 0],
+                    place.in_plane(hops[axis]),
+                )
+            ]
+        copies = []
+        for offset in range(1, groups):
+            owner = (place.z + groups - offset) % groups
+            slot = total.at[rows_at(away + owner * size if arriving else keep, size), :]
+            copies.append(
+                remote(
+                    slot,
+                    slot,
+                    rs_send.at[unit, 4 + stage, offset - 1],
+                    rs_recv.at[unit, 4 + stage, offset - 1],
+                    place.in_column(offset),
+                )
+            )
+        return copies
+
+    def gather_start(unit, stage):
+        for copy in gather_copies(unit, stage, False):
+            copy.start()
+
+    def gather_finish(unit, stage):
+        for copy in gather_copies(unit, stage, False):
+            copy.wait_send()
+        for copy in gather_copies(unit, stage, True):
+            copy.wait_recv()
+
+    def result_copy(unit):
+        base, count, _ = units[unit]
+        at = pl.ds(base, count)
+        return pltpu.make_async_copy(total.at[at, :], sums_hbm.at[at, :], done_sem.at[unit])
+
+    def step(unit, stage):
+        if stage < 3:
+            reduce_finish(unit, stage)
+            reduce_start(unit, stage + 1)
+        elif stage == 3:
+            reduce_finish(unit, stage)
+            gather_start(unit, 3)
+        elif stage < 7:
+            gather_finish(unit, 7 - stage)
+            gather_start(unit, 6 - stage)
+        else:
+            gather_finish(unit, 0)
+            result_copy(unit).start()
+
+    def ready_units(j, tile):
+        for unit, (base, count, _) in enumerate(units):
+            last = (base + count) // WIDE - 1
+            if last in tile:
+
+                @pl.when(j == last - tile[0])
+                def _():
+                    reduce_start(unit, 0)
+
+    def steps_at(name, index):
+        for at, unit, stage in plan[name]:
+
+            @pl.when(index == at)
+            def _():
+                step(unit, stage)
+
+    def keep_part(base, value):
+        part[pl.ds(aligned(base, 128), value.shape[0]), :] = value.astype(bfloat)
+
+    outer_tiles = range(0, ff // WIDE)
+    inner_tiles = range(ff // WIDE, 2 * ff // WIDE)
+
+    def outer_tile(j, _):
+        at = pl.ds(aligned(j * WIDE, WIDE), WIDE)
+        keep_part(j * WIDE, dot(hidden[:, at], grad_outer[...], 0, 0))
+        ready_units(j, outer_tiles)
+        return 0
+
+    def inner_tile(j, _):
+        at = pl.ds(aligned(j * WIDE, WIDE), WIDE)
+        keep_part(ff + j * WIDE, dot(low1[...], grad_inner[:, at], 0, 0))
+        ready_units(j, inner_tiles)
+        steps_at("inner", j)
+        return 0
+
+    lax.fori_loop(0, ff // WIDE, outer_tile, 0)
+
+    def backward(s, _):
+        here = seq_lanes(s)
+        back = grad_resid[here, :]
+        grad_low = grad_outer[here, :]
+        for j in range(ff // WIDE):
+            span = slice(j * WIDE, (j + 1) * WIDE)
+            grad_hidden = dot(grad_low, w2[span, :], 1, 1)
+            inner = (grad_hidden * slope[here, span]).astype(bfloat)
+            grad_inner[here, span] = inner
+            add_small(5 + j, inner.astype(single))
+            back = back + dot(inner, w1[:, span], 1, 1)
+        normed1 = hat1[here, :]
+        add_small(3, back * normed1)
+        add_small(4, back)
+        scaled = back * vec(g1_ref)
+        grad = rstd1[here, :] * (scaled - mean_of(scaled) - normed1 * mean_of(scaled * normed1))
+        grad_resid[here, :] = grad
+        grad = grad.astype(bfloat)
+        grad_branch[here, :] = grad
+        add_small(2, grad.astype(single))
+        gatt_t[:, here] = dot(wo[...], grad, 1, 1).astype(bfloat)
+        for k in (6, 7, 2, 3, 4, 5, 1):
+            dout_copy(s, k).start()
+        dout_t[s, :, lanes_of(me)] = gatt_t[head_rows_of(me), seq_lanes(s)]
+        steps_at("backward", s)
+        return 0
+
+    lax.fori_loop(0, seqs, backward, 0)
+    lax.fori_loop(0, ff // WIDE, inner_tile, 0)
+    keep_part(2 * ff, jnp.dot(att_t[...], grad_branch[...], preferred_element_type=single))
+    ready_units(0, (2 * ff // WIDE,))
+    steps_at("inner", ff // WIDE)
+
+    def pack_copies(s, k):
+        other = place.peer(k)
+        return [
+            remote(
+                dqkv.at[s, j * HEAD : (j + 1) * HEAD, lanes_of(other)],
+                gpacked_t.at[j, head_rows_of(me), seq_lanes(s)],
+                p_send.at[s, k, j],
+                p_recv.at[s, k, j],
+                place.in_plane(k),
+            )
+            for j in range(3)
+        ]
+
+    def back_chunk(turn, _):
+        s = turn // chunks
+        i = turn % chunks
+
+        @pl.when(i == 0)
+        def _():
+            arrived_at(lambda other: dout_t.at[s, :, lanes_of(other)], d_send, d_recv, s)
+            dk_acc[...] = jnp.zeros(dk_acc.shape, single)
+            dv_acc[...] = jnp.zeros(dv_acc.shape, single)
+
+        at = pl.ds(aligned(i * QUERIES, QUERIES), QUERIES)
+        cot_t = dout_t[s, :, at].astype(single)
+        inverse = inv_total[s, :, at]
+        delta = inverse * jnp.sum(cot_t * out_wide[s, :, at], axis=0, keepdims=True)
+        cot_low = (cot_t * inverse).astype(bfloat)
+        grown = probs[s, :, at]
+        grad = jnp.dot(vrow[s], cot_low, preferred_element_type=single) - delta
+        grad = (grown.astype(single) * grad).astype(bfloat)
+        query_grad = jnp.dot(qkv[s, HEAD : 2 * HEAD, :], grad, preferred_element_type=single)
+        dqkv[s, 0:HEAD, at] = (query_grad.astype(bfloat) * HEAD**-0.5).astype(bfloat)
+        dv_acc[...] += dot(cot_low, grown, 1, 1)
+        dk_acc[...] += dot(qkv[s, 0:HEAD, at], grad, 1, 1)
+
+        @pl.when(i == chunks - 1)
+        def _():
+            dqkv[s, HEAD : 2 * HEAD, :] = dk_acc[...].astype(bfloat)
+            dqkv[s, 2 * HEAD :, :] = dv_acc[...].astype(bfloat)
+            for k in (6, 7, 2, 3, 4, 5, 1):
+                for copy in pack_copies(s, k):
+                    copy.start()
+            for j in range(3):
+                gpacked_t[j, head_rows_of(me), seq_lanes(s)] = dqkv[
+                    s, j * HEAD : (j + 1) * HEAD, lanes_of(me)
+                ]
+            entry_acc[...] += jnp.dot(dqkv[s], xall[s], preferred_element_type=single)
+
+        steps_at("attention", turn)
+        return 0
+
+    lax.fori_loop(0, seqs * chunks, back_chunk, 0)
+
+    entry_base = 2 * ff + width
+    head_share = 3 * HEAD
+    fourth = head_share // groups
+
+    def entry_rows(device, z=None):
+        start = entry_base + device * head_share
+        if z is None:
+            return rows_at(start, head_share)
+        return rows_at(start + z * fourth, fourth)
+
+    def entry_copy(offset):
+        target = (place.z + offset) % groups
+        return remote(
+            entry_part.at[rows_at(target * fourth, fourth), :],
+            entry_in.at[offset - 1],
+            e_send.at[0, offset],
+            e_recv.at[0, offset],
+            place.in_column(offset),
+        )
+
+    def entry_back(offset, arriving):
+        owner = (place.z + groups - offset) % groups if arriving else place.z
+        slot = total.at[entry_rows(me, owner), :]
+        return remote(slot, slot, e_send.at[1, offset], e_recv.at[1, offset], place.in_column(offset))
+
+    def entry_plane(k, owner, to):
+        slot = total.at[entry_rows(owner), :]
+        return remote(slot, slot, e_send.at[2, k], e_recv.at[2, k], place.in_plane(to))
+
+    def entry_result():
+        rows = pl.ds(entry_base, HEADS * head_share)
+        return pltpu.make_async_copy(total.at[rows, :], entry_hbm, done_sem.at[len(units)])
+
+    def entry_step(stage):
+        if stage == 0:
+            entry_part[...] = entry_acc[...].astype(bfloat)
+            for offset in range(1, groups):
+                entry_copy(offset).start()
+        elif stage == 1:
+            value = entry_part[rows_at(place.z * fourth, fourth), :].astype(single)
+            for offset in range(1, groups):
+                entry_copy(offset).wait()
+                value = value + entry_in[offset - 1].astype(single)
+            total[entry_rows(me, place.z), :] = value.astype(bfloat)
+            for offset in range(1, groups):
+                entry_back(offset, False).start()
+        elif stage == 2:
+            for offset in range(1, groups):
+                entry_back(offset, False).wait_send()
+                entry_back(offset, True).wait_recv()
+            for k in (6, 2, 4, 1):
+                entry_plane(k, me, k).start()
+        elif stage == 3:
+            for k in (2, 4, 6):
+                entry_plane(k, place.peer(k), k).wait_recv()
+                entry_plane(k + 1, place.peer(k), 1).start()
+        else:
+            for k in (1, 3, 5, 7):
+                entry_plane(k, place.peer(k), 1).wait_recv()
+            for k in (1, 2, 4, 6):
+                entry_plane(k, me, k).wait_send()
+            for k in (3, 5, 7):
+                entry_plane(k, place.peer(k - 1), 1).wait_send()
+            entry_result().start()
+
+    def small_copy(turn, device):
+        return remote(
+            small_ref, small_in.at[turn], v_send.at[turn], v_recv.at[turn], device
+        )
+
+    def small_column(offset):
+        return small_copy(2 + offset, place.in_column(offset))
+
+    def small_step(stage):
+        if stage == 0:
+            ones = jnp.ones((8, length), bfloat)
+            sums = jnp.zeros((8, head_share), single)
+            for s in range(seqs):
+                sums = sums + dot(ones, dqkv[s], 1, 1)
+            here = lax.broadcasted_iota(jnp.int32, (1, width), 1) // HEAD == me
+            for at, start in ((0, 0), (1, 2 * HEAD)):
+                wide = jnp.concatenate([sums[0:1, start : start + HEAD]] * HEADS, axis=1)
+                small_ref[at : at + 1, :] = jnp.where(here, wide, 0.0)
+            small_copy(0, place.in_plane(1)).start()
+        elif stage < 3:
+            small_copy(stage - 1, place.in_plane(2 ** (stage - 1))).wait()
+            small_ref[...] += small_in[stage - 1]
+            small_copy(stage, place.in_plane(2**stage)).start()
+        elif stage == 3:
+            small_copy(2, place.in_plane(4)).wait()
+            small_ref[...] += small_in[2]
+            for offset in range(1, groups):
+                small_column(offset).start()
+        else:
+            for offset in range(1, groups):
+                small_column(offset).wait()
+            mine = small_ref[...]
+            sum_small = jnp.zeros(small_ref.shape, single)
+            for source in range(groups):
+                for offset in range(groups):
+                    term = mine if offset == 0 else small_in[2 + offset]
+                    sum_small = sum_small + jnp.where(
+                        (place.z + groups - offset) % groups == source, term, 0.0
+                    )
+            small_ref[...] = sum_small
+            small_store.start()
+
+    small_store = pltpu.make_async_copy(small_ref, small_hbm, store_sem.at[2, 0])
+
+    def input_step():
+        for s in range(seqs):
+            for k in range(1, 8):
+                other = place.peer(k)
+                for j in range(3):
+                    slot = gpacked_t.at[j, head_rows_of(other), seq_lanes(s)]
+                    remote(
+                        slot, slot, p_send.at[s, k, j], p_recv.at[s, k, j], place.in_plane(k)
+                    ).wait_recv()
+        grad_in = grad_resid[...]
+        for j in range(3):
+            grad_in = grad_in + dot(gpacked_t[j], we[:, j * width : (j + 1) * width], 0, 1)
+        for s in range(seqs):
+            dx_ref[s] = grad_in[s * tokens : (s + 1) * tokens].astype(bfloat)
+            store(1, s).start()
+
+    for kind, *what in plan["tail"]:
+        if kind == "unit":
+            step(*what)
+        elif kind == "entry":
+            entry_step(*what)
+        elif kind == "small":
+            small_step(*what)
+        else:
+            input_step()
+    for unit in range(len(units)):
+        result_copy(unit).wait()
+    entry_result().wait()
+    small_store.wait()
+    for s in range(seqs):
+        store(0, s).wait()
+        store(1, s).wait()
+        for k in (1, 2, 4, 6):
+            x_copy(s, k).wait_send()
+        for k in (2, 4, 6):
+            x_forward(s, k).wait_send()
+        sent(lambda other: out_low.at[s, :, lanes_of(other)], o_send, o_recv, s)
+        sent(lambda other: gatt_t.at[head_rows_of(other), seq_lanes(s)], d_send, d_recv, s)
+        for k in range(1, 8):
+            for copy in pack_copies(s, k):
+                copy.wait_send()
+    for k in range(1, 8):
+        ids_copy(k).wait_send()
+
+
+def widen_kernel(sums_hbm, entry_hbm, small_hbm, out_in, dx_in, *refs):
+    outs, vectors, scratch = refs[:15], refs[15:23], refs[23:]
+    sums, entry_low, small, passed, inner_bias, outer_v, inner_v, out_v, entry_v = scratch[:9]
+    in_sem, out_sem = scratch[9:]
+    out_ref, dx_ref, entry, query_b, value_b, out_w, out_b = outs[:7]
+    gain1, shift1, inner_w, inner_b, outer_w, outer_b, gain2, shift2 = outs[7:]
+    width = WIDE
+    ff = outer_w.shape[0]
+    pieces = sums.shape[0] // WIDE
+    reads = []
+    writes = []
+
+    def read(src, dst):
+        reads.append(pltpu.make_async_copy(src, dst, in_sem.at[len(reads)]))
+        reads[-1].start()
+
+    def write(src, dst):
+        writes.append(pltpu.make_async_copy(src, dst, out_sem.at[len(writes)]))
+        writes[-1].start()
+
+    for i in range(pieces):
+        rows = slice(i * WIDE, (i + 1) * WIDE)
+        read(sums_hbm.at[rows, :], sums.at[rows, :])
+    read(entry_hbm, entry_low)
+    read(small_hbm, small)
+    read(out_in, passed.at[0])
+    read(dx_in, passed.at[1])
+    for i in range(pieces):
+        reads[i].wait()
+        rows = slice(i * WIDE, (i + 1) * WIDE)
+        value = sums[rows, :].astype(single)
+        j = i - ff // WIDE
+        if j < 0:
+            outer_v[rows, :] = value
+            write(outer_v.at[rows], outer_w.at[rows])
+        elif j < ff // WIDE:
+            columns = slice(j * WIDE, (j + 1) * WIDE)
+            inner_v[:, columns] = value
+            write(inner_v.at[:, columns], inner_w.at[:, columns])
+        else:
+            out_v[...] = value
+            write(out_v, out_w)
+    reads[pieces].wait()
+    for j in range(3):
+        columns = slice(j * width, (j + 1) * width)
+        value = entry_low[:, j * HEAD : (j + 1) * HEAD, :].reshape(width, width)
+        entry_v[:, columns] = value.astype(single).T
+        write(entry_v.at[:, columns], entry.at[:, columns])
+    for read_done in reads[pieces + 1 :]:
+        read_done.wait()
+    write(passed.at[0], out_ref)
+    write(passed.at[1], dx_ref)
+
+    def small_row(at):
+        return small[at : at + 1, :].reshape(width)
+
+    for j, (ref, at) in enumerate(
+        (
+            (query_b, 0),
+            (value_b, 1),
+            (out_b, 2),
+            (gain1, 3),
+            (shift1, 4),
+            (outer_b, 9),
+            (gain2, 10),
+            (shift2, 11),
+        )
+    ):
+        vectors[j][...] = small_row(at)
+        write(vectors[j], ref)
+    for j in range(ff // WIDE):
+        inner_bias[j * WIDE : (j + 1) * WIDE] = small_row(5 + j)
+    write(inner_bias, inner_b)
+    for copy in writes:
+        copy.wait()
+
+
+UNITS = (
+    (0, 1024, "xyz"),
+    (1024, 1024, "yxz"),
+    (2048, 1024, "xyz"),
+    (3072, 1024, "zyx"),
+    (4096, 512, "xyz"),
+)
+PLAN = {
+    "backward": (
+        (0, 0, 0),
+        (0, 1, 0),
+    ),
+    "inner": (
+    ),
+    "attention": (
+        (0, 2, 0),
+        (0, 3, 0),
+        (0, 0, 1),
+        (0, 1, 1),
+        (0, 4, 0),
+        (3, 0, 2),
+        (5, 2, 1),
+        (6, 1, 2),
+        (8, 3, 1),
+        (8, 2, 2),
+        (8, 4, 1),
+        (9, 0, 3),
+        (11, 1, 3),
+        (11, 3, 2),
+    ),
+    "tail": (
+        ("entry", 0),
+        ("small", 0),
+        ("unit", 2, 3),
+        ("unit", 4, 2),
+        ("small", 1),
+        ("unit", 0, 4),
+        ("input",),
+        ("small", 2),
+        ("unit", 1, 4),
+        ("unit", 3, 3),
+        ("unit", 0, 5),
+        ("entry", 1),
+        ("small", 3),
+        ("unit", 1, 5),
+        ("unit", 2, 4),
+        ("unit", 3, 4),
+        ("unit", 4, 3),
+        ("entry", 2),
+        ("unit", 0, 6),
+        ("unit", 0, 7),
+        ("unit", 1, 6),
+        ("small", 4),
+        ("unit", 4, 4),
+        ("unit", 1, 7),
+        ("unit", 2, 5),
+        ("unit", 3, 5),
+        ("entry", 3),
+        ("unit", 4, 5),
+        ("unit", 2, 6),
+        ("entry", 4),
+        ("unit", 2, 7),
+        ("unit", 3, 6),
+        ("unit", 4, 6),
+        ("unit", 3, 7),
+        ("unit", 4, 7),
+    ),
+}
+
+
+def by_heads(groups):
+    def run(inputs, blocks, we, qb, vb, wo, bo, g1, s1, w1, b1, w2, b2, g2, s2, cot):
+        seqs, tokens, width = inputs.shape
+        ff = w1.shape[1]
+        rows = seqs * tokens
+        length = tokens * HEADS
+        grad_rows = 2 * ff + width
+        units = UNITS
+        others = max(groups - 1, 1)
+        head_share = 3 * HEAD
+        smem = pl.BlockSpec(memory_space=pltpu.SMEM)
+        hbm = pl.BlockSpec(memory_space=pl.ANY)
+        dma = pltpu.SemaphoreType.DMA
+
+        def shape(*dims):
+            return jax.ShapeDtypeStruct(dims, single)
+
+        entry_shape = (HEADS, head_share, width)
+        out, dx, sums, entry, small = pl.pallas_call(
+            partial(layer_kernel, groups, units, PLAN),
+            out_shape=[
+                jax.ShapeDtypeStruct(inputs.shape, bfloat),
+                jax.ShapeDtypeStruct(inputs.shape, bfloat),
+                jax.ShapeDtypeStruct((grad_rows, width), bfloat),
+                jax.ShapeDtypeStruct((HEADS * head_share, width), bfloat),
+                shape(16, width),
+            ],
+            in_specs=[hbm, smem] + [hbm] * 14,
+            out_specs=[hbm] * 5,
+            scratch_shapes=[
+                pltpu.VMEM(inputs.shape, bfloat),
+                pltpu.VMEM(qb.shape, bfloat),
+                pltpu.VMEM(vb.shape, bfloat),
+                pltpu.VMEM(bo.shape, bfloat),
+                pltpu.VMEM(g1.shape, bfloat),
+                pltpu.VMEM(s1.shape, bfloat),
+                pltpu.VMEM(b1.shape, bfloat),
+                pltpu.VMEM(b2.shape, bfloat),
+                pltpu.VMEM(g2.shape, bfloat),
+                pltpu.VMEM(s2.shape, bfloat),
+                pltpu.VMEM(inputs.shape, bfloat),
+                pltpu.VMEM(inputs.shape, bfloat),
+                pltpu.VMEM((16, width), single),
+                pltpu.VMEM(we.shape, bfloat),
+                pltpu.VMEM(wo.shape, bfloat),
+                pltpu.VMEM(w1.shape, bfloat),
+                pltpu.VMEM(w2.shape, bfloat),
+                pltpu.VMEM(cot.shape, bfloat),
+                dma((15,)),
+                pltpu.VMEM((head_share, width), bfloat),
+                pltpu.VMEM((seqs, length, width), bfloat),
+                pltpu.VMEM((HEADS, 16, tokens), bfloat),
+                pltpu.VMEM((16, length), bfloat),
+                pltpu.VMEM((seqs, 8, length), single),
+                pltpu.VMEM((seqs, head_share, length), bfloat),
+                pltpu.VMEM((seqs, length, HEAD), bfloat),
+                pltpu.VMEM((seqs, length, HEAD), bfloat),
+                pltpu.VMEM((seqs, length, length), bfloat),
+                pltpu.VMEM((seqs, 1, length), single),
+                pltpu.VMEM((seqs, HEAD, length), single),
+                pltpu.VMEM((seqs, HEAD, length), bfloat),
+                pltpu.VMEM((width, rows), bfloat),
+                pltpu.VMEM((rows, width), single),
+                pltpu.VMEM((rows, 1), single),
+                pltpu.VMEM((rows, width), bfloat),
+                pltpu.VMEM((rows, ff), bfloat),
+                pltpu.VMEM((rows, ff), single),
+                pltpu.VMEM((rows, ff), bfloat),
+                pltpu.VMEM((rows, width), bfloat),
+                pltpu.VMEM((rows, width), single),
+                pltpu.VMEM((rows, width), bfloat),
+                pltpu.VMEM((width, rows), bfloat),
+                pltpu.VMEM((seqs, HEAD, length), bfloat),
+                pltpu.VMEM((seqs, head_share, length), bfloat),
+                pltpu.VMEM((HEAD, length), single),
+                pltpu.VMEM((HEAD, length), single),
+                pltpu.VMEM((3, width, rows), bfloat),
+                pltpu.VMEM((head_share, width), single),
+                pltpu.VMEM((head_share, width), bfloat),
+                pltpu.VMEM((others, head_share // groups, width), bfloat),
+                pltpu.VMEM((grad_rows, width), bfloat),
+                pltpu.VMEM((grad_rows, width), bfloat),
+                pltpu.VMEM((grad_rows + HEADS * head_share, width), bfloat),
+                pltpu.VMEM((3 + groups, 16, width), single),
+                dma((seqs, 8)),
+                dma((seqs, 8)),
+                dma((8,)),
+                dma((8,)),
+                dma((seqs, 8)),
+                dma((seqs, 8)),
+                dma((seqs, 8)),
+                dma((seqs, 8)),
+                dma((seqs, 8, 3)),
+                dma((seqs, 8, 3)),
+                dma((len(units), 8, others)),
+                dma((len(units), 8, others)),
+                dma((3, 8)),
+                dma((3, 8)),
+                dma((3 + groups,)),
+                dma((3 + groups,)),
+                dma((len(units) + 1,)),
+                dma((3, seqs)),
+            ],
+            compiler_params=pltpu.CompilerParams(
+                collective_id=0, has_side_effects=True, vmem_limit_bytes=60 * 2**20
+            ),
+            name="layer",
+        )(
+            inputs, blocks.transpose(0, 3, 2, 1), we, qb, vb, wo, bo, g1, s1, w1, b1, w2, b2,
+            g2, s2, cot,
+        )
+        pieces = grad_rows // WIDE
+        return pl.pallas_call(
+            widen_kernel,
+            in_specs=[hbm] * 5,
+            out_specs=[hbm] * 15,
+            out_shape=[
+                jax.ShapeDtypeStruct(inputs.shape, bfloat),
+                jax.ShapeDtypeStruct(inputs.shape, bfloat),
+                shape(width, 3 * width),
+                shape(width),
+                shape(width),
+                shape(width, width),
+                shape(width),
+                shape(width),
+                shape(width),
+                shape(width, ff),
+                shape(ff),
+                shape(ff, width),
+                shape(width),
+                shape(width),
+                shape(width),
+            ],
+            scratch_shapes=[
+                *[pltpu.VMEM((width,), single)] * 8,
+                pltpu.VMEM((grad_rows, width), bfloat),
+                pltpu.VMEM(entry_shape, bfloat),
+                pltpu.VMEM((16, width), single),
+                pltpu.VMEM((2, *inputs.shape), bfloat),
+                pltpu.VMEM((ff,), single),
+                pltpu.VMEM((ff, width), single),
+                pltpu.VMEM((width, ff), single),
+                pltpu.VMEM((width, width), single),
+                pltpu.VMEM((width, 3 * width), single),
+                dma((pieces + 4,)),
+                dma((pieces + 14,)),
+            ],
+            compiler_params=pltpu.CompilerParams(vmem_limit_bytes=60 * 2**20),
+            name="widen",
+        )(sums, entry.reshape(entry_shape), small, out, dx)
+
+    return run
+
+
 def solution(mesh):
     in_specs = (
         P("dp", "seq", None),
@@ -493,6 +1640,8 @@
         P(),
         P(),
     )
+    heads_fit = mesh.shape["seq"] == HEADS
+    plan = by_heads(mesh.shape["dp"]) if heads_fit else on_device
     return jax.shard_map(
-        on_device, mesh=mesh, in_specs=in_specs, out_specs=out_specs, check_vma=False
-    )
+        plan, mesh=mesh, in_specs=in_specs, out_specs=out_specs, check_vma=False
+    )

time: 873 us -> 128 us (0.15); the launches traced: 861 us -> 127 us
  waiting for transfers between devices: 315 us -> 0 us
  local copies, waits for them, and re-layouts: 228 us -> 0 us
  Pallas kernels: 0 us -> 126 us
  other arithmetic: 108 us -> 0 us
  blocking collectives: 88.4 us -> 0 us
  matrix products: 82.8 us -> 0 us
  starting transfers between devices: 23.1 us -> 0 us
  between operations: 15.2 us -> 0.66 us
    psum x4 -> x0, waiting for transfers between devices: 315 us -> none  [the longest x1 187 us: on_device(): lax.psum((entry_weight_grad, query_bias_grad, value_bias_grad, out_weight...]
    pallas_call x0 -> x2, Pallas kernels: none -> 126 us  [the longest x1 119 us: run(): pl.pallas_call(partial(layer_kernel, groups, units, PLAN), out_shape=[jax...]
    dot_general x24 -> x0, matrix products: 82.8 us -> none  [the longest x1 9.39 us: on_device(): jnp.einsum('shiqk,shikd->shiqd', prob_low, value_part, preferred_element_...]
    psum x2 -> x0, blocking collectives: 69.2 us -> none  [the longest x1 41.4 us: on_device(): lax.psum((entry_weight_grad, query_bias_grad, value_bias_grad, out_weight...]
    reshape x22 -> x0, local copies, waits for them, and re-layouts: 62.8 us -> none  [the longest x4 17.4 us: pair_blocks(): row_data.reshape(seq_count, length_here // block_rows, block_rows, 2, hea...]
    add x19 -> x0, other arithmetic: 30.6 us -> none  [the longest x7 22.7 us: merge_parts(): out_one * factor_one[..., None] + out_two * factor_two[..., None]]
    transpose x6 -> x0, local copies, waits for them, and re-layouts: 26.7 us -> none  [the longest x3 18.1 us: pair_tokens(): shaped.transpose(0, 2, 3, 4, 1, 5)]
    unnamed x103 -> x0, local copies, waits for them, and re-layouts: 25.3 us -> none
  transfers between devices with their start and end apart: 12 -> 0, of which waited for: 4 -> 0; matrix products, arithmetic and copies ran while one was open for 17% -> 0% of each run, Pallas kernels for 0% -> 0%
where the time goes in v2:
time: 128 us; the launch traced here: 127 us
  Pallas kernels  126 us (98%)
    pallas_call x1, Pallas kernels, run(): pl.pallas_call(partial(layer_kernel, groups, units, PLAN), out_shape=[jax...  119 us
    pallas_call x1, Pallas kernels, run(): pl.pallas_call(widen_kernel, in_specs=[hbm] * 5, out_specs=[hbm] * 15, ou...  7.07 us

profile of v2, /device:TPU:0, one launch (start us, length us, event | category | flops | bytes accessed | tf_op | source)
XLA Modules:
  0.0 126.6 jit_solution(7054333208847857734)
XLA Ops:
  0.7 118.8 %layer.1 = (bf16[3,128,512]{2,1,0:T(8,128)(2,1)}, bf16[3,128,512]{2,1,0:T(8,128)(2,1)}, bf16[4608,512]{1,0:T(8,128)(2,1)}, bf16[1536,512]{1,0:T(8,128)(2,1)}, f32[16,512]{1,0:T(8,128)}) custom-call(bf16[3,128,512]{2,1,0:T(8,128)(2,1)} %x_hbm.1, s32[3,3,2,8]{3,2,1,0:T(2,128)} %bitcast.3, bf16[512,1536]{1,0:T(8,128)(2,1)} %we_hbm.1, bf16[512]{0:T(512)(128)(2,1)} %qb_hbm.1, ...), custom_call_target="tpu_custom_call" | custom-call | tf_op jit(solution)/shard_map/layer/pallas_call | solution.py:1471
  119.5 7.1 %widen.1 = (bf16[3,128,512]{2,1,0:T(8,128)(2,1)}, bf16[3,128,512]{2,1,0:T(8,128)(2,1)}, f32[512,1536]{1,0:T(8,128)}, f32[512]{0:T(512)}, f32[512]{0:T(512)}, /*i...) custom-call(bf16[4608,512]{1,0:T(8,128)(2,1)} %get-tuple-element.20., ...), custom_call_target="tpu_custom_call" | custom-call | tf_op jit(solution)/shard_map/widen/pallas_call | solution.py:1565

commit v3 on v2

--- a/solution.py
+++ b/solution.py
@@ -463,7 +463,11 @@
 bfloat = jnp.bfloat16
 single = jnp.float32
 WIDE = 512
-QUERIES = 256
+QUERIES = 1024
+BACK_QUERIES = 512
+FORWARD = ((0, 2), (2, 3))
+BACKWARD = ((0, 1), (1, 3))
+TILES = 1024
 INV_SQRT2 = 0.7071067811865476
 INV_SQRT_2PI = 0.3989422804014327
 
@@ -538,6 +542,7 @@
     sums_hbm,
     entry_hbm,
     small_hbm,
+    bias_hbm,
     x_ref,
     qb_ref,
     vb_ref,
@@ -592,6 +597,10 @@
     landed,
     total,
     small_in,
+    bias_own,
+    bias_in,
+    bias_all,
+    bias_rows,
     x_send,
     x_recv,
     i_send,
@@ -608,6 +617,8 @@
     e_recv,
     v_send,
     v_recv,
+    b_send,
+    b_recv,
     done_sem,
     store_sem,
 ):
@@ -660,6 +671,14 @@
     def vec(ref):
         return ref[...].astype(single).reshape(1, ref.shape[0])
 
+    others = HEADS - 1
+
+    def take(ref, sem):
+        remote(ref, ref, sem, sem, place.in_plane(1)).wait_recv()
+
+    def gone(ref, sem):
+        remote(ref, ref, sem, sem, place.in_plane(1)).wait_send()
+
     lane = lax.broadcasted_iota(jnp.int32, (16, tokens), 1)
     row = lax.broadcasted_iota(jnp.int32, (16, tokens), 0)
     for h in range(HEADS):
@@ -672,46 +691,61 @@
                 numbers = jnp.where(row == s * 3 + j, picked, numbers)
         ids_send[h] = numbers.astype(single).astype(bfloat)
     small_ref[...] = jnp.zeros(small_ref.shape, single)
+    bias_rows[...] = jnp.zeros(bias_rows.shape, single)
+    bias_own[...] = jnp.zeros(bias_own.shape, single)
     entry_acc[...] = jnp.zeros(entry_acc.shape, single)
 
     load_x[0].wait()
     pl.semaphore_wait(barrier, 7 + groups - 1)
+
+    half_width = width // 2
 
     def x_copy(s, k):
         return remote(
             x_ref.at[s],
             xall.at[s, lanes_of(me), :],
-            x_send.at[s, k],
-            x_recv.at[s, k],
+            x_send,
+            x_recv.at[s, 2 if k == 1 else 0],
             place.in_plane(k),
         )
 
+    def x_across(s, k):
+        columns = slice(0, half_width) if k == 2 else slice(half_width, width)
+        slab = xall.at[s, lanes_of(place.peer(6 - k)), columns]
+        return remote(slab, slab, x_send, x_recv.at[s, 1], place.in_plane(k))
+
     def x_forward(s, k):
         slab = xall.at[s, lanes_of(place.peer(k)), :]
-        return remote(
-            slab, slab, x_send.at[s, k + 1], x_recv.at[s, k + 1], place.in_plane(1)
-        )
-
-    def x_arrived(s, k):
-        slab = xall.at[s, lanes_of(place.peer(k)), :]
-        remote(slab, slab, x_send.at[s, k], x_recv.at[s, k], place.in_plane(k)).wait_recv()
+        return remote(slab, slab, x_send, x_recv.at[s, 2], place.in_plane(1))
+
+    def x_arrived(s, which):
+        slabs = (2, 1, 4)[which]
+        take(xall.at[s, 0 : slabs * tokens, :], x_recv.at[s, which])
+
+    def x_begin(s):
+        for k in (2, 4, 1):
+            x_copy(s, k).start()
+
+    def x_pass(s):
+        x_arrived(s, 0)
+        for k in (2, 4):
+            x_across(s, k).start()
+            x_forward(s, k).start()
 
     def ids_copy(k):
         other = place.peer(k)
         return remote(
             ids_send.at[other],
             ids_all.at[:, lanes_of(me)],
-            i_send.at[k],
-            i_recv.at[k],
+            i_send,
+            i_recv,
             place.in_plane(k),
         )
 
-    for s in range(seqs):
-        for k in (6, 2, 4, 1):
-            x_copy(s, k).start()
-        if s == 0:
-            for k in range(1, 8):
-                ids_copy(k).start()
+    x_begin(0)
+    for k in range(1, 8):
+        ids_copy(k).start()
+    x_begin(1)
     ids_all[:, lanes_of(me)] = ids_send[me]
     for s in range(seqs):
         xall[s, lanes_of(me), :] = x_ref[s]
@@ -735,19 +769,7 @@
     query_column = column(qb_ref)
     value_column = column(vb_ref)
 
-    def arrived_at(ref_of, send, recv, s):
-        for k in range(1, 8):
-            slot = ref_of(place.peer(k))
-            remote(slot, slot, send.at[s, k], recv.at[s, k], place.in_plane(k)).wait_recv()
-
-    def sent(ref_of, send, recv, s):
-        for k in range(1, 8):
-            slot = ref_of(place.peer(k))
-            remote(slot, slot, send.at[s, k], recv.at[s, k], place.in_plane(k)).wait_send()
-
-    for k in range(1, 8):
-        slot = ids_all.at[:, lanes_of(place.peer(k))]
-        remote(slot, slot, i_send.at[k], i_recv.at[k], place.in_plane(k)).wait_recv()
+    take(ids_all.at[:, 0 : others * tokens], i_recv)
     for s in range(seqs):
         ids[s, 0:3, :] = ids_all[...].astype(single)[3 * s : 3 * s + 3]
 
@@ -761,29 +783,27 @@
         return remote(
             out_low.at[s, :, lanes_of(place.peer(k))],
             att_t.at[head_rows_of(me), seq_lanes(s)],
-            o_send.at[s, k],
-            o_recv.at[s, k],
+            o_send,
+            o_recv.at[s],
             place.in_plane(k),
         )
 
-    def project(s, k):
-        owner = place.peer(k)
-        packed = dot(wh_t[...], xall[s, lanes_of(owner), :], 1, 1)
-        qkv[s, 0:HEAD, lanes_of(owner)] = (
-            (packed[0:HEAD] + query_column) * HEAD**-0.5
-        ).astype(bfloat)
-        qkv[s, HEAD : 2 * HEAD, lanes_of(owner)] = packed[HEAD : 2 * HEAD].astype(bfloat)
-        qkv[s, 2 * HEAD :, lanes_of(owner)] = (packed[2 * HEAD :] + value_column).astype(bfloat)
+    def take_x(s):
+        x_arrived(s, 1)
+        x_forward(s, 6).start()
+
+        @pl.when(s < seqs - 2)
+        def _():
+            x_pass(s + 2)
+
+        x_arrived(s, 2)
+        packed = dot(wh_t[...], xall[s], 1, 1)
+        qkv[s, 0:HEAD, :] = ((packed[0:HEAD] + query_column) * HEAD**-0.5).astype(bfloat)
+        qkv[s, HEAD : 2 * HEAD, :] = packed[HEAD : 2 * HEAD].astype(bfloat)
+        qkv[s, 2 * HEAD :, :] = (packed[2 * HEAD :] + value_column).astype(bfloat)
 
     def attend(s, _):
-        for k in (2, 4, 6):
-            x_arrived(s, k)
-            x_forward(s, k).start()
-        for k in (0, 2, 4, 6):
-            project(s, k)
-        for k in (1, 3, 5, 7):
-            x_arrived(s, k)
-            project(s, k)
+        take_x(s)
         krow[s] = qkv[s, HEAD : 2 * HEAD, :].T
         vrow[s] = qkv[s, 2 * HEAD : 3 * HEAD, :].T
 
@@ -822,6 +842,10 @@
         att_t[head_rows_of(me), seq_lanes(s)] = out_low[s, :, lanes_of(me)]
         return 0
 
+    x_pass(0)
+    for s in range(2, seqs):
+        x_begin(s)
+    x_pass(1)
     lax.fori_loop(0, seqs, attend, 0)
     for copy in load_rest:
         copy.wait()
@@ -830,8 +854,8 @@
         return remote(
             gatt_t.at[head_rows_of(place.peer(k)), seq_lanes(s)],
             dout_t.at[s, :, lanes_of(me)],
-            d_send.at[s, k],
-            d_recv.at[s, k],
+            d_send,
+            d_recv.at[s],
             place.in_plane(k),
         )
 
@@ -845,13 +869,15 @@
 
     def store(which, s):
         src, dst = ((out_ref, out_hbm), (dx_ref, dx_hbm))[which]
-        return pltpu.make_async_copy(src.at[s], dst.at[s], store_sem.at[which, s])
-
-    def forward(s, _):
-        arrived_at(lambda other: att_t.at[head_rows_of(other), seq_lanes(s)], o_send, o_recv, s)
-        here = seq_lanes(s)
+        return pltpu.make_async_copy(src.at[s], dst.at[s], store_sem.at[which])
+
+    def forward(first_seq, last_seq):
+        for s in range(first_seq, last_seq):
+            take(att_t.at[0 : others * HEAD, seq_lanes(s)], o_recv.at[s])
+        here = slice(first_seq * tokens, last_seq * tokens)
+        count = (last_seq - first_seq) * tokens
         branch = dot(att_t[:, here], wo[...], 0, 0) + vec(bo_ref)
-        resid = x_ref[s].astype(single) + branch
+        resid = x_ref[first_seq:last_seq].reshape(count, width).astype(single) + branch
         center = resid - mean_of(resid)
         scale1 = lax.rsqrt(mean_of(center * center) + EPSILON)
         normed1 = center * scale1
@@ -873,9 +899,11 @@
         center = second - mean_of(second)
         scale2 = lax.rsqrt(mean_of(center * center) + EPSILON)
         normed2 = center * scale2
-        out_ref[s] = (normed2 * vec(g2_ref) + vec(s2_ref)).astype(bfloat)
-        store(0, s).start()
-        incoming = cot[s].astype(single)
+        result = (normed2 * vec(g2_ref) + vec(s2_ref)).astype(bfloat)
+        out_ref[first_seq:last_seq] = result.reshape(last_seq - first_seq, tokens, width)
+        for s in range(first_seq, last_seq):
+            store(0, s).start()
+        incoming = cot[first_seq:last_seq].reshape(count, width).astype(single)
         add_small(10, incoming * normed2)
         add_small(11, incoming)
         scaled = incoming * vec(g2_ref)
@@ -886,9 +914,9 @@
         grad_low = grad_second.astype(bfloat)
         grad_outer[here, :] = grad_low
         add_small(9, grad_low.astype(single))
-        return 0
-
-    lax.fori_loop(0, seqs, forward, 0)
+
+    for group in FORWARD:
+        forward(*group)
 
     def stages_of(unit):
         base, count, order = units[unit]
@@ -902,12 +930,17 @@
                 start = start + place.z * size
             else:
                 size = size // 2
-                index = place.x if axis == "x" else place.y
+                index = {"x": place.x, "y": place.y, "u": place.z % 2, "v": place.z // 2}[axis]
                 stages.append((axis, start + index * size, start + (1 - index) * size, size))
                 start = start + index * size
         return stages
 
-    hops = {"c": 1, "x": 2, "y": 4}
+    def partner(axis):
+        if axis in "uv":
+            step = 1 if axis == "u" else 2
+            bit = (place.z // step) % 2
+            return (place.z + step * (1 - 2 * bit), me)
+        return place.in_plane({"c": 1, "x": 2, "y": 4}[axis])
 
     def rows_at(start, count):
         return pl.ds(aligned(start, 16), count)
@@ -924,22 +957,23 @@
     def reduce_copies(unit, stage):
         axis, _, away, size = stages_of(unit)[stage]
         at = landing(unit, stage)
+        send, recv = rs_send.at[unit], rs_recv.at[unit, stage]
         if axis != "z":
             return [
                 remote(
                     part.at[rows_at(away, size), :],
                     landed.at[at : at + size, :],
-                    rs_send.at[unit, stage, 0],
-                    rs_recv.at[unit, stage, 0],
-                    place.in_plane(hops[axis]),
+                    send,
+                    recv,
+                    partner(axis),
                 )
             ]
         return [
             remote(
                 part.at[rows_at(away + ((place.z + offset) % groups) * size, size), :],
                 landed.at[at + (offset - 1) * size : at + offset * size, :],
-                rs_send.at[unit, stage, offset - 1],
-                rs_recv.at[unit, stage, offset - 1],
+                send,
+                recv,
                 place.in_column(offset),
             )
             for offset in range(1, groups)
@@ -950,120 +984,139 @@
             copy.start()
 
     def reduce_finish(unit, stage):
-        copies = reduce_copies(unit, stage)
-        for copy in copies:
-            copy.wait()
-        _, keep, _, size = stages_of(unit)[stage]
+        axis, keep, _, size = stages_of(unit)[stage]
         at = landing(unit, stage)
-        result = total if stage == 3 else part
-        tile = next(rows for rows in (64, 32, 16) if size % rows == 0)
+        count = groups - 1 if axis == "z" else 1
+        arrived = landed.at[at : at + count * size, :]
+        gone(arrived, rs_send.at[unit])
+        take(arrived, rs_recv.at[unit, stage])
+        result = total if stage == len(units[unit][2]) else part
+        tile = next(rows for rows in (128, 64, 32, 16) if size % rows == 0)
 
         def add(i, _):
             mine = rows_at(keep + i * tile, tile)
-            value = part[mine, :].astype(single)
-            for j in range(len(copies)):
-                value = value + landed[rows_at(at + j * size + i * tile, tile), :].astype(single)
+            if count == 1:
+                value = part[mine, :] + landed[rows_at(at + i * tile, tile), :]
+            else:
+                value = part[mine, :].astype(single)
+                for j in range(count):
+                    other = landed[rows_at(at + j * size + i * tile, tile), :]
+                    value = value + other.astype(single)
             result[mine, :] = value.astype(bfloat)
             return 0
 
-        lax.fori_loop(0, size // tile, add, 0)
-
-    def gather_copies(unit, stage, arriving):
-        axis, keep, away, size = stages_of(unit)[stage]
+        if size == tile:
+            add(0, 0)
+        else:
+            lax.fori_loop(0, size // tile, add, 0)
+
+    def gather_start(unit, stage):
+        axis, keep, _, size = stages_of(unit)[stage]
+        slot = total.at[rows_at(keep, size), :]
+        send, recv = rs_send.at[unit], rs_recv.at[unit, 5 + stage]
         if axis != "z":
-            slot = total.at[rows_at(away if arriving else keep, size), :]
-            return [
-                remote(
-                    slot,
-                    slot,
-                    rs_send.at[unit, 4 + stage, 0],
-                    rs_recv.at[unit, 4 + stage, 0],
-                    place.in_plane(hops[axis]),
-                )
-            ]
-        copies = []
-        for offset in range(1, groups):
-            owner = (place.z + groups - offset) % groups
-            slot = total.at[rows_at(away + owner * size if arriving else keep, size), :]
-            copies.append(
-                remote(
-                    slot,
-                    slot,
-                    rs_send.at[unit, 4 + stage, offset - 1],
-                    rs_recv.at[unit, 4 + stage, offset - 1],
-                    place.in_column(offset),
-                )
-            )
-        return copies
-
-    def gather_start(unit, stage):
-        for copy in gather_copies(unit, stage, False):
-            copy.start()
+            remote(slot, slot, send, recv, partner(axis)).start()
+        else:
+            for offset in range(1, groups):
+                remote(slot, slot, send, recv, place.in_column(offset)).start()
 
     def gather_finish(unit, stage):
-        for copy in gather_copies(unit, stage, False):
-            copy.wait_send()
-        for copy in gather_copies(unit, stage, True):
-            copy.wait_recv()
+        axis, _, away, size = stages_of(unit)[stage]
+        count = groups - 1 if axis == "z" else 1
+        slot = total.at[rows_at(away, count * size), :]
+        gone(slot, rs_send.at[unit])
+        take(slot, rs_recv.at[unit, 5 + stage])
 
     def result_copy(unit):
         base, count, _ = units[unit]
         at = pl.ds(base, count)
-        return pltpu.make_async_copy(total.at[at, :], sums_hbm.at[at, :], done_sem.at[unit])
+        return pltpu.make_async_copy(total.at[at, :], sums_hbm.at[at, :], done_sem.at[0])
 
     def step(unit, stage):
-        if stage < 3:
+        last = len(units[unit][2])
+        if stage < last:
             reduce_finish(unit, stage)
             reduce_start(unit, stage + 1)
-        elif stage == 3:
+        elif stage == last:
             reduce_finish(unit, stage)
-            gather_start(unit, 3)
-        elif stage < 7:
-            gather_finish(unit, 7 - stage)
-            gather_start(unit, 6 - stage)
+            gather_start(unit, last)
+        elif stage <= 2 * last:
+            gather_finish(unit, 2 * last + 1 - stage)
+            gather_start(unit, 2 * last - stage)
         else:
             gather_finish(unit, 0)
             result_copy(unit).start()
 
-    def ready_units(j, tile):
+    def ready_units(begin, end):
         for unit, (base, count, _) in enumerate(units):
-            last = (base + count) // WIDE - 1
-            if last in tile:
-
-                @pl.when(j == last - tile[0])
-                def _():
-                    reduce_start(unit, 0)
+            if begin < base + count <= end:
+                reduce_start(unit, 0)
 
     def steps_at(name, index):
-        for at, unit, stage in plan[name]:
-
-            @pl.when(index == at)
-            def _():
-                step(unit, stage)
+        for at, kind, *what in plan[name]:
+
+            def do():
+                small_step(*what) if kind == "small" else step(*what)
+
+            if not isinstance(index, int):
+                pl.when(index == at)(do)
+            elif index == at:
+                do()
 
     def keep_part(base, value):
-        part[pl.ds(aligned(base, 128), value.shape[0]), :] = value.astype(bfloat)
-
-    outer_tiles = range(0, ff // WIDE)
-    inner_tiles = range(ff // WIDE, 2 * ff // WIDE)
-
-    def outer_tile(j, _):
-        at = pl.ds(aligned(j * WIDE, WIDE), WIDE)
-        keep_part(j * WIDE, dot(hidden[:, at], grad_outer[...], 0, 0))
-        ready_units(j, outer_tiles)
-        return 0
-
-    def inner_tile(j, _):
-        at = pl.ds(aligned(j * WIDE, WIDE), WIDE)
-        keep_part(ff + j * WIDE, dot(low1[...], grad_inner[:, at], 0, 0))
-        ready_units(j, inner_tiles)
-        steps_at("inner", j)
-        return 0
-
-    lax.fori_loop(0, ff // WIDE, outer_tile, 0)
-
-    def backward(s, _):
-        here = seq_lanes(s)
+        part[base : base + value.shape[0], :] = value.astype(bfloat)
+
+    def small_copy(turn, device):
+        return remote(small_ref, small_in.at[turn], v_send, v_recv.at[min(turn, 3)], device)
+
+    def small_arrived(turn, count):
+        slot = small_in.at[turn : turn + count]
+        gone(slot, v_send)
+        take(slot, v_recv.at[turn])
+
+    def in_place_order(mine, others):
+        result = jnp.zeros(mine.shape, single)
+        for source in range(groups):
+            for offset in range(groups):
+                term = mine if offset == 0 else others[offset - 1]
+                result = result + jnp.where(
+                    (place.z + groups - offset) % groups == source, term, 0.0
+                )
+        return result
+
+    small_store = pltpu.make_async_copy(small_ref, small_hbm, store_sem.at[2])
+
+    def small_step(stage):
+        if stage > 0 and stage < 4:
+            small_arrived(stage - 1, 1)
+            small_ref[...] += small_in[stage - 1]
+        if stage < 3:
+            small_copy(stage, place.in_plane(2**stage)).start()
+        elif stage == 3:
+            for offset in range(1, groups):
+                small_copy(2 + offset, place.in_column(offset)).start()
+        else:
+            if groups > 1:
+                small_arrived(3, groups - 1)
+            terms = [small_in[2 + offset] for offset in range(1, groups)]
+            small_ref[...] = in_place_order(small_ref[...], terms)
+            small_store.start()
+
+    def outer_tile(start):
+        at = slice(start, start + TILES)
+        keep_part(start, dot(hidden[:, at], grad_outer[...], 0, 0))
+        ready_units(start, start + TILES)
+
+    def inner_tile(start):
+        for j in range(start, start + TILES, WIDE):
+            keep_part(ff + j, dot(low1[...], grad_inner[:, j : j + WIDE], 0, 0))
+        ready_units(ff + start, ff + start + TILES)
+
+    for start in range(0, ff, TILES):
+        outer_tile(start)
+
+    def backward(first_seq, last_seq):
+        here = slice(first_seq * tokens, last_seq * tokens)
         back = grad_resid[here, :]
         grad_low = grad_outer[here, :]
         for j in range(ff // WIDE):
@@ -1083,17 +1136,21 @@
         grad_branch[here, :] = grad
         add_small(2, grad.astype(single))
         gatt_t[:, here] = dot(wo[...], grad, 1, 1).astype(bfloat)
-        for k in (6, 7, 2, 3, 4, 5, 1):
-            dout_copy(s, k).start()
-        dout_t[s, :, lanes_of(me)] = gatt_t[head_rows_of(me), seq_lanes(s)]
-        steps_at("backward", s)
-        return 0
-
-    lax.fori_loop(0, seqs, backward, 0)
-    lax.fori_loop(0, ff // WIDE, inner_tile, 0)
+        for s in range(first_seq, last_seq):
+            for k in (6, 7, 2, 3, 4, 5, 1):
+                dout_copy(s, k).start()
+        for s in range(first_seq, last_seq):
+            dout_t[s, :, lanes_of(me)] = gatt_t[head_rows_of(me), seq_lanes(s)]
+
+    for index, group in enumerate(BACKWARD):
+        backward(*group)
+        steps_at("backward", index)
+    for index, start in enumerate(range(0, ff, TILES)):
+        inner_tile(start)
+        steps_at("inner", index)
     keep_part(2 * ff, jnp.dot(att_t[...], grad_branch[...], preferred_element_type=single))
-    ready_units(0, (2 * ff // WIDE,))
-    steps_at("inner", ff // WIDE)
+    ready_units(2 * ff, 2 * ff + width)
+    steps_at("inner", ff // TILES)
 
     def pack_copies(s, k):
         other = place.peer(k)
@@ -1101,24 +1158,17 @@
             remote(
                 dqkv.at[s, j * HEAD : (j + 1) * HEAD, lanes_of(other)],
                 gpacked_t.at[j, head_rows_of(me), seq_lanes(s)],
-                p_send.at[s, k, j],
-                p_recv.at[s, k, j],
+                p_send,
+                p_recv,
                 place.in_plane(k),
             )
             for j in range(3)
         ]
 
-    def back_chunk(turn, _):
-        s = turn // chunks
-        i = turn % chunks
-
-        @pl.when(i == 0)
-        def _():
-            arrived_at(lambda other: dout_t.at[s, :, lanes_of(other)], d_send, d_recv, s)
-            dk_acc[...] = jnp.zeros(dk_acc.shape, single)
-            dv_acc[...] = jnp.zeros(dv_acc.shape, single)
-
-        at = pl.ds(aligned(i * QUERIES, QUERIES), QUERIES)
+    turns = length // BACK_QUERIES
+
+    def back_math(s, i):
+        at = pl.ds(aligned(i * BACK_QUERIES, BACK_QUERIES), BACK_QUERIES)
         cot_t = dout_t[s, :, at].astype(single)
         inverse = inv_total[s, :, at]
         delta = inverse * jnp.sum(cot_t * out_wide[s, :, at], axis=0, keepdims=True)
@@ -1128,10 +1178,23 @@
         grad = (grown.astype(single) * grad).astype(bfloat)
         query_grad = jnp.dot(qkv[s, HEAD : 2 * HEAD, :], grad, preferred_element_type=single)
         dqkv[s, 0:HEAD, at] = (query_grad.astype(bfloat) * HEAD**-0.5).astype(bfloat)
-        dv_acc[...] += dot(cot_low, grown, 1, 1)
-        dk_acc[...] += dot(qkv[s, 0:HEAD, at], grad, 1, 1)
-
-        @pl.when(i == chunks - 1)
+        return dot(qkv[s, 0:HEAD, at], grad, 1, 1), dot(cot_low, grown, 1, 1)
+
+    def back_chunk(turn, _):
+        s = turn // turns
+        i = turn % turns
+
+        @pl.when(i == 0)
+        def _():
+            take(dout_t.at[s, :, 0 : others * tokens], d_recv.at[s])
+            dk_acc[...] = jnp.zeros(dk_acc.shape, single)
+            dv_acc[...] = jnp.zeros(dv_acc.shape, single)
+
+        key_grad, value_grad = back_math(s, i)
+        dk_acc[...] += key_grad
+        dv_acc[...] += value_grad
+
+        @pl.when(i == turns - 1)
         def _():
             dqkv[s, HEAD : 2 * HEAD, :] = dk_acc[...].astype(bfloat)
             dqkv[s, 2 * HEAD :, :] = dv_acc[...].astype(bfloat)
@@ -1147,7 +1210,7 @@
         steps_at("attention", turn)
         return 0
 
-    lax.fori_loop(0, seqs * chunks, back_chunk, 0)
+    lax.fori_loop(0, seqs * turns, back_chunk, 0)
 
     entry_base = 2 * ff + width
     head_share = 3 * HEAD
@@ -1164,23 +1227,26 @@
         return remote(
             entry_part.at[rows_at(target * fourth, fourth), :],
             entry_in.at[offset - 1],
-            e_send.at[0, offset],
-            e_recv.at[0, offset],
+            e_send.at[0],
+            e_recv.at[0],
             place.in_column(offset),
         )
 
-    def entry_back(offset, arriving):
-        owner = (place.z + groups - offset) % groups if arriving else place.z
-        slot = total.at[entry_rows(me, owner), :]
-        return remote(slot, slot, e_send.at[1, offset], e_recv.at[1, offset], place.in_column(offset))
-
-    def entry_plane(k, owner, to):
+    def entry_back(offset):
+        slot = total.at[entry_rows(me, place.z), :]
+        return remote(slot, slot, e_send.at[1], e_recv.at[1], place.in_column(offset))
+
+    def entry_plane(owner, to):
         slot = total.at[entry_rows(owner), :]
-        return remote(slot, slot, e_send.at[2, k], e_recv.at[2, k], place.in_plane(to))
+        recv = e_recv.at[3 if to == 1 else 2]
+        return remote(slot, slot, e_send.at[2], recv, place.in_plane(to))
+
+    def entry_shares(count):
+        return total.at[pl.ds(entry_base, count * head_share), :]
 
     def entry_result():
         rows = pl.ds(entry_base, HEADS * head_share)
-        return pltpu.make_async_copy(total.at[rows, :], entry_hbm, done_sem.at[len(units)])
+        return pltpu.make_async_copy(total.at[rows, :], entry_hbm, done_sem.at[1])
 
     def entry_step(stage):
         if stage == 0:
@@ -1188,85 +1254,75 @@
             for offset in range(1, groups):
                 entry_copy(offset).start()
         elif stage == 1:
+            if groups > 1:
+                gone(entry_in, e_send.at[0])
+                take(entry_in, e_recv.at[0])
             value = entry_part[rows_at(place.z * fourth, fourth), :].astype(single)
             for offset in range(1, groups):
-                entry_copy(offset).wait()
                 value = value + entry_in[offset - 1].astype(single)
             total[entry_rows(me, place.z), :] = value.astype(bfloat)
             for offset in range(1, groups):
-                entry_back(offset, False).start()
+                entry_back(offset).start()
         elif stage == 2:
-            for offset in range(1, groups):
-                entry_back(offset, False).wait_send()
-                entry_back(offset, True).wait_recv()
+            if groups > 1:
+                slot = total.at[pl.ds(entry_base, (groups - 1) * fourth), :]
+                gone(slot, e_send.at[1])
+                take(slot, e_recv.at[1])
             for k in (6, 2, 4, 1):
-                entry_plane(k, me, k).start()
+                entry_plane(me, k).start()
         elif stage == 3:
+            take(entry_shares(3), e_recv.at[2])
             for k in (2, 4, 6):
-                entry_plane(k, place.peer(k), k).wait_recv()
-                entry_plane(k + 1, place.peer(k), 1).start()
+                entry_plane(place.peer(k), 1).start()
         else:
-            for k in (1, 3, 5, 7):
-                entry_plane(k, place.peer(k), 1).wait_recv()
-            for k in (1, 2, 4, 6):
-                entry_plane(k, me, k).wait_send()
-            for k in (3, 5, 7):
-                entry_plane(k, place.peer(k - 1), 1).wait_send()
+            take(entry_shares(4), e_recv.at[3])
+            gone(entry_shares(7), e_send.at[2])
             entry_result().start()
 
-    def small_copy(turn, device):
+    bias_store = pltpu.make_async_copy(bias_rows, bias_hbm, store_sem.at[3])
+
+    def bias_column(offset):
         return remote(
-            small_ref, small_in.at[turn], v_send.at[turn], v_recv.at[turn], device
+            bias_own,
+            bias_in.at[offset - 1],
+            b_send.at[0],
+            b_recv.at[0],
+            place.in_column(offset),
         )
 
-    def small_column(offset):
-        return small_copy(2 + offset, place.in_column(offset))
-
-    def small_step(stage):
+    def bias_plane(k, owner):
+        slot = bias_all.at[owner]
+        return remote(slot, slot, b_send.at[1], b_recv.at[1], place.in_plane(k))
+
+    def bias_step(stage):
         if stage == 0:
             ones = jnp.ones((8, length), bfloat)
             sums = jnp.zeros((8, head_share), single)
             for s in range(seqs):
                 sums = sums + dot(ones, dqkv[s], 1, 1)
-            here = lax.broadcasted_iota(jnp.int32, (1, width), 1) // HEAD == me
+            bias_own[:, 0:head_share] = sums
+            for offset in range(1, groups):
+                bias_column(offset).start()
+        elif stage == 1:
+            if groups > 1:
+                gone(bias_in, b_send.at[0])
+                take(bias_in, b_recv.at[0])
+            terms = [bias_in[offset - 1] for offset in range(1, groups)]
+            bias_all[me] = in_place_order(bias_own[...], terms)
+            for k in range(1, 8):
+                bias_plane(k, me).start()
+        else:
+            gone(bias_all.at[0:others], b_send.at[1])
+            take(bias_all.at[0:others], b_recv.at[1])
             for at, start in ((0, 0), (1, 2 * HEAD)):
-                wide = jnp.concatenate([sums[0:1, start : start + HEAD]] * HEADS, axis=1)
-                small_ref[at : at + 1, :] = jnp.where(here, wide, 0.0)
-            small_copy(0, place.in_plane(1)).start()
-        elif stage < 3:
-            small_copy(stage - 1, place.in_plane(2 ** (stage - 1))).wait()
-            small_ref[...] += small_in[stage - 1]
-            small_copy(stage, place.in_plane(2**stage)).start()
-        elif stage == 3:
-            small_copy(2, place.in_plane(4)).wait()
-            small_ref[...] += small_in[2]
-            for offset in range(1, groups):
-                small_column(offset).start()
-        else:
-            for offset in range(1, groups):
-                small_column(offset).wait()
-            mine = small_ref[...]
-            sum_small = jnp.zeros(small_ref.shape, single)
-            for source in range(groups):
-                for offset in range(groups):
-                    term = mine if offset == 0 else small_in[2 + offset]
-                    sum_small = sum_small + jnp.where(
-                        (place.z + groups - offset) % groups == source, term, 0.0
-                    )
-            small_ref[...] = sum_small
-            small_store.start()
-
-    small_store = pltpu.make_async_copy(small_ref, small_hbm, store_sem.at[2, 0])
+                bias_rows[at : at + 1, :] = jnp.concatenate(
+                    [bias_all[p, 0:1, start : start + HEAD] for p in range(HEADS)], axis=1
+                )
+            bias_store.start()
+
 
     def input_step():
-        for s in range(seqs):
-            for k in range(1, 8):
-                other = place.peer(k)
-                for j in range(3):
-                    slot = gpacked_t.at[j, head_rows_of(other), seq_lanes(s)]
-                    remote(
-                        slot, slot, p_send.at[s, k, j], p_recv.at[s, k, j], place.in_plane(k)
-                    ).wait_recv()
+        take(gpacked_t.at[:, 0 : others * HEAD, :], p_recv)
         grad_in = grad_resid[...]
         for j in range(3):
             grad_in = grad_in + dot(gpacked_t[j], we[:, j * width : (j + 1) * width], 0, 1)
@@ -1279,34 +1335,29 @@
             step(*what)
         elif kind == "entry":
             entry_step(*what)
+        elif kind == "bias":
+            bias_step(*what)
         elif kind == "small":
             small_step(*what)
         else:
             input_step()
-    for unit in range(len(units)):
-        result_copy(unit).wait()
+    pltpu.make_async_copy(total.at[0 : sums_hbm.shape[0], :], sums_hbm, done_sem.at[0]).wait()
     entry_result().wait()
     small_store.wait()
-    for s in range(seqs):
-        store(0, s).wait()
-        store(1, s).wait()
-        for k in (1, 2, 4, 6):
-            x_copy(s, k).wait_send()
-        for k in (2, 4, 6):
-            x_forward(s, k).wait_send()
-        sent(lambda other: out_low.at[s, :, lanes_of(other)], o_send, o_recv, s)
-        sent(lambda other: gatt_t.at[head_rows_of(other), seq_lanes(s)], d_send, d_recv, s)
-        for k in range(1, 8):
-            for copy in pack_copies(s, k):
-                copy.wait_send()
-    for k in range(1, 8):
-        ids_copy(k).wait_send()
-
-
-def widen_kernel(sums_hbm, entry_hbm, small_hbm, out_in, dx_in, *refs):
+    bias_store.wait()
+    pltpu.make_async_copy(out_ref, out_hbm, store_sem.at[0]).wait()
+    pltpu.make_async_copy(dx_ref, dx_hbm, store_sem.at[1]).wait()
+    gone(xall.at[:, 0 : others * tokens, :], x_send)
+    gone(ids_all.at[:, 0 : others * tokens], i_send)
+    gone(out_low.at[:, :, 0 : others * tokens], o_send)
+    gone(gatt_t.at[0 : others * HEAD, :], d_send)
+    gone(dqkv.at[:, :, 0 : others * tokens], p_send)
+
+
+def widen_kernel(sums_hbm, entry_hbm, small_hbm, bias_hbm, out_in, dx_in, *refs):
     outs, vectors, scratch = refs[:15], refs[15:23], refs[23:]
-    sums, entry_low, small, passed, inner_bias, outer_v, inner_v, out_v, entry_v = scratch[:9]
-    in_sem, out_sem = scratch[9:]
+    sums, entry_low, small, bias, passed, inner_bias, outer_v, inner_v, out_v, entry_v = scratch[:10]
+    in_sem, out_sem = scratch[10:]
     out_ref, dx_ref, entry, query_b, value_b, out_w, out_b = outs[:7]
     gain1, shift1, inner_w, inner_b, outer_w, outer_b, gain2, shift2 = outs[7:]
     width = WIDE
@@ -1328,6 +1379,7 @@
         read(sums_hbm.at[rows, :], sums.at[rows, :])
     read(entry_hbm, entry_low)
     read(small_hbm, small)
+    read(bias_hbm, bias)
     read(out_in, passed.at[0])
     read(dx_in, passed.at[1])
     for i in range(pieces):
@@ -1357,7 +1409,7 @@
     write(passed.at[1], dx_ref)
 
     def small_row(at):
-        return small[at : at + 1, :].reshape(width)
+        return (bias if at < 2 else small)[at : at + 1, :].reshape(width)
 
     for j, (ref, at) in enumerate(
         (
@@ -1381,71 +1433,124 @@
 
 
 UNITS = (
-    (0, 1024, "xyz"),
-    (1024, 1024, "yxz"),
-    (2048, 1024, "xyz"),
-    (3072, 1024, "zyx"),
-    (4096, 512, "xyz"),
+    (0, 512, "yxuv"),
+    (512, 512, "zyx"),
+    (1024, 512, "xuvy"),
+    (1536, 512, "uxvy"),
+    (2048, 512, "yzx"),
+    (2560, 512, "xuyv"),
+    (3072, 512, "yxuv"),
+    (3584, 512, "xyuv"),
+    (4096, 512, "uxyv"),
 )
 PLAN = {
     "backward": (
-        (0, 0, 0),
-        (0, 1, 0),
+        (0, "unit", 1, 0),
+        (0, "unit", 2, 0),
+        (0, "unit", 0, 0),
+        (0, "unit", 3, 0),
     ),
     "inner": (
+        (0, "small", 0),
+        (2, "unit", 4, 0),
     ),
     "attention": (
-        (0, 2, 0),
-        (0, 3, 0),
-        (0, 0, 1),
-        (0, 1, 1),
-        (0, 4, 0),
-        (3, 0, 2),
-        (5, 2, 1),
-        (6, 1, 2),
-        (8, 3, 1),
-        (8, 2, 2),
-        (8, 4, 1),
-        (9, 0, 3),
-        (11, 1, 3),
-        (11, 3, 2),
+        (0, "unit", 5, 0),
+        (0, "unit", 6, 0),
+        (0, "unit", 7, 0),
+        (0, "unit", 0, 1),
+        (0, "small", 1),
+        (0, "unit", 2, 1),
+        (0, "unit", 8, 0),
+        (1, "unit", 3, 1),
+        (1, "unit", 1, 1),
+        (3, "unit", 4, 1),
+        (3, "unit", 2, 2),
+        (3, "unit", 5, 1),
+        (4, "unit", 6, 1),
+        (4, "unit", 8, 1),
+        (4, "unit", 7, 1),
+        (5, "unit", 0, 2),
+        (5, "small", 2),
     ),
     "tail": (
         ("entry", 0),
-        ("small", 0),
+        ("bias", 0),
+        ("unit", 4, 2),
+        ("unit", 1, 2),
+        ("unit", 5, 2),
         ("unit", 2, 3),
-        ("unit", 4, 2),
-        ("small", 1),
+        ("unit", 0, 3),
+        ("unit", 3, 2),
+        ("entry", 1),
+        ("unit", 7, 2),
+        ("bias", 1),
         ("unit", 0, 4),
+        ("unit", 3, 3),
+        ("unit", 6, 2),
+        ("unit", 8, 2),
+        ("small", 3),
+        ("unit", 5, 3),
+        ("unit", 2, 4),
+        ("unit", 7, 3),
+        ("unit", 3, 4),
+        ("unit", 6, 3),
+        ("entry", 2),
+        ("unit", 8, 3),
+        ("unit", 0, 5),
+        ("unit", 2, 5),
+        ("unit", 4, 3),
         ("input",),
-        ("small", 2),
+        ("bias", 2),
+        ("unit", 1, 3),
+        ("small", 4),
+        ("unit", 3, 5),
+        ("unit", 5, 4),
+        ("unit", 0, 6),
+        ("unit", 7, 4),
+        ("unit", 6, 4),
+        ("unit", 8, 4),
+        ("unit", 2, 6),
+        ("unit", 3, 6),
+        ("unit", 5, 5),
+        ("unit", 7, 5),
+        ("unit", 6, 5),
+        ("unit", 2, 7),
+        ("unit", 4, 4),
+        ("entry", 3),
+        ("unit", 8, 5),
         ("unit", 1, 4),
-        ("unit", 3, 3),
-        ("unit", 0, 5),
-        ("entry", 1),
-        ("small", 3),
+        ("unit", 5, 6),
+        ("unit", 0, 7),
+        ("unit", 7, 6),
+        ("entry", 4),
+        ("unit", 6, 6),
+        ("unit", 3, 7),
+        ("unit", 8, 6),
         ("unit", 1, 5),
-        ("unit", 2, 4),
-        ("unit", 3, 4),
-        ("unit", 4, 3),
-        ("entry", 2),
-        ("unit", 0, 6),
-        ("unit", 0, 7),
+        ("unit", 2, 8),
+        ("unit", 5, 7),
+        ("unit", 4, 5),
+        ("unit", 2, 9),
+        ("unit", 0, 8),
+        ("unit", 6, 7),
+        ("unit", 0, 9),
+        ("unit", 7, 7),
+        ("unit", 8, 7),
+        ("unit", 3, 8),
+        ("unit", 3, 9),
+        ("unit", 5, 8),
+        ("unit", 4, 6),
+        ("unit", 5, 9),
+        ("unit", 4, 7),
         ("unit", 1, 6),
-        ("small", 4),
-        ("unit", 4, 4),
+        ("unit", 7, 8),
+        ("unit", 6, 8),
         ("unit", 1, 7),
-        ("unit", 2, 5),
-        ("unit", 3, 5),
-        ("entry", 3),
-        ("unit", 4, 5),
-        ("unit", 2, 6),
-        ("entry", 4),
-        ("unit", 2, 7),
-        ("unit", 3, 6),
-        ("unit", 4, 6),
-        ("unit", 3, 7),
-        ("unit", 4, 7),
+        ("unit", 7, 9),
+        ("unit", 8, 8),
+        ("unit", 6, 9),
+        ("unit", 8, 9),
     ),
 }
 
@@ -1468,7 +1573,7 @@
             return jax.ShapeDtypeStruct(dims, single)
 
         entry_shape = (HEADS, head_share, width)
-        out, dx, sums, entry, small = pl.pallas_call(
+        out, dx, sums, entry, small, bias = pl.pallas_call(
             partial(layer_kernel, groups, units, PLAN),
             out_shape=[
                 jax.ShapeDtypeStruct(inputs.shape, bfloat),
@@ -1476,9 +1581,10 @@
                 jax.ShapeDtypeStruct((grad_rows, width), bfloat),
                 jax.ShapeDtypeStruct((HEADS * head_share, width), bfloat),
                 shape(16, width),
+                shape(8, width),
             ],
             in_specs=[hbm, smem] + [hbm] * 14,
-            out_specs=[hbm] * 5,
+            out_specs=[hbm] * 6,
             scratch_shapes=[
                 pltpu.VMEM(inputs.shape, bfloat),
                 pltpu.VMEM(qb.shape, bfloat),
@@ -1534,24 +1640,30 @@
                 pltpu.VMEM((grad_rows, width), bfloat),
                 pltpu.VMEM((grad_rows + HEADS * head_share, width), bfloat),
                 pltpu.VMEM((3 + groups, 16, width), single),
-                dma((seqs, 8)),
-                dma((seqs, 8)),
-                dma((8,)),
-                dma((8,)),
-                dma((seqs, 8)),
-                dma((seqs, 8)),
-                dma((seqs, 8)),
-                dma((seqs, 8)),
-                dma((seqs, 8, 3)),
-                dma((seqs, 8, 3)),
-                dma((len(units), 8, others)),
-                dma((len(units), 8, others)),
-                dma((3, 8)),
-                dma((3, 8)),
-                dma((3 + groups,)),
-                dma((3 + groups,)),
-                dma((len(units) + 1,)),
-                dma((3, seqs)),
+                pltpu.VMEM((8, 256), single),
+                pltpu.VMEM((others, 8, 256), single),
+                pltpu.VMEM((HEADS, 8, 256), single),
+                pltpu.VMEM((8, width), single),
+                dma(()),
+                dma((seqs, 3)),
+                dma(()),
+                dma(()),
+                dma(()),
+                dma((seqs,)),
+                dma(()),
+                dma((seqs,)),
+                dma(()),
+                dma(()),
+                dma((len(units),)),
+                dma((len(units), 10)),
+                dma((3,)),
+                dma((4,)),
+                dma(()),
+                dma((4,)),
+                dma((2,)),
+                dma((2,)),
+                dma((2,)),
+                dma((4,)),
             ],
             compiler_params=pltpu.CompilerParams(
                 collective_id=0, has_side_effects=True, vmem_limit_bytes=60 * 2**20
@@ -1564,7 +1676,7 @@
         pieces = grad_rows // WIDE
         return pl.pallas_call(
             widen_kernel,
-            in_specs=[hbm] * 5,
+            in_specs=[hbm] * 6,
             out_specs=[hbm] * 15,
             out_shape=[
                 jax.ShapeDtypeStruct(inputs.shape, bfloat),
@@ -1588,18 +1700,19 @@
                 pltpu.VMEM((grad_rows, width), bfloat),
                 pltpu.VMEM(entry_shape, bfloat),
                 pltpu.VMEM((16, width), single),
+                pltpu.VMEM((8, width), single),
                 pltpu.VMEM((2, *inputs.shape), bfloat),
                 pltpu.VMEM((ff,), single),
                 pltpu.VMEM((ff, width), single),
                 pltpu.VMEM((width, ff), single),
                 pltpu.VMEM((width, width), single),
                 pltpu.VMEM((width, 3 * width), single),
-                dma((pieces + 4,)),
+                dma((pieces + 5,)),
                 dma((pieces + 14,)),
             ],
             compiler_params=pltpu.CompilerParams(vmem_limit_bytes=60 * 2**20),
             name="widen",
-        )(sums, entry.reshape(entry_shape), small, out, dx)
+        )(sums, entry.reshape(entry_shape), small, bias, out, dx)
 
     return run
 

time: 128 us -> 109 us (0.85)
  Pallas kernels: 126 us -> 108 us
    pallas_call x1, Pallas kernels: 119 us -> 101 us  [run(): pl.pallas_call(partial(layer_kernel, groups, units, PLAN), out_shape=[jax...]
where the time goes in v3:
time: 109 us; the launch traced here: 108 us
  Pallas kernels  108 us (99%)
    pallas_call x1, Pallas kernels, run(): pl.pallas_call(partial(layer_kernel, groups, units, PLAN), out_shape=[jax...  101 us
    pallas_call x1, Pallas kernels, run(): pl.pallas_call(widen_kernel, in_specs=[hbm] * 6, out_specs=[hbm] * 15, ou...  7.08 us

profile of v3, /device:TPU:0, one launch (start us, length us, event | category | flops | bytes accessed | tf_op | source)
XLA Modules:
  0.0 108.5 jit_solution(3458834177153846680)
XLA Ops:
  0.7 100.6 %layer.1 = (bf16[3,128,512]{2,1,0:T(8,128)(2,1)}, bf16[3,128,512]{2,1,0:T(8,128)(2,1)}, bf16[4608,512]{1,0:T(8,128)(2,1)}, bf16[1536,512]{1,0:T(8,128)(2,1)}, f32[16,512]{1,0:T(8,128)}, /*index=5*/f32[8,512]{1,0:T(8,128)}) custom-call(bf16[3,128,512]{2,1,0:T(8,128)(2,1)} %x_hbm.1, s32[3,3,2,8]{3,2,1,0:T(2,128)} %bitcast.3, bf16[512,1536]{1,0:T(8,128)(2,1)} %we_hbm.1, ...), custom_call_target="tpu_custom_call" | custom-call | tf_op jit(solution)/shard_map/layer/pallas_call | solution.py:1576
  101.2 7.1 %widen.1 = (bf16[3,128,512]{2,1,0:T(8,128)(2,1)}, bf16[3,128,512]{2,1,0:T(8,128)(2,1)}, f32[512,1536]{1,0:T(8,128)}, f32[512]{0:T(512)}, f32[512]{0:T(512)}, /*i...) custom-call(bf16[4608,512]{1,0:T(8,128)(2,1)} %get-tuple-element.21., ...), custom_call_target="tpu_custom_call" | custom-call | tf_op jit(solution)/shard_map/widen/pallas_call | solution.py:1677

commit v4 on v3

--- a/solution.py
+++ b/solution.py
@@ -466,8 +466,18 @@
 QUERIES = 1024
 BACK_QUERIES = 512
 FORWARD = ((0, 2), (2, 3))
-BACKWARD = ((0, 1), (1, 3))
+EARLY = (
+    ("outer", 0),
+    ("back", 0, 1),
+    ("outer", 1024),
+    ("back", 1, 3),
+    ("inner", 0),
+    ("inner", 1024),
+    ("out",),
+)
 TILES = 1024
+LAYER_VMEM = 56 * 2**20
+WIDEN_VMEM = 56 * 2**20
 INV_SQRT2 = 0.7071067811865476
 INV_SQRT_2PI = 0.3989422804014327
 
@@ -539,8 +549,7 @@
     cot_hbm,
     out_hbm,
     dx_hbm,
-    sums_hbm,
-    entry_hbm,
+    total,
     small_hbm,
     bias_hbm,
     x_ref,
@@ -595,7 +604,6 @@
     entry_in,
     part,
     landed,
-    total,
     small_in,
     bias_own,
     bias_in,
@@ -619,7 +627,6 @@
     v_recv,
     b_send,
     b_recv,
-    done_sem,
     store_sem,
 ):
     seqs, tokens, width = x_ref.shape
@@ -1027,11 +1034,6 @@
         gone(slot, rs_send.at[unit])
         take(slot, rs_recv.at[unit, 5 + stage])
 
-    def result_copy(unit):
-        base, count, _ = units[unit]
-        at = pl.ds(base, count)
-        return pltpu.make_async_copy(total.at[at, :], sums_hbm.at[at, :], done_sem.at[0])
-
     def step(unit, stage):
         last = len(units[unit][2])
         if stage < last:
@@ -1045,7 +1047,6 @@
             gather_start(unit, 2 * last - stage)
         else:
             gather_finish(unit, 0)
-            result_copy(unit).start()
 
     def ready_units(begin, end):
         for unit, (base, count, _) in enumerate(units):
@@ -1111,9 +1112,6 @@
         for j in range(start, start + TILES, WIDE):
             keep_part(ff + j, dot(low1[...], grad_inner[:, j : j + WIDE], 0, 0))
         ready_units(ff + start, ff + start + TILES)
-
-    for start in range(0, ff, TILES):
-        outer_tile(start)
 
     def backward(first_seq, last_seq):
         here = slice(first_seq * tokens, last_seq * tokens)
@@ -1142,15 +1140,13 @@
         for s in range(first_seq, last_seq):
             dout_t[s, :, lanes_of(me)] = gatt_t[head_rows_of(me), seq_lanes(s)]
 
-    for index, group in enumerate(BACKWARD):
-        backward(*group)
-        steps_at("backward", index)
-    for index, start in enumerate(range(0, ff, TILES)):
-        inner_tile(start)
-        steps_at("inner", index)
-    keep_part(2 * ff, jnp.dot(att_t[...], grad_branch[...], preferred_element_type=single))
-    ready_units(2 * ff, 2 * ff + width)
-    steps_at("inner", ff // TILES)
+    def out_tile():
+        keep_part(2 * ff, jnp.dot(att_t[...], grad_branch[...], preferred_element_type=single))
+        ready_units(2 * ff, 2 * ff + width)
+
+    for index, (kind, *what) in enumerate(EARLY):
+        {"outer": outer_tile, "back": backward, "inner": inner_tile, "out": out_tile}[kind](*what)
+        steps_at("early", index)
 
     def pack_copies(s, k):
         other = place.peer(k)
@@ -1236,17 +1232,13 @@
         slot = total.at[entry_rows(me, place.z), :]
         return remote(slot, slot, e_send.at[1], e_recv.at[1], place.in_column(offset))
 
-    def entry_plane(owner, to):
-        slot = total.at[entry_rows(owner), :]
-        recv = e_recv.at[3 if to == 1 else 2]
-        return remote(slot, slot, e_send.at[2], recv, place.in_plane(to))
+    def entry_plane(owner, to, half, turn=2):
+        columns = (slice(0, half_width), slice(half_width, width), slice(0, width))[half]
+        slot = total.at[entry_rows(owner), columns]
+        return remote(slot, slot, e_send.at[2], e_recv.at[turn], place.in_plane(to))
 
     def entry_shares(count):
         return total.at[pl.ds(entry_base, count * head_share), :]
-
-    def entry_result():
-        rows = pl.ds(entry_base, HEADS * head_share)
-        return pltpu.make_async_copy(total.at[rows, :], entry_hbm, done_sem.at[1])
 
     def entry_step(stage):
         if stage == 0:
@@ -1268,16 +1260,22 @@
                 slot = total.at[pl.ds(entry_base, (groups - 1) * fourth), :]
                 gone(slot, e_send.at[1])
                 take(slot, e_recv.at[1])
-            for k in (6, 2, 4, 1):
-                entry_plane(me, k).start()
+            entry_plane(me, 2, 0).start()
+            entry_plane(me, 4, 1).start()
+            entry_plane(me, 1, 2, 4).start()
         elif stage == 3:
-            take(entry_shares(3), e_recv.at[2])
+            take(entry_shares(1), e_recv.at[2])
+            for owner in (me, place.peer(2)):
+                entry_plane(owner, 4, 0, 3).start()
+            for owner in (me, place.peer(4)):
+                entry_plane(owner, 2, 1, 3).start()
+        elif stage == 4:
+            take(entry_shares(2), e_recv.at[3])
             for k in (2, 4, 6):
-                entry_plane(place.peer(k), 1).start()
+                entry_plane(place.peer(k), 1, 2, 4).start()
         else:
-            take(entry_shares(4), e_recv.at[3])
+            take(entry_shares(4), e_recv.at[4])
             gone(entry_shares(7), e_send.at[2])
-            entry_result().start()
 
     bias_store = pltpu.make_async_copy(bias_rows, bias_hbm, store_sem.at[3])
 
@@ -1300,7 +1298,7 @@
             sums = jnp.zeros((8, head_share), single)
             for s in range(seqs):
                 sums = sums + dot(ones, dqkv[s], 1, 1)
-            bias_own[:, 0:head_share] = sums
+            bias_own[...] = jnp.concatenate([sums[:, 0:HEAD], sums[:, 2 * HEAD :]], axis=1)
             for offset in range(1, groups):
                 bias_column(offset).start()
         elif stage == 1:
@@ -1314,7 +1312,7 @@
         else:
             gone(bias_all.at[0:others], b_send.at[1])
             take(bias_all.at[0:others], b_recv.at[1])
-            for at, start in ((0, 0), (1, 2 * HEAD)):
+            for at, start in ((0, 0), (1, HEAD)):
                 bias_rows[at : at + 1, :] = jnp.concatenate(
                     [bias_all[p, 0:1, start : start + HEAD] for p in range(HEADS)], axis=1
                 )
@@ -1341,8 +1339,6 @@
             small_step(*what)
         else:
             input_step()
-    pltpu.make_async_copy(total.at[0 : sums_hbm.shape[0], :], sums_hbm, done_sem.at[0]).wait()
-    entry_result().wait()
     small_store.wait()
     bias_store.wait()
     pltpu.make_async_copy(out_ref, out_hbm, store_sem.at[0]).wait()
@@ -1354,15 +1350,16 @@
     gone(dqkv.at[:, :, 0 : others * tokens], p_send)
 
 
-def widen_kernel(sums_hbm, entry_hbm, small_hbm, bias_hbm, out_in, dx_in, *refs):
+def widen_kernel(sums, small_hbm, bias_hbm, out_in, dx_in, *refs):
     outs, vectors, scratch = refs[:15], refs[15:23], refs[23:]
-    sums, entry_low, small, bias, passed, inner_bias, outer_v, inner_v, out_v, entry_v = scratch[:10]
-    in_sem, out_sem = scratch[10:]
+    small, bias, passed, inner_bias, outer_v, inner_v, out_v, entry_v = scratch[:8]
+    in_sem, out_sem = scratch[8:]
     out_ref, dx_ref, entry, query_b, value_b, out_w, out_b = outs[:7]
     gain1, shift1, inner_w, inner_b, outer_w, outer_b, gain2, shift2 = outs[7:]
     width = WIDE
     ff = outer_w.shape[0]
-    pieces = sums.shape[0] // WIDE
+    pieces = (2 * ff + width) // WIDE
+    head_share = 3 * HEAD
     reads = []
     writes = []
 
@@ -1374,16 +1371,11 @@
         writes.append(pltpu.make_async_copy(src, dst, out_sem.at[len(writes)]))
         writes[-1].start()
 
-    for i in range(pieces):
-        rows = slice(i * WIDE, (i + 1) * WIDE)
-        read(sums_hbm.at[rows, :], sums.at[rows, :])
-    read(entry_hbm, entry_low)
     read(small_hbm, small)
     read(bias_hbm, bias)
     read(out_in, passed.at[0])
     read(dx_in, passed.at[1])
     for i in range(pieces):
-        reads[i].wait()
         rows = slice(i * WIDE, (i + 1) * WIDE)
         value = sums[rows, :].astype(single)
         j = i - ff // WIDE
@@ -1397,13 +1389,13 @@
         else:
             out_v[...] = value
             write(out_v, out_w)
-    reads[pieces].wait()
     for j in range(3):
         columns = slice(j * width, (j + 1) * width)
-        value = entry_low[:, j * HEAD : (j + 1) * HEAD, :].reshape(width, width)
+        starts = [2 * ff + width + h * head_share + j * HEAD for h in range(HEADS)]
+        value = jnp.concatenate([sums[at : at + HEAD, :] for at in starts], axis=0)
         entry_v[:, columns] = value.astype(single).T
         write(entry_v.at[:, columns], entry.at[:, columns])
-    for read_done in reads[pieces + 1 :]:
+    for read_done in reads:
         read_done.wait()
     write(passed.at[0], out_ref)
     write(passed.at[1], dx_ref)
@@ -1433,124 +1425,117 @@
 
 
 UNITS = (
-    (0, 512, "yxuv"),
-    (512, 512, "zyx"),
-    (1024, 512, "xuvy"),
-    (1536, 512, "uxvy"),
-    (2048, 512, "yzx"),
-    (2560, 512, "xuyv"),
-    (3072, 512, "yxuv"),
-    (3584, 512, "xyuv"),
-    (4096, 512, "uxyv"),
+    (0, 512, "xyz"),
+    (512, 512, "yuvx"),
+    (1024, 512, "zyx"),
+    (1536, 512, "uyxv"),
+    (2048, 512, "xyuv"),
+    (2560, 512, "yuxv"),
+    (3072, 512, "xyz"),
+    (3584, 512, "xyz"),
+    (4096, 512, "zyx"),
 )
 PLAN = {
-    "backward": (
-        (0, "unit", 1, 0),
-        (0, "unit", 2, 0),
-        (0, "unit", 0, 0),
-        (0, "unit", 3, 0),
-    ),
-    "inner": (
-        (0, "small", 0),
-        (2, "unit", 4, 0),
+    "early": (
+        (1, "unit", 1, 0),
+        (1, "unit", 0, 0),
+        (3, "small", 0),
+        (3, "unit", 3, 0),
+        (3, "unit", 2, 0),
+        (4, "small", 1),
+        (6, "unit", 0, 1),
+        (6, "unit", 4, 0),
+        (6, "unit", 5, 0),
+        (6, "unit", 1, 1),
     ),
     "attention": (
-        (0, "unit", 5, 0),
+        (0, "unit", 7, 0),
+        (0, "unit", 8, 0),
         (0, "unit", 6, 0),
-        (0, "unit", 7, 0),
-        (0, "unit", 0, 1),
-        (0, "small", 1),
-        (0, "unit", 2, 1),
-        (0, "unit", 8, 0),
+        (1, "unit", 0, 2),
         (1, "unit", 3, 1),
-        (1, "unit", 1, 1),
+        (1, "small", 2),
         (3, "unit", 4, 1),
-        (3, "unit", 2, 2),
         (3, "unit", 5, 1),
-        (4, "unit", 6, 1),
-        (4, "unit", 8, 1),
+        (3, "unit", 2, 1),
         (4, "unit", 7, 1),
-        (5, "unit", 0, 2),
-        (5, "small", 2),
+        (4, "unit", 1, 2),
     ),
     "tail": (
         ("entry", 0),
         ("bias", 0),
+        ("unit", 6, 1),
+        ("unit", 3, 2),
+        ("small", 3),
+        ("unit", 8, 1),
+        ("unit", 0, 3),
+        ("unit", 5, 2),
+        ("unit", 1, 3),
         ("unit", 4, 2),
-        ("unit", 1, 2),
-        ("unit", 5, 2),
-        ("unit", 2, 3),
-        ("unit", 0, 3),
-        ("unit", 3, 2),
+        ("unit", 2, 2),
         ("entry", 1),
+        ("bias", 1),
         ("unit", 7, 2),
-        ("bias", 1),
+        ("small", 4),
+        ("unit", 4, 3),
         ("unit", 0, 4),
         ("unit", 3, 3),
+        ("input",),
+        ("unit", 1, 4),
+        ("unit", 5, 3),
+        ("unit", 8, 2),
+        ("unit", 2, 3),
         ("unit", 6, 2),
-        ("unit", 8, 2),
-        ("small", 3),
-        ("unit", 5, 3),
+        ("entry", 2),
+        ("bias", 2),
+        ("unit", 0, 5),
+        ("unit", 7, 3),
+        ("unit", 4, 4),
+        ("unit", 1, 5),
+        ("unit", 3, 4),
+        ("unit", 8, 3),
         ("unit", 2, 4),
-        ("unit", 7, 3),
-        ("unit", 3, 4),
+        ("unit", 5, 4),
         ("unit", 6, 3),
-        ("entry", 2),
-        ("unit", 8, 3),
-        ("unit", 0, 5),
+        ("entry", 3),
         ("unit", 2, 5),
-        ("unit", 4, 3),
-        ("input",),
-        ("bias", 2),
-        ("unit", 1, 3),
-        ("small", 4),
+        ("unit", 7, 4),
+        ("unit", 4, 5),
+        ("unit", 0, 6),
+        ("unit", 1, 6),
+        ("unit", 8, 4),
         ("unit", 3, 5),
-        ("unit", 5, 4),
-        ("unit", 0, 6),
-        ("unit", 7, 4),
+        ("unit", 0, 7),
+        ("unit", 5, 5),
         ("unit", 6, 4),
-        ("unit", 8, 4),
+        ("entry", 4),
+        ("unit", 3, 6),
+        ("unit", 7, 5),
+        ("unit", 5, 6),
+        ("unit", 4, 6),
+        ("unit", 8, 5),
+        ("entry", 5),
+        ("unit", 1, 7),
+        ("unit", 6, 5),
         ("unit", 2, 6),
-        ("unit", 3, 6),
-        ("unit", 5, 5),
-        ("unit", 7, 5),
-        ("unit", 6, 5),
+        ("unit", 3, 7),
+        ("unit", 5, 7),
         ("unit", 2, 7),
-        ("unit", 4, 4),
-        ("entry", 3),
-        ("unit", 8, 5),
-        ("unit", 1, 4),
-        ("unit", 5, 6),
-        ("unit", 0, 7),
+        ("unit", 4, 7),
         ("unit", 7, 6),
-        ("entry", 4),
+        ("unit", 7, 7),
+        ("unit", 1, 8),
         ("unit", 6, 6),
-        ("unit", 3, 7),
+        ("unit", 1, 9),
+        ("unit", 6, 7),
         ("unit", 8, 6),
-        ("unit", 1, 5),
-        ("unit", 2, 8),
-        ("unit", 5, 7),
-        ("unit", 4, 5),
-        ("unit", 2, 9),
-        ("unit", 0, 8),
-        ("unit", 6, 7),
-        ("unit", 0, 9),
-        ("unit", 7, 7),
+        ("unit", 5, 8),
+        ("unit", 4, 8),
         ("unit", 8, 7),
         ("unit", 3, 8),
+        ("unit", 5, 9),
+        ("unit", 4, 9),
         ("unit", 3, 9),
-        ("unit", 5, 8),
-        ("unit", 4, 6),
-        ("unit", 5, 9),
-        ("unit", 4, 7),
-        ("unit", 1, 6),
-        ("unit", 7, 8),
-        ("unit", 6, 8),
-        ("unit", 1, 7),
-        ("unit", 7, 9),
-        ("unit", 8, 8),
-        ("unit", 6, 9),
-        ("unit", 8, 9),
     ),
 }
 
@@ -1566,25 +1551,24 @@
         others = max(groups - 1, 1)
         head_share = 3 * HEAD
         smem = pl.BlockSpec(memory_space=pltpu.SMEM)
+        vmem = pl.BlockSpec(memory_space=pltpu.VMEM)
         hbm = pl.BlockSpec(memory_space=pl.ANY)
         dma = pltpu.SemaphoreType.DMA
 
         def shape(*dims):
             return jax.ShapeDtypeStruct(dims, single)
 
-        entry_shape = (HEADS, head_share, width)
-        out, dx, sums, entry, small, bias = pl.pallas_call(
+        out, dx, total, small, bias = pl.pallas_call(
             partial(layer_kernel, groups, units, PLAN),
             out_shape=[
                 jax.ShapeDtypeStruct(inputs.shape, bfloat),
                 jax.ShapeDtypeStruct(inputs.shape, bfloat),
-                jax.ShapeDtypeStruct((grad_rows, width), bfloat),
-                jax.ShapeDtypeStruct((HEADS * head_share, width), bfloat),
+                pltpu.VMEM((grad_rows + HEADS * head_share, width), bfloat),
                 shape(16, width),
                 shape(8, width),
             ],
             in_specs=[hbm, smem] + [hbm] * 14,
-            out_specs=[hbm] * 6,
+            out_specs=[hbm, hbm, vmem, hbm, hbm],
             scratch_shapes=[
                 pltpu.VMEM(inputs.shape, bfloat),
                 pltpu.VMEM(qb.shape, bfloat),
@@ -1638,11 +1622,10 @@
                 pltpu.VMEM((others, head_share // groups, width), bfloat),
                 pltpu.VMEM((grad_rows, width), bfloat),
                 pltpu.VMEM((grad_rows, width), bfloat),
-                pltpu.VMEM((grad_rows + HEADS * head_share, width), bfloat),
                 pltpu.VMEM((3 + groups, 16, width), single),
-                pltpu.VMEM((8, 256), single),
-                pltpu.VMEM((others, 8, 256), single),
-                pltpu.VMEM((HEADS, 8, 256), single),
+                pltpu.VMEM((8, 2 * HEAD), single),
+                pltpu.VMEM((others, 8, 2 * HEAD), single),
+                pltpu.VMEM((HEADS, 8, 2 * HEAD), single),
                 pltpu.VMEM((8, width), single),
                 dma(()),
                 dma((seqs, 3)),
@@ -1657,16 +1640,15 @@
                 dma((len(units),)),
                 dma((len(units), 10)),
                 dma((3,)),
-                dma((4,)),
+                dma((5,)),
                 dma(()),
                 dma((4,)),
-                dma((2,)),
                 dma((2,)),
                 dma((2,)),
                 dma((4,)),
             ],
             compiler_params=pltpu.CompilerParams(
-                collective_id=0, has_side_effects=True, vmem_limit_bytes=60 * 2**20
+                collective_id=0, has_side_effects=True, vmem_limit_bytes=LAYER_VMEM
             ),
             name="layer",
         )(
@@ -1676,7 +1658,7 @@
         pieces = grad_rows // WIDE
         return pl.pallas_call(
             widen_kernel,
-            in_specs=[hbm] * 6,
+            in_specs=[vmem] + [hbm] * 4,
             out_specs=[hbm] * 15,
             out_shape=[
                 jax.ShapeDtypeStruct(inputs.shape, bfloat),
@@ -1697,8 +1679,6 @@
             ],
             scratch_shapes=[
                 *[pltpu.VMEM((width,), single)] * 8,
-                pltpu.VMEM((grad_rows, width), bfloat),
-                pltpu.VMEM(entry_shape, bfloat),
                 pltpu.VMEM((16, width), single),
                 pltpu.VMEM((8, width), single),
                 pltpu.VMEM((2, *inputs.shape), bfloat),
@@ -1707,12 +1687,12 @@
                 pltpu.VMEM((width, ff), single),
                 pltpu.VMEM((width, width), single),
                 pltpu.VMEM((width, 3 * width), single),
-                dma((pieces + 5,)),
+                dma((4,)),
                 dma((pieces + 14,)),
             ],
-            compiler_params=pltpu.CompilerParams(vmem_limit_bytes=60 * 2**20),
+            compiler_params=pltpu.CompilerParams(vmem_limit_bytes=WIDEN_VMEM),
             name="widen",
-        )(sums, entry.reshape(entry_shape), small, bias, out, dx)
+        )(pltpu.with_memory_space_constraint(total, pltpu.VMEM), small, bias, out, dx)
 
     return run
 

time: 109 us -> 105 us (0.963)
  Pallas kernels: 108 us -> 104 us
    pallas_call x1, Pallas kernels: 101 us -> 98.3 us  [run(): pl.pallas_call(partial(layer_kernel, groups, units, PLAN), out_shape=[jax...]
    pallas_call x1, Pallas kernels: 7.08 us -> 5.3 us  [run(): pl.pallas_call(widen_kernel, in_specs=[vmem] + [hbm] * 4, out_specs=[hbm]...]
where the time goes in v4:
time: 105 us; the launch traced here: 104 us
  Pallas kernels  104 us (99%)
    pallas_call x1, Pallas kernels, run(): pl.pallas_call(partial(layer_kernel, groups, units, PLAN), out_shape=[jax...  98.3 us
    pallas_call x1, Pallas kernels, run(): pl.pallas_call(widen_kernel, in_specs=[vmem] + [hbm] * 4, out_specs=[hbm]...  5.3 us

profile of v4, /device:TPU:0, one launch (start us, length us, event | category | flops | bytes accessed | tf_op | source)
XLA Modules:
  0.0 104.4 jit_solution(1886879994552574932)
XLA Ops:
  0.7 98.3 %layer.1 = (bf16[3,128,512]{2,1,0:T(8,128)(2,1)}, bf16[3,128,512]{2,1,0:T(8,128)(2,1)}, bf16[6144,512]{1,0:T(8,128)(2,1)S(1)}, f32[16,512]{1,0:T(8,128)}, f32[8,512]{1,0:T(8,128)}) custom-call(bf16[3,128,512]{2,1,0:T(8,128)(2,1)} %x_hbm.1, s32[3,3,2,8]{3,2,1,0:T(2,128)} %bitcast.1, bf16[512,1536]{1,0:T(8,128)(2,1)} %we_hbm.1, bf16[512]{0:T(512)(128)(2,1)} %qb_hbm.1, ...), custom_call_target="tpu_custom_call" | custom-call | tf_op jit(solution)/shard_map/layer/pallas_call | solution.py:1561
  98.9 5.3 %widen.1 = (bf16[3,128,512]{2,1,0:T(8,128)(2,1)}, bf16[3,128,512]{2,1,0:T(8,128)(2,1)}, f32[512,1536]{1,0:T(8,128)}, f32[512]{0:T(512)}, f32[512]{0:T(512)}, /*i...) custom-call(bf16[6144,512]{1,0:T(8,128)(2,1)S(1)} %get-tuple-element, ...), custom_call_target="tpu_custom_call" | custom-call | tf_op jit(solution)/shard_map/widen/pallas_call | solution.py:1659

commit v5 on v4

--- a/solution.py
+++ b/solution.py
@@ -532,7 +532,7 @@
     units,
     plan,
     x_hbm,
-    blocks_ref,
+    blocks_hbm,
     we_hbm,
     qb_hbm,
     vb_hbm,
@@ -552,6 +552,7 @@
     total,
     small_hbm,
     bias_hbm,
+    blocks_ref,
     x_ref,
     qb_ref,
     vb_ref,
@@ -628,19 +629,29 @@
     b_send,
     b_recv,
     store_sem,
+    second_round,
+    third_round,
 ):
     seqs, tokens, width = x_ref.shape
     place = Place(groups)
     me = place.me
     barrier = pltpu.get_barrier_semaphore()
-    for k in range(1, 8):
-        pl.semaphore_signal(
-            barrier, inc=1, device_id=place.in_plane(k), device_id_type=MESH
-        )
-    for k in range(1, groups):
-        pl.semaphore_signal(
-            barrier, inc=1, device_id=place.in_column(k), device_id_type=MESH
-        )
+    neighbours = 3 + (place.z > 0).astype(jnp.int32) + (place.z < groups - 1).astype(jnp.int32)
+
+    def greet(sem):
+        for k in (1, 2, 4):
+            pl.semaphore_signal(sem, inc=1, device_id=place.in_plane(k), device_id_type=MESH)
+
+        @pl.when(place.z > 0)
+        def _():
+            pl.semaphore_signal(sem, inc=1, device_id=(place.z - 1, me), device_id_type=MESH)
+
+        @pl.when(place.z < groups - 1)
+        def _():
+            pl.semaphore_signal(sem, inc=1, device_id=(place.z + 1, me), device_id_type=MESH)
+
+    greet(barrier)
+
     def load(*pairs):
         copies = []
         for src, dst in pairs:
@@ -651,7 +662,83 @@
 
     loads = []
     load_x = load((x_hbm, x_ref))
+    load_blocks = load((blocks_hbm, blocks_ref))
+    def lanes_of(device):
+        return pl.ds(aligned(device * tokens, 128), tokens)
+
+    def head_rows_of(device):
+        return pl.ds(aligned(device * HEAD, HEAD), HEAD)
+
+    def seq_lanes(s):
+        return pl.ds(aligned(s * tokens, 128), tokens)
+
+    def vec(ref):
+        return ref[...].astype(single).reshape(1, ref.shape[0])
+
+    others = HEADS - 1
+
+    def take(ref, sem):
+        remote(ref, ref, sem, sem, place.in_plane(1)).wait_recv()
+
+    def gone(ref, sem):
+        remote(ref, ref, sem, sem, place.in_plane(1)).wait_send()
+
+    small_ref[...] = jnp.zeros(small_ref.shape, single)
+    bias_rows[...] = jnp.zeros(bias_rows.shape, single)
+    bias_own[...] = jnp.zeros(bias_own.shape, single)
+    entry_acc[...] = jnp.zeros(entry_acc.shape, single)
+
+    load_x[0].wait()
+    pl.semaphore_wait(barrier, neighbours)
+    greet(second_round)
+
+    half_width = width // 2
+
+    def x_copy(s, k):
+        return remote(
+            x_ref.at[s],
+            xall.at[s, lanes_of(me), :],
+            x_send,
+            x_recv.at[s, 2 if k == 1 else 0],
+            place.in_plane(k),
+        )
+
+    def x_across(s, k):
+        columns = slice(0, half_width) if k == 2 else slice(half_width, width)
+        slab = xall.at[s, lanes_of(place.peer(6 - k)), columns]
+        return remote(slab, slab, x_send, x_recv.at[s, 1], place.in_plane(k))
+
+    def x_forward(s, k):
+        slab = xall.at[s, lanes_of(place.peer(k)), :]
+        return remote(slab, slab, x_send, x_recv.at[s, 2], place.in_plane(1))
+
+    def x_arrived(s, which):
+        slabs = (2, 1, 4)[which]
+        take(xall.at[s, 0 : slabs * tokens, :], x_recv.at[s, which])
+
+    def x_begin(s):
+        for k in (2, 4, 1):
+            x_copy(s, k).start()
+
+    def x_pass(s):
+        x_arrived(s, 0)
+        for k in (2, 4):
+            x_across(s, k).start()
+            x_forward(s, k).start()
+
+    def ids_copy(k):
+        other = place.peer(k)
+        return remote(
+            ids_send.at[other],
+            ids_all.at[:, lanes_of(me)],
+            i_send,
+            i_recv,
+            place.in_plane(k),
+        )
+
+    x_begin(0)
     load_entry = load((we_hbm, we), (qb_hbm, qb_ref), (vb_hbm, vb_ref))
+    x_begin(1)
     load_rest = load(
         (wo_hbm, wo),
         (bo_hbm, bo_ref),
@@ -665,26 +752,10 @@
         (s2_hbm, s2_ref),
         (cot_hbm, cot),
     )
-
-    def lanes_of(device):
-        return pl.ds(aligned(device * tokens, 128), tokens)
-
-    def head_rows_of(device):
-        return pl.ds(aligned(device * HEAD, HEAD), HEAD)
-
-    def seq_lanes(s):
-        return pl.ds(aligned(s * tokens, 128), tokens)
-
-    def vec(ref):
-        return ref[...].astype(single).reshape(1, ref.shape[0])
-
-    others = HEADS - 1
-
-    def take(ref, sem):
-        remote(ref, ref, sem, sem, place.in_plane(1)).wait_recv()
-
-    def gone(ref, sem):
-        remote(ref, ref, sem, sem, place.in_plane(1)).wait_send()
+    for s in range(seqs):
+        xall[s, lanes_of(me), :] = x_ref[s]
+
+    load_blocks[0].wait()
 
     lane = lax.broadcasted_iota(jnp.int32, (16, tokens), 1)
     row = lax.broadcasted_iota(jnp.int32, (16, tokens), 0)
@@ -697,65 +768,8 @@
                 )
                 numbers = jnp.where(row == s * 3 + j, picked, numbers)
         ids_send[h] = numbers.astype(single).astype(bfloat)
-    small_ref[...] = jnp.zeros(small_ref.shape, single)
-    bias_rows[...] = jnp.zeros(bias_rows.shape, single)
-    bias_own[...] = jnp.zeros(bias_own.shape, single)
-    entry_acc[...] = jnp.zeros(entry_acc.shape, single)
-
-    load_x[0].wait()
-    pl.semaphore_wait(barrier, 7 + groups - 1)
-
-    half_width = width // 2
-
-    def x_copy(s, k):
-        return remote(
-            x_ref.at[s],
-            xall.at[s, lanes_of(me), :],
-            x_send,
-            x_recv.at[s, 2 if k == 1 else 0],
-            place.in_plane(k),
-        )
-
-    def x_across(s, k):
-        columns = slice(0, half_width) if k == 2 else slice(half_width, width)
-        slab = xall.at[s, lanes_of(place.peer(6 - k)), columns]
-        return remote(slab, slab, x_send, x_recv.at[s, 1], place.in_plane(k))
-
-    def x_forward(s, k):
-        slab = xall.at[s, lanes_of(place.peer(k)), :]
-        return remote(slab, slab, x_send, x_recv.at[s, 2], place.in_plane(1))
-
-    def x_arrived(s, which):
-        slabs = (2, 1, 4)[which]
-        take(xall.at[s, 0 : slabs * tokens, :], x_recv.at[s, which])
-
-    def x_begin(s):
-        for k in (2, 4, 1):
-            x_copy(s, k).start()
-
-    def x_pass(s):
-        x_arrived(s, 0)
-        for k in (2, 4):
-            x_across(s, k).start()
-            x_forward(s, k).start()
-
-    def ids_copy(k):
-        other = place.peer(k)
-        return remote(
-            ids_send.at[other],
-            ids_all.at[:, lanes_of(me)],
-            i_send,
-            i_recv,
-            place.in_plane(k),
-        )
-
-    x_begin(0)
-    for k in range(1, 8):
-        ids_copy(k).start()
-    x_begin(1)
-    ids_all[:, lanes_of(me)] = ids_send[me]
-    for s in range(seqs):
-        xall[s, lanes_of(me), :] = x_ref[s]
+    pl.semaphore_wait(second_round, neighbours)
+    greet(third_round)
 
     for copy in load_entry:
         copy.wait()
@@ -776,6 +790,14 @@
     query_column = column(qb_ref)
     value_column = column(vb_ref)
 
+    ids_all[:, lanes_of(me)] = ids_send[me]
+    pl.semaphore_wait(third_round, neighbours)
+    for k in range(1, 8):
+        ids_copy(k).start()
+    x_pass(0)
+    for s in range(2, seqs):
+        x_begin(s)
+    x_pass(1)
     take(ids_all.at[:, 0 : others * tokens], i_recv)
     for s in range(seqs):
         ids[s, 0:3, :] = ids_all[...].astype(single)[3 * s : 3 * s + 3]
@@ -807,7 +829,8 @@
         packed = dot(wh_t[...], xall[s], 1, 1)
         qkv[s, 0:HEAD, :] = ((packed[0:HEAD] + query_column) * HEAD**-0.5).astype(bfloat)
         qkv[s, HEAD : 2 * HEAD, :] = packed[HEAD : 2 * HEAD].astype(bfloat)
-        qkv[s, 2 * HEAD :, :] = (packed[2 * HEAD :] + value_column).astype(bfloat)
+        qkv[s, 2 * HEAD : 3 * HEAD, :] = (packed[2 * HEAD :] + value_column).astype(bfloat)
+        qkv[s, 3 * HEAD :, :] = jnp.ones((16, length), bfloat)
 
     def attend(s, _):
         take_x(s)
@@ -832,13 +855,12 @@
             score = score.reshape(length, QUERIES)
             peak = jnp.max(score, axis=0, keepdims=True)
             grown = jnp.exp(score - peak)
-            inverse = 1.0 / jnp.sum(grown, axis=0, keepdims=True)
             grown = grown.astype(bfloat)
             probs[s, :, at] = grown
+            summed = jnp.dot(qkv[s, 2 * HEAD :, :], grown, preferred_element_type=single)
+            inverse = 1.0 / summed[HEAD : HEAD + 1]
             inv_total[s, :, at] = inverse
-            result = inverse * jnp.dot(
-                qkv[s, 2 * HEAD :, :], grown, preferred_element_type=single
-            )
+            result = inverse * summed[0:HEAD]
             out_wide[s, :, at] = result
             out_low[s, :, at] = result.astype(bfloat)
             return 0
@@ -849,10 +871,6 @@
         att_t[head_rows_of(me), seq_lanes(s)] = out_low[s, :, lanes_of(me)]
         return 0
 
-    x_pass(0)
-    for s in range(2, seqs):
-        x_begin(s)
-    x_pass(1)
     lax.fori_loop(0, seqs, attend, 0)
     for copy in load_rest:
         copy.wait()
@@ -922,8 +940,18 @@
         grad_outer[here, :] = grad_low
         add_small(9, grad_low.astype(single))
 
-    for group in FORWARD:
-        forward(*group)
+    def outer_early(start, rows):
+        at = slice(start, start + TILES)
+        keep_part(start, dot(hidden[0:rows, at], grad_outer[0:rows, :], 0, 0))
+
+    def keep_part(base, value):
+        part[base : base + value.shape[0], :] = value.astype(bfloat)
+
+    forward(*FORWARD[0])
+    rows_early = FORWARD[0][1] * tokens
+    for start in range(0, ff, TILES):
+        outer_early(start, rows_early)
+    forward(*FORWARD[1])
 
     def stages_of(unit):
         base, count, order = units[unit]
@@ -1064,9 +1092,6 @@
             elif index == at:
                 do()
 
-    def keep_part(base, value):
-        part[base : base + value.shape[0], :] = value.astype(bfloat)
-
     def small_copy(turn, device):
         return remote(small_ref, small_in.at[turn], v_send, v_recv.at[min(turn, 3)], device)
 
@@ -1103,15 +1128,23 @@
             small_ref[...] = in_place_order(small_ref[...], terms)
             small_store.start()
 
+    ticks = iter(range(100))
+
+    def tick():
+        steps_at("early", next(ticks))
+
     def outer_tile(start):
         at = slice(start, start + TILES)
-        keep_part(start, dot(hidden[:, at], grad_outer[...], 0, 0))
+        late = dot(hidden[rows_early:, at], grad_outer[rows_early:, :], 0, 0)
+        keep_part(start, part[at, :].astype(single) + late)
         ready_units(start, start + TILES)
+        tick()
 
     def inner_tile(start):
         for j in range(start, start + TILES, WIDE):
             keep_part(ff + j, dot(low1[...], grad_inner[:, j : j + WIDE], 0, 0))
         ready_units(ff + start, ff + start + TILES)
+        tick()
 
     def backward(first_seq, last_seq):
         here = slice(first_seq * tokens, last_seq * tokens)
@@ -1124,6 +1157,8 @@
             grad_inner[here, span] = inner
             add_small(5 + j, inner.astype(single))
             back = back + dot(inner, w1[:, span], 1, 1)
+            if j % 2 == 1:
+                tick()
         normed1 = hat1[here, :]
         add_small(3, back * normed1)
         add_small(4, back)
@@ -1139,14 +1174,15 @@
                 dout_copy(s, k).start()
         for s in range(first_seq, last_seq):
             dout_t[s, :, lanes_of(me)] = gatt_t[head_rows_of(me), seq_lanes(s)]
+        tick()
 
     def out_tile():
         keep_part(2 * ff, jnp.dot(att_t[...], grad_branch[...], preferred_element_type=single))
         ready_units(2 * ff, 2 * ff + width)
-
-    for index, (kind, *what) in enumerate(EARLY):
+        tick()
+
+    for kind, *what in EARLY:
         {"outer": outer_tile, "back": backward, "inner": inner_tile, "out": out_tile}[kind](*what)
-        steps_at("early", index)
 
     def pack_copies(s, k):
         other = place.peer(k)
@@ -1167,8 +1203,8 @@
         at = pl.ds(aligned(i * BACK_QUERIES, BACK_QUERIES), BACK_QUERIES)
         cot_t = dout_t[s, :, at].astype(single)
         inverse = inv_total[s, :, at]
-        delta = inverse * jnp.sum(cot_t * out_wide[s, :, at], axis=0, keepdims=True)
         cot_low = (cot_t * inverse).astype(bfloat)
+        delta = jnp.sum(cot_low.astype(single) * out_wide[s, :, at], axis=0, keepdims=True)
         grown = probs[s, :, at]
         grad = jnp.dot(vrow[s], cot_low, preferred_element_type=single) - delta
         grad = (grown.astype(single) * grad).astype(bfloat)
@@ -1425,117 +1461,123 @@
 
 
 UNITS = (
-    (0, 512, "xyz"),
-    (512, 512, "yuvx"),
-    (1024, 512, "zyx"),
-    (1536, 512, "uyxv"),
-    (2048, 512, "xyuv"),
-    (2560, 512, "yuxv"),
-    (3072, 512, "xyz"),
-    (3584, 512, "xyz"),
+    (0, 512, "yuvx"),
+    (512, 512, "uvxy"),
+    (1024, 512, "yxuv"),
+    (1536, 512, "xuvy"),
+    (2048, 512, "uxyv"),
+    (2560, 512, "xyuv"),
+    (3072, 512, "yxz"),
+    (3584, 512, "xyuv"),
     (4096, 512, "zyx"),
 )
 PLAN = {
     "early": (
-        (1, "unit", 1, 0),
-        (1, "unit", 0, 0),
-        (3, "small", 0),
-        (3, "unit", 3, 0),
-        (3, "unit", 2, 0),
-        (4, "small", 1),
-        (6, "unit", 0, 1),
-        (6, "unit", 4, 0),
-        (6, "unit", 5, 0),
-        (6, "unit", 1, 1),
+        (2, "unit", 0, 0),
+        (3, "unit", 1, 0),
+        (6, "unit", 3, 0),
+        (6, "unit", 2, 0),
+        (7, "small", 0),
+        (8, "small", 1),
+        (8, "unit", 0, 1),
+        (9, "unit", 4, 0),
+        (9, "unit", 1, 1),
+        (10, "unit", 5, 0),
     ),
     "attention": (
         (0, "unit", 7, 0),
+        (0, "unit", 3, 1),
         (0, "unit", 8, 0),
         (0, "unit", 6, 0),
+        (0, "unit", 2, 1),
         (1, "unit", 0, 2),
-        (1, "unit", 3, 1),
-        (1, "small", 2),
-        (3, "unit", 4, 1),
+        (2, "unit", 4, 1),
+        (2, "small", 2),
+        (3, "unit", 1, 2),
         (3, "unit", 5, 1),
-        (3, "unit", 2, 1),
-        (4, "unit", 7, 1),
-        (4, "unit", 1, 2),
+        (3, "unit", 6, 1),
+        (3, "unit", 3, 2),
+        (5, "unit", 7, 1),
     ),
     "tail": (
         ("entry", 0),
         ("bias", 0),
-        ("unit", 6, 1),
-        ("unit", 3, 2),
+        ("unit", 2, 2),
         ("small", 3),
         ("unit", 8, 1),
         ("unit", 0, 3),
+        ("unit", 3, 3),
+        ("unit", 4, 2),
+        ("unit", 2, 3),
         ("unit", 5, 2),
-        ("unit", 1, 3),
-        ("unit", 4, 2),
-        ("unit", 2, 2),
         ("entry", 1),
         ("bias", 1),
+        ("unit", 5, 3),
+        ("small", 4),
+        ("unit", 1, 3),
+        ("unit", 2, 4),
         ("unit", 7, 2),
-        ("small", 4),
+        ("unit", 6, 2),
+        ("unit", 8, 2),
+        ("unit", 3, 4),
         ("unit", 4, 3),
+        ("unit", 1, 4),
+        ("entry", 2),
+        ("unit", 7, 3),
+        ("unit", 5, 4),
+        ("unit", 3, 5),
+        ("unit", 2, 5),
         ("unit", 0, 4),
-        ("unit", 3, 3),
         ("input",),
-        ("unit", 1, 4),
-        ("unit", 5, 3),
-        ("unit", 8, 2),
-        ("unit", 2, 3),
-        ("unit", 6, 2),
-        ("entry", 2),
         ("bias", 2),
-        ("unit", 0, 5),
-        ("unit", 7, 3),
+        ("unit", 8, 3),
         ("unit", 4, 4),
         ("unit", 1, 5),
-        ("unit", 3, 4),
-        ("unit", 8, 3),
-        ("unit", 2, 4),
-        ("unit", 5, 4),
         ("unit", 6, 3),
+        ("unit", 7, 4),
+        ("unit", 5, 5),
         ("entry", 3),
-        ("unit", 2, 5),
-        ("unit", 7, 4),
+        ("unit", 2, 6),
+        ("unit", 0, 5),
+        ("unit", 3, 6),
+        ("unit", 8, 4),
+        ("unit", 1, 6),
         ("unit", 4, 5),
+        ("unit", 5, 6),
+        ("unit", 6, 4),
+        ("unit", 7, 5),
+        ("unit", 3, 7),
         ("unit", 0, 6),
-        ("unit", 1, 6),
-        ("unit", 8, 4),
-        ("unit", 3, 5),
+        ("entry", 4),
+        ("unit", 8, 5),
+        ("unit", 7, 6),
+        ("unit", 4, 6),
+        ("unit", 2, 7),
+        ("unit", 1, 7),
+        ("entry", 5),
+        ("unit", 5, 7),
+        ("unit", 6, 5),
         ("unit", 0, 7),
-        ("unit", 5, 5),
-        ("unit", 6, 4),
-        ("entry", 4),
-        ("unit", 3, 6),
-        ("unit", 7, 5),
-        ("unit", 5, 6),
-        ("unit", 4, 6),
-        ("unit", 8, 5),
-        ("entry", 5),
-        ("unit", 1, 7),
-        ("unit", 6, 5),
-        ("unit", 2, 6),
-        ("unit", 3, 7),
-        ("unit", 5, 7),
-        ("unit", 2, 7),
+        ("unit", 7, 7),
+        ("unit", 3, 8),
+        ("unit", 3, 9),
         ("unit", 4, 7),
-        ("unit", 7, 6),
-        ("unit", 7, 7),
+        ("unit", 2, 8),
+        ("unit", 2, 9),
+        ("unit", 5, 8),
+        ("unit", 8, 6),
         ("unit", 1, 8),
         ("unit", 6, 6),
+        ("unit", 5, 9),
+        ("unit", 8, 7),
         ("unit", 1, 9),
+        ("unit", 7, 8),
         ("unit", 6, 7),
-        ("unit", 8, 6),
-        ("unit", 5, 8),
         ("unit", 4, 8),
-        ("unit", 8, 7),
-        ("unit", 3, 8),
-        ("unit", 5, 9),
+        ("unit", 0, 8),
+        ("unit", 7, 9),
         ("unit", 4, 9),
-        ("unit", 3, 9),
+        ("unit", 0, 9),
     ),
 }
 
@@ -1550,7 +1592,6 @@
         units = UNITS
         others = max(groups - 1, 1)
         head_share = 3 * HEAD
-        smem = pl.BlockSpec(memory_space=pltpu.SMEM)
         vmem = pl.BlockSpec(memory_space=pltpu.VMEM)
         hbm = pl.BlockSpec(memory_space=pl.ANY)
         dma = pltpu.SemaphoreType.DMA
@@ -1567,9 +1608,10 @@
                 shape(16, width),
                 shape(8, width),
             ],
-            in_specs=[hbm, smem] + [hbm] * 14,
+            in_specs=[hbm] * 16,
             out_specs=[hbm, hbm, vmem, hbm, hbm],
             scratch_shapes=[
+                pltpu.SMEM((seqs, 3, 2, HEADS), jnp.int32),
                 pltpu.VMEM(inputs.shape, bfloat),
                 pltpu.VMEM(qb.shape, bfloat),
                 pltpu.VMEM(vb.shape, bfloat),
@@ -1588,13 +1630,13 @@
                 pltpu.VMEM(w1.shape, bfloat),
                 pltpu.VMEM(w2.shape, bfloat),
                 pltpu.VMEM(cot.shape, bfloat),
-                dma((15,)),
+                dma((16,)),
                 pltpu.VMEM((head_share, width), bfloat),
                 pltpu.VMEM((seqs, length, width), bfloat),
                 pltpu.VMEM((HEADS, 16, tokens), bfloat),
                 pltpu.VMEM((16, length), bfloat),
                 pltpu.VMEM((seqs, 8, length), single),
-                pltpu.VMEM((seqs, head_share, length), bfloat),
+                pltpu.VMEM((seqs, head_share + 16, length), bfloat),
                 pltpu.VMEM((seqs, length, HEAD), bfloat),
                 pltpu.VMEM((seqs, length, HEAD), bfloat),
                 pltpu.VMEM((seqs, length, length), bfloat),
@@ -1646,6 +1688,8 @@
                 dma((2,)),
                 dma((2,)),
                 dma((4,)),
+                pltpu.SemaphoreType.REGULAR,
+                pltpu.SemaphoreType.REGULAR,
             ],
             compiler_params=pltpu.CompilerParams(
                 collective_id=0, has_side_effects=True, vmem_limit_bytes=LAYER_VMEM

time: 105 us -> 102 us (0.971)
  Pallas kernels: 104 us -> 101 us
    pallas_call x1, Pallas kernels: 98.3 us -> 95.7 us  [run(): pl.pallas_call(partial(layer_kernel, groups, units, PLAN), out_shape=[jax...]
where the time goes in v5:
time: 102 us
  Pallas kernels  101 us (99%)
    pallas_call x1, Pallas kernels, run(): pl.pallas_call(partial(layer_kernel, groups, units, PLAN), out_shape=[jax...  95.7 us
    pallas_call x1, Pallas kernels, run(): pl.pallas_call(widen_kernel, in_specs=[vmem] + [hbm] * 4, out_specs=[hbm]...  5.3 us

profile of v5, /device:TPU:0, one launch (start us, length us, event | category | flops | bytes accessed | tf_op | source)
XLA Modules:
  0.0 101.8 jit_solution(13024981106130024982)
XLA Ops:
  0.7 95.7 %layer.1 = (bf16[3,128,512]{2,1,0:T(8,128)(2,1)}, bf16[3,128,512]{2,1,0:T(8,128)(2,1)}, bf16[6144,512]{1,0:T(8,128)(2,1)S(1)}, f32[16,512]{1,0:T(8,128)}, f32[8,512]{1,0:T(8,128)}) custom-call(bf16[3,128,512]{2,1,0:T(8,128)(2,1)} %x_hbm.1, s32[3,3,2,8]{3,2,1,0:T(2,128)} %bitcast.1, bf16[512,1536]{1,0:T(8,128)(2,1)} %we_hbm.1, bf16[512]{0:T(512)(128)(2,1)} %qb_hbm.1, ...), custom_call_target="tpu_custom_call" | custom-call | tf_op jit(solution)/shard_map/layer/pallas_call | solution.py:1602
  96.3 5.3 %widen.1 = (bf16[3,128,512]{2,1,0:T(8,128)(2,1)}, bf16[3,128,512]{2,1,0:T(8,128)(2,1)}, f32[512,1536]{1,0:T(8,128)}, f32[512]{0:T(512)}, f32[512]{0:T(512)}, /*i...) custom-call(bf16[6144,512]{1,0:T(8,128)(2,1)S(1)} %get-tuple-element, ...), custom_call_target="tpu_custom_call" | custom-call | tf_op jit(solution)/shard_map/widen/pallas_call | solution.py:1703

commit v6 on v5

--- a/solution.py
+++ b/solution.py
@@ -468,8 +468,8 @@
 FORWARD = ((0, 2), (2, 3))
 EARLY = (
     ("outer", 0),
+    ("outer", 1024),
     ("back", 0, 1),
-    ("outer", 1024),
     ("back", 1, 3),
     ("inner", 0),
     ("inner", 1024),
@@ -577,6 +577,7 @@
     ids_send,
     ids_all,
     ids,
+    send_last,
     qkv,
     krow,
     vrow,
@@ -614,6 +615,8 @@
     x_recv,
     i_send,
     i_recv,
+    l_send,
+    l_recv,
     o_send,
     o_recv,
     d_send,
@@ -768,11 +771,35 @@
                 )
                 numbers = jnp.where(row == s * 3 + j, picked, numbers)
         ids_send[h] = numbers.astype(single).astype(bfloat)
-    pl.semaphore_wait(second_round, neighbours)
-    greet(third_round)
+    last = seqs - 1
+    head_share = 3 * HEAD
+
+    def last_copy(k):
+        return remote(
+            send_last.at[place.peer(k)],
+            qkv.at[last, 0:head_share, lanes_of(me)],
+            l_send,
+            l_recv,
+            place.in_plane(k),
+        )
+
+    def pack_last():
+        packed = jnp.dot(x_ref[last], we[...], preferred_element_type=single)
+        for j, bias in enumerate((qb_ref, None, vb_ref)):
+            piece = packed[:, j * width : (j + 1) * width]
+            if bias is not None:
+                piece = piece + vec(bias)
+            if j == 0:
+                piece = piece * HEAD**-0.5
+            piece = piece.astype(bfloat).T
+            for h in range(HEADS):
+                send_last[h, j * HEAD : (j + 1) * HEAD, :] = piece[h * HEAD : (h + 1) * HEAD]
+        qkv[last, 0:head_share, lanes_of(me)] = send_last[me]
+        qkv[last, head_share:, :] = jnp.ones((16, qkv.shape[2]), bfloat)
 
     for copy in load_entry:
         copy.wait()
+    pack_last()
     pair = me // 2
     odd = me % 2
     for j in range(3):
@@ -784,6 +811,9 @@
         lax.broadcasted_iota(jnp.int32, (HEAD, width), 0)
     )
 
+    pl.semaphore_wait(second_round, neighbours)
+    greet(third_round)
+
     def column(ref):
         return jnp.sum(jnp.where(spread, vec(ref), 0.0), axis=1, keepdims=True)
 
@@ -795,9 +825,10 @@
     for k in range(1, 8):
         ids_copy(k).start()
     x_pass(0)
-    for s in range(2, seqs):
-        x_begin(s)
+    last_copy(6).start()
     x_pass(1)
+    for k in (7, 2, 3, 4, 5, 1):
+        last_copy(k).start()
     take(ids_all.at[:, 0 : others * tokens], i_recv)
     for s in range(seqs):
         ids[s, 0:3, :] = ids_all[...].astype(single)[3 * s : 3 * s + 3]
@@ -818,19 +849,20 @@
         )
 
     def take_x(s):
-        x_arrived(s, 1)
-        x_forward(s, 6).start()
-
-        @pl.when(s < seqs - 2)
+        @pl.when(s < last)
         def _():
-            x_pass(s + 2)
-
-        x_arrived(s, 2)
-        packed = dot(wh_t[...], xall[s], 1, 1)
-        qkv[s, 0:HEAD, :] = ((packed[0:HEAD] + query_column) * HEAD**-0.5).astype(bfloat)
-        qkv[s, HEAD : 2 * HEAD, :] = packed[HEAD : 2 * HEAD].astype(bfloat)
-        qkv[s, 2 * HEAD : 3 * HEAD, :] = (packed[2 * HEAD :] + value_column).astype(bfloat)
-        qkv[s, 3 * HEAD :, :] = jnp.ones((16, length), bfloat)
+            x_arrived(s, 1)
+            x_forward(s, 6).start()
+            x_arrived(s, 2)
+            packed = dot(wh_t[...], xall[s], 1, 1)
+            qkv[s, 0:HEAD, :] = ((packed[0:HEAD] + query_column) * HEAD**-0.5).astype(bfloat)
+            qkv[s, HEAD : 2 * HEAD, :] = packed[HEAD : 2 * HEAD].astype(bfloat)
+            qkv[s, 2 * HEAD : head_share, :] = (packed[2 * HEAD :] + value_column).astype(bfloat)
+            qkv[s, head_share:, :] = jnp.ones((16, length), bfloat)
+
+        @pl.when(s == last)
+        def _():
+            take(qkv.at[last, 0:head_share, 0 : others * tokens], l_recv)
 
     def attend(s, _):
         take_x(s)
@@ -872,6 +904,7 @@
         return 0
 
     lax.fori_loop(0, seqs, attend, 0)
+    x_begin(last)
     for copy in load_rest:
         copy.wait()
 
@@ -940,18 +973,9 @@
         grad_outer[here, :] = grad_low
         add_small(9, grad_low.astype(single))
 
-    def outer_early(start, rows):
-        at = slice(start, start + TILES)
-        keep_part(start, dot(hidden[0:rows, at], grad_outer[0:rows, :], 0, 0))
-
-    def keep_part(base, value):
-        part[base : base + value.shape[0], :] = value.astype(bfloat)
-
-    forward(*FORWARD[0])
-    rows_early = FORWARD[0][1] * tokens
-    for start in range(0, ff, TILES):
-        outer_early(start, rows_early)
-    forward(*FORWARD[1])
+    for group in FORWARD:
+        forward(*group)
+    x_pass(last)
 
     def stages_of(unit):
         base, count, order = units[unit]
@@ -1092,6 +1116,9 @@
             elif index == at:
                 do()
 
+    def keep_part(base, value):
+        part[base : base + value.shape[0], :] = value.astype(bfloat)
+
     def small_copy(turn, device):
         return remote(small_ref, small_in.at[turn], v_send, v_recv.at[min(turn, 3)], device)
 
@@ -1135,8 +1162,7 @@
 
     def outer_tile(start):
         at = slice(start, start + TILES)
-        late = dot(hidden[rows_early:, at], grad_outer[rows_early:, :], 0, 0)
-        keep_part(start, part[at, :].astype(single) + late)
+        keep_part(start, dot(hidden[:, at], grad_outer[...], 0, 0))
         ready_units(start, start + TILES)
         tick()
 
@@ -1182,6 +1208,9 @@
         tick()
 
     for kind, *what in EARLY:
+        if kind == "out":
+            x_arrived(last, 1)
+            x_forward(last, 6).start()
         {"outer": outer_tile, "back": backward, "inner": inner_tile, "out": out_tile}[kind](*what)
 
     def pack_copies(s, k):
@@ -1237,6 +1266,11 @@
                 gpacked_t[j, head_rows_of(me), seq_lanes(s)] = dqkv[
                     s, j * HEAD : (j + 1) * HEAD, lanes_of(me)
                 ]
+
+            @pl.when(s == last)
+            def _():
+                x_arrived(last, 2)
+
             entry_acc[...] += jnp.dot(dqkv[s], xall[s], preferred_element_type=single)
 
         steps_at("attention", turn)
@@ -1245,7 +1279,6 @@
     lax.fori_loop(0, seqs * turns, back_chunk, 0)
 
     entry_base = 2 * ff + width
-    head_share = 3 * HEAD
     fourth = head_share // groups
 
     def entry_rows(device, z=None):
@@ -1381,6 +1414,7 @@
     pltpu.make_async_copy(dx_ref, dx_hbm, store_sem.at[1]).wait()
     gone(xall.at[:, 0 : others * tokens, :], x_send)
     gone(ids_all.at[:, 0 : others * tokens], i_send)
+    gone(qkv.at[last, 0:head_share, 0 : others * tokens], l_send)
     gone(out_low.at[:, :, 0 : others * tokens], o_send)
     gone(gatt_t.at[0 : others * HEAD, :], d_send)
     gone(dqkv.at[:, :, 0 : others * tokens], p_send)
@@ -1461,123 +1495,115 @@
 
 
 UNITS = (
-    (0, 512, "yuvx"),
-    (512, 512, "uvxy"),
-    (1024, 512, "yxuv"),
-    (1536, 512, "xuvy"),
-    (2048, 512, "uxyv"),
+    (0, 512, "yuxv"),
+    (512, 512, "uyxv"),
+    (1024, 512, "zxy"),
+    (1536, 512, "xyz"),
+    (2048, 512, "yxz"),
     (2560, 512, "xyuv"),
-    (3072, 512, "yxz"),
-    (3584, 512, "xyuv"),
-    (4096, 512, "zyx"),
+    (3072, 512, "zyx"),
+    (3584, 512, "xyz"),
+    (4096, 512, "xyz"),
 )
 PLAN = {
     "early": (
         (2, "unit", 0, 0),
         (3, "unit", 1, 0),
-        (6, "unit", 3, 0),
-        (6, "unit", 2, 0),
+        (3, "unit", 2, 0),
+        (4, "unit", 3, 0),
         (7, "small", 0),
+        (8, "unit", 0, 1),
         (8, "small", 1),
-        (8, "unit", 0, 1),
-        (9, "unit", 4, 0),
         (9, "unit", 1, 1),
+        (10, "unit", 4, 0),
         (10, "unit", 5, 0),
     ),
     "attention": (
+        (0, "unit", 3, 1),
+        (0, "unit", 6, 0),
         (0, "unit", 7, 0),
-        (0, "unit", 3, 1),
         (0, "unit", 8, 0),
-        (0, "unit", 6, 0),
-        (0, "unit", 2, 1),
-        (1, "unit", 0, 2),
-        (2, "unit", 4, 1),
+        (1, "unit", 2, 1),
+        (2, "unit", 0, 2),
+        (2, "unit", 1, 2),
         (2, "small", 2),
-        (3, "unit", 1, 2),
+        (3, "unit", 4, 1),
         (3, "unit", 5, 1),
-        (3, "unit", 6, 1),
-        (3, "unit", 3, 2),
+        (4, "unit", 3, 2),
         (5, "unit", 7, 1),
     ),
     "tail": (
         ("entry", 0),
         ("bias", 0),
+        ("unit", 6, 1),
+        ("unit", 8, 1),
+        ("small", 3),
+        ("unit", 3, 3),
         ("unit", 2, 2),
-        ("small", 3),
-        ("unit", 8, 1),
         ("unit", 0, 3),
-        ("unit", 3, 3),
-        ("unit", 4, 2),
-        ("unit", 2, 3),
         ("unit", 5, 2),
         ("entry", 1),
+        ("unit", 1, 3),
         ("bias", 1),
+        ("small", 4),
+        ("unit", 3, 4),
+        ("unit", 0, 4),
         ("unit", 5, 3),
-        ("small", 4),
-        ("unit", 1, 3),
-        ("unit", 2, 4),
         ("unit", 7, 2),
+        ("unit", 4, 2),
         ("unit", 6, 2),
         ("unit", 8, 2),
-        ("unit", 3, 4),
-        ("unit", 4, 3),
+        ("unit", 2, 3),
+        ("entry", 2),
+        ("unit", 3, 5),
         ("unit", 1, 4),
-        ("entry", 2),
-        ("unit", 7, 3),
-        ("unit", 5, 4),
-        ("unit", 3, 5),
-        ("unit", 2, 5),
-        ("unit", 0, 4),
         ("input",),
         ("bias", 2),
+        ("unit", 2, 4),
+        ("unit", 0, 5),
+        ("unit", 5, 4),
+        ("unit", 6, 3),
+        ("unit", 7, 3),
+        ("entry", 3),
+        ("unit", 4, 3),
         ("unit", 8, 3),
+        ("unit", 1, 5),
+        ("unit", 5, 5),
+        ("unit", 3, 6),
+        ("unit", 2, 5),
+        ("unit", 7, 4),
+        ("unit", 0, 6),
+        ("unit", 3, 7),
+        ("unit", 6, 4),
         ("unit", 4, 4),
-        ("unit", 1, 5),
-        ("unit", 6, 3),
-        ("unit", 7, 4),
-        ("unit", 5, 5),
-        ("entry", 3),
-        ("unit", 2, 6),
-        ("unit", 0, 5),
-        ("unit", 3, 6),
+        ("unit", 5, 6),
         ("unit", 8, 4),
+        ("unit", 7, 5),
+        ("entry", 4),
+        ("unit", 6, 5),
         ("unit", 1, 6),
         ("unit", 4, 5),
-        ("unit", 5, 6),
-        ("unit", 6, 4),
-        ("unit", 7, 5),
-        ("unit", 3, 7),
-        ("unit", 0, 6),
-        ("entry", 4),
+        ("unit", 5, 7),
+        ("entry", 5),
         ("unit", 8, 5),
+        ("unit", 2, 6),
+        ("unit", 0, 7),
+        ("unit", 1, 7),
         ("unit", 7, 6),
+        ("unit", 2, 7),
+        ("unit", 7, 7),
         ("unit", 4, 6),
-        ("unit", 2, 7),
-        ("unit", 1, 7),
-        ("entry", 5),
-        ("unit", 5, 7),
-        ("unit", 6, 5),
-        ("unit", 0, 7),
-        ("unit", 7, 7),
-        ("unit", 3, 8),
-        ("unit", 3, 9),
+        ("unit", 5, 8),
         ("unit", 4, 7),
-        ("unit", 2, 8),
-        ("unit", 2, 9),
-        ("unit", 5, 8),
-        ("unit", 8, 6),
-        ("unit", 1, 8),
         ("unit", 6, 6),
         ("unit", 5, 9),
+        ("unit", 0, 8),
+        ("unit", 8, 6),
+        ("unit", 6, 7),
+        ("unit", 1, 8),
+        ("unit", 0, 9),
         ("unit", 8, 7),
         ("unit", 1, 9),
-        ("unit", 7, 8),
-        ("unit", 6, 7),
-        ("unit", 4, 8),
-        ("unit", 0, 8),
-        ("unit", 7, 9),
-        ("unit", 4, 9),
-        ("unit", 0, 9),
     ),
 }
 
@@ -1636,6 +1662,7 @@
                 pltpu.VMEM((HEADS, 16, tokens), bfloat),
                 pltpu.VMEM((16, length), bfloat),
                 pltpu.VMEM((seqs, 8, length), single),
+                pltpu.VMEM((HEADS, head_share, tokens), bfloat),
                 pltpu.VMEM((seqs, head_share + 16, length), bfloat),
                 pltpu.VMEM((seqs, length, HEAD), bfloat),
                 pltpu.VMEM((seqs, length, HEAD), bfloat),
@@ -1671,6 +1698,8 @@
                 pltpu.VMEM((8, width), single),
                 dma(()),
                 dma((seqs, 3)),
+                dma(()),
+                dma(()),
                 dma(()),
                 dma(()),
                 dma(()),

time: 102 us -> 101 us (level)
  no operation moved by 1% of the time
where the time goes in v6:
time: 101 us
  Pallas kernels  100 us (99%)
    pallas_call x1, Pallas kernels, run(): pl.pallas_call(partial(layer_kernel, groups, units, PLAN), out_shape=[jax...  95 us
    pallas_call x1, Pallas kernels, run(): pl.pallas_call(widen_kernel, in_specs=[vmem] + [hbm] * 4, out_specs=[hbm]...  5.3 us

profile of v6, /device:TPU:0, one launch (start us, length us, event | category | flops | bytes accessed | tf_op | source)
XLA Modules:
  0.0 101.2 jit_solution(8313753528993143555)
XLA Ops:
  0.7 95.0 %layer.1 = (bf16[3,128,512]{2,1,0:T(8,128)(2,1)}, bf16[3,128,512]{2,1,0:T(8,128)(2,1)}, bf16[6144,512]{1,0:T(8,128)(2,1)S(1)}, f32[16,512]{1,0:T(8,128)}, f32[8,512]{1,0:T(8,128)}) custom-call(bf16[3,128,512]{2,1,0:T(8,128)(2,1)} %x_hbm.1, s32[3,3,2,8]{3,2,1,0:T(2,128)} %bitcast.1, bf16[512,1536]{1,0:T(8,128)(2,1)} %we_hbm.1, bf16[512]{0:T(512)(128)(2,1)} %qb_hbm.1, ...), custom_call_target="tpu_custom_call" | custom-call | tf_op jit(solution)/shard_map/layer/pallas_call | solution.py:1628
  95.7 5.3 %widen.1 = (bf16[3,128,512]{2,1,0:T(8,128)(2,1)}, bf16[3,128,512]{2,1,0:T(8,128)(2,1)}, f32[512,1536]{1,0:T(8,128)}, f32[512]{0:T(512)}, f32[512]{0:T(512)}, /*i...) custom-call(bf16[6144,512]{1,0:T(8,128)(2,1)S(1)} %get-tuple-element, ...), custom_call_target="tpu_custom_call" | custom-call | tf_op jit(solution)/shard_map/widen/pallas_call | solution.py:1732

commit v7 on v6

--- a/solution.py
+++ b/solution.py
@@ -1004,6 +1004,9 @@
     def rows_at(start, count):
         return pl.ds(aligned(start, 16), count)
 
+    def recv_slot(unit, stage):
+        return sum(2 * len(order) + 2 for _, _, order in units[:unit]) + stage
+
     def landing(unit, stage):
         before = 0
         for other in range(unit):
@@ -1016,7 +1019,7 @@
     def reduce_copies(unit, stage):
         axis, _, away, size = stages_of(unit)[stage]
         at = landing(unit, stage)
-        send, recv = rs_send.at[unit], rs_recv.at[unit, stage]
+        send, recv = rs_send.at[unit], rs_recv.at[recv_slot(unit, stage)]
         if axis != "z":
             return [
                 remote(
@@ -1048,7 +1051,7 @@
         count = groups - 1 if axis == "z" else 1
         arrived = landed.at[at : at + count * size, :]
         gone(arrived, rs_send.at[unit])
-        take(arrived, rs_recv.at[unit, stage])
+        take(arrived, rs_recv.at[recv_slot(unit, stage)])
         result = total if stage == len(units[unit][2]) else part
         tile = next(rows for rows in (128, 64, 32, 16) if size % rows == 0)
 
@@ -1072,7 +1075,7 @@
     def gather_start(unit, stage):
         axis, keep, _, size = stages_of(unit)[stage]
         slot = total.at[rows_at(keep, size), :]
-        send, recv = rs_send.at[unit], rs_recv.at[unit, 5 + stage]
+        send, recv = rs_send.at[unit], rs_recv.at[recv_slot(unit, len(units[unit][2]) + 1 + stage)]
         if axis != "z":
             remote(slot, slot, send, recv, partner(axis)).start()
         else:
@@ -1084,7 +1087,7 @@
         count = groups - 1 if axis == "z" else 1
         slot = total.at[rows_at(away, count * size), :]
         gone(slot, rs_send.at[unit])
-        take(slot, rs_recv.at[unit, 5 + stage])
+        take(slot, rs_recv.at[recv_slot(unit, len(units[unit][2]) + 1 + stage)])
 
     def step(unit, stage):
         last = len(units[unit][2])
@@ -1709,7 +1712,7 @@
                 dma(()),
                 dma(()),
                 dma((len(units),)),
-                dma((len(units), 10)),
+                dma((sum(2 * len(order) + 2 for _, _, order in units),)),
                 dma((3,)),
                 dma((5,)),
                 dma(()),

time: 101 us -> 101 us (level)
  no operation moved by 1% of the time
where the time goes in v7:
time: 101 us
  Pallas kernels  100 us (99%)
    pallas_call x1, Pallas kernels, run(): pl.pallas_call(partial(layer_kernel, groups, units, PLAN), out_shape=[jax...  94.9 us
    pallas_call x1, Pallas kernels, run(): pl.pallas_call(widen_kernel, in_specs=[vmem] + [hbm] * 4, out_specs=[hbm]...  5.3 us

profile of v7, /device:TPU:0, one launch (start us, length us, event | category | flops | bytes accessed | tf_op | source)
XLA Modules:
  0.0 101.1 jit_solution(6218465091658134079)
XLA Ops:
  0.7 94.9 %layer.1 = (bf16[3,128,512]{2,1,0:T(8,128)(2,1)}, bf16[3,128,512]{2,1,0:T(8,128)(2,1)}, bf16[6144,512]{1,0:T(8,128)(2,1)S(1)}, f32[16,512]{1,0:T(8,128)}, f32[8,512]{1,0:T(8,128)}) custom-call(bf16[3,128,512]{2,1,0:T(8,128)(2,1)} %x_hbm.1, s32[3,3,2,8]{3,2,1,0:T(2,128)} %bitcast.1, bf16[512,1536]{1,0:T(8,128)(2,1)} %we_hbm.1, bf16[512]{0:T(512)(128)(2,1)} %qb_hbm.1, ...), custom_call_target="tpu_custom_call" | custom-call | tf_op jit(solution)/shard_map/layer/pallas_call | solution.py:1631
  95.6 5.3 %widen.1 = (bf16[3,128,512]{2,1,0:T(8,128)(2,1)}, bf16[3,128,512]{2,1,0:T(8,128)(2,1)}, f32[512,1536]{1,0:T(8,128)}, f32[512]{0:T(512)}, f32[512]{0:T(512)}, /*i...) custom-call(bf16[6144,512]{1,0:T(8,128)(2,1)S(1)} %get-tuple-element, ...), custom_call_target="tpu_custom_call" | custom-call | tf_op jit(solution)/shard_map/widen/pallas_call | solution.py:1735
